TPU v7x, 512 devices: a whole 4x8x8 slice. The times are simulated.
512 devices in a mesh: ma: 8 (over x, z_lo), ka: 16 (over y, core), an: 4 (over z_hi).
Axes of the slice: x: 4, y: 8, z: 8 (z_hi: 4, z_lo: 2; z = z_hi * 2 + z_lo), core: 2. Of those that a mesh axis runs over, the one named last changes fastest.
Arguments:
- left_matrix: float32 [16384, 16384], P('ma', 'ka'), may hold values from -6 to 6
- right_panel: float32 [16384, 2048], P(('ka', 'ma'), 'an'), may hold values from -0.046875 to 0.046875
Outputs:
- product_panel: float32 [16384, 2048], P(('ma', 'ka'), 'an')
All inputs are finite; a program needn't handle non-finite values.
Results may differ from a plain program's by a relative error of at most 0.000073.
Values sent between devices are 32-bit elements; how exact they have to be, the bound alone decides.
No kernel may reach another device: no remote copies, remote signals or barrier semaphores. Data moves between devices by JAX's collectives and lax.ppermute only.
A program may use at most 64 MiB of HBM per device.

v0:
```python
import jax
import jax.numpy as jnp
from jax import lax
from jax.sharding import PartitionSpec as P


def shards(left_matrix, right_panel):
    b_local = lax.all_gather(right_panel, "ma", axis=0, tiled=True)
    partial_value = jnp.dot(
        left_matrix, b_local, preferred_element_type=jnp.float32, precision=lax.Precision.HIGHEST
    )
    return lax.psum_scatter(partial_value, "ka", scatter_dimension=0, tiled=True)


def solution(mesh):
    in_specs = (P("ma", "ka"), P(("ka", "ma"), "an"))
    out_specs = P(("ma", "ka"), "an")
    return jax.shard_map(shards, mesh=mesh, in_specs=in_specs, out_specs=out_specs, check_vma=False)
```

profile of v0, /device:TPU:1, one launch (start us, length us, event | category | flops | bytes accessed | tf_op | source)
XLA Modules:
  0.0 159.3 jit_solution(685670179831027107)
XLA Ops:
  6.5 0.0 all-gather.2.cloned.1.call-start
  6.5 0.7 all-gather.2.cloned.1.call-update
  7.3 0.0 reduce-scatter.2.cloned.1.call-start
  7.3 65.0 %all-gather.2.cloned.1.call-done = f32[1024,512]{1,0:T(8,128)} async-done(((f32[128,512]{1,0:T(8,128)}), f32[1024,512]{1,0:T(8,128)}) %all-gather.2.cloned.1.call-update) | async-done | bytes 2097168 | tf_op jit(solution)/shard_map/all_gather | solution.py:8
  72.3 17.5 %fusion = f32[2048,512]{1,0:T(8,128)} fusion(f32[2048,1024]{1,0:T(8,128)} %param.2, f32[1024,512]{1,0:T(8,128)} %all-gather.2.cloned.1.call-done), kind=kOutput, calls=%fused_computation | convolution fusion | flops 12884901888 | bytes 14680064 | tf_op jit(solution)/shard_map/dot_general | solution.py:9
  89.9 0.0 reduce-scatter.2.cloned.1.call-update
  89.9 62.6 %reduce-scatter.2.cloned.1.call-done = f32[128,512]{1,0:T(8,128)} async-done(((f32[2048,512]{1,0:T(8,128)}), f32[128,512]{1,0:T(8,128)}) %reduce-scatter.2.cloned.1.call-update) | async-done | bytes 262160 | tf_op jit(solution)/shard_map/reduce_scatter | solution.py:12
Async XLA Ops:
  6.5 65.8 %all-gather.2.cloned.1.call-start = ((), (), s32[]{:S(2)}) async-start(), calls=%async_computation.1 | async-start | bytes 2359296 | tf_op jit(solution)/shard_map/all_gather | solution.py:8
  7.3 145.2 %reduce-scatter.2.cloned.1.call-start = ((), (), s32[]{:S(2)}) async-start(), calls=%async_computation.2 | async-start | bytes 4456448 | tf_op jit(solution)/shard_map/reduce_scatter | solution.py:12
Sparse Core Ops, SparseCore 0:
  9.4 62.8 all-gather.1
  90.0 62.4 reduce-scatter.1
where the time goes:
time: 161 us; the launch traced here: 159 us
  waiting for transfers between devices  128 us (80%)
  matrix products  17.5 us (11%)
  between operations  13.4 us (8%)
    all_gather x1, waiting for transfers between devices, shards(): b_local = lax.all_gather(right_panel, 'ma', axis=0, tiled=True)  65 us
    reduce_scatter x1, waiting for transfers between devices, shards(): lax.psum_scatter(partial_value, 'ka', scatter_dimension=0, tiled=True)  62.6 us
    dot_general x1, matrix products, shards(): jnp.dot(left_matrix, b_local, preferred_element_type=jnp.float32, precisi...  17.5 us
  transfers between devices with their start and end apart: 2, of which 2 were waited for; matrix products, arithmetic and copies ran while one was open for 0% of the time, Pallas kernels for 0%

commit v1 on v0

v1 whole, which is shorter than its diff:
```python
import jax
import jax.numpy as jnp
from jax import lax
from jax.experimental import pallas as pl
from jax.experimental.pallas import tpu as pltpu
from jax.sharding import PartitionSpec as P

F32, BF16 = jnp.float32, jnp.bfloat16
VMEM_LIMIT = 48 * 1024 * 1024


def params():
    return pltpu.CompilerParams(vmem_limit_bytes=VMEM_LIMIT)


def two_parts(value):
    high = value.astype(BF16)
    return high, (value - high.astype(F32)).astype(BF16)


def split_kernel(a_ref, high_ref, low_ref):
    high_ref[...], low_ref[...] = two_parts(a_ref[...])


def split(a):
    rows, cols = a.shape
    spec = pl.BlockSpec((256, cols), lambda i: (i, 0))
    return pl.pallas_call(
        split_kernel,
        grid=(rows // 256,),
        in_specs=[spec],
        out_specs=[spec, spec],
        out_shape=[jax.ShapeDtypeStruct(a.shape, BF16)] * 2,
        compiler_params=params(),
        cost_estimate=pl.CostEstimate(flops=4 * rows * cols, bytes_accessed=8 * rows * cols, transcendentals=0),
    )(a)


def split_b_kernel(place, b_ref, high_ref, low_ref):
    core = place[1]
    for slot in range(2):
        block = b_ref[:, core if slot == 0 else 1 - core].reshape(1024, 256)
        high_ref[slot], low_ref[slot] = two_parts(block)


def split_b(place, gathered):
    return pl.pallas_call(
        split_b_kernel,
        grid_spec=pltpu.PrefetchScalarGridSpec(
            num_scalar_prefetch=1,
            in_specs=[pl.BlockSpec(memory_space=pltpu.VMEM)],
            out_specs=[pl.BlockSpec(memory_space=pltpu.VMEM)] * 2,
        ),
        out_shape=[jax.ShapeDtypeStruct((2, 1024, 256), BF16)] * 2,
        compiler_params=params(),
        cost_estimate=pl.CostEstimate(flops=2 << 20, bytes_accessed=4 << 20, transcendentals=0),
    )(place, gathered)


def product_kernel(count, place, own_high, own_low, other_high, other_low, b_high, b_low, *outs):
    step = pl.program_id(0)

    def dot(a_ref, b):
        return jnp.dot(a_ref[...], b, preferred_element_type=F32)

    total = dot(own_high, b_low[0]) + dot(own_low, b_high[0])
    total += dot(other_high, b_low[1]) + dot(other_low, b_high[1])
    total += dot(own_high, b_high[0]) + dot(other_high, b_high[1])
    for index, out in enumerate(outs):

        @pl.when(step == index)
        def _(out=out):
            out[...] = total


def products(place, shifts, parts, b_high, b_low):
    count = len(shifts)

    def chosen(i, place):
        shift = shifts[0]
        for index in range(1, count):
            shift = jnp.where(i == index, shifts[index], shift)
        return ((place[0] + shift) % 8, 0)

    a_spec = pl.BlockSpec((256, 1024), chosen)
    whole = pl.BlockSpec(memory_space=pltpu.VMEM)
    flops = 2 * 3 * 256 * 2048 * 256 * count
    return pl.pallas_call(
        lambda *refs: product_kernel(count, *refs),
        grid_spec=pltpu.PrefetchScalarGridSpec(
            num_scalar_prefetch=1,
            grid=(count,),
            in_specs=[a_spec] * 4 + [whole] * 2,
            out_specs=[whole] * count,
        ),
        out_shape=[jax.ShapeDtypeStruct((256, 256), F32)] * count,
        compiler_params=params(),
        cost_estimate=pl.CostEstimate(flops=flops, bytes_accessed=count * (2 << 20), transcendentals=0),
    )(place, *parts, b_high, b_low)


def along_y(distance):
    return [(i, (i + 2 * distance) % 16) for i in range(16)]


def by_core(distance):
    return [(i, (i + (2 * distance if i % 2 == 0 else -2 * distance)) % 16) for i in range(16)]


CORES = [(i, i ^ 1) for i in range(16)]
PLANES = [[m * 16 + 2 * y + c for m in range(8) for c in range(2)] for y in range(8)]


def shards(left_matrix, right_panel):
    ka = lax.axis_index("ka")
    y, core = ka // 2, ka % 2
    place = jnp.stack([y, core]).astype(jnp.int32)

    halves = right_panel.reshape(128, 2, 256).transpose(1, 0, 2)
    sent = jnp.broadcast_to(halves[None], (8, 2, 128, 256)).reshape(16, 128, 256)
    gathered = lax.all_to_all(sent, ("ma", "ka"), 0, 0, axis_index_groups=PLANES).reshape(8, 2, 128, 256)
    other = lax.ppermute(left_matrix, "ka", CORES)

    parts = [*split(left_matrix), *split(other)]
    b_high, b_low = split_b(place, gathered)

    up3, down3, four = products(place, (3, -3, 4), parts, b_high, b_low)
    got_up3 = lax.ppermute(up3, "ka", along_y(1))
    got_down3 = lax.ppermute(down3, "ka", along_y(-1))
    got_four = lax.ppermute(four, "ka", by_core(2))
    up1, down1, up2, down2, mine = products(place, (1, -1, 2, -2, 0), parts, b_high, b_low)
    got_up1 = lax.ppermute(up1, "ka", along_y(1))
    got_down1 = lax.ppermute(down1, "ka", along_y(-1))

    up2 = up2 + got_up3 + jnp.where(core == 0, got_four, 0.0)
    down2 = down2 + got_down3 + jnp.where(core == 1, got_four, 0.0)
    got_up2 = lax.ppermute(up2, "ka", along_y(2))
    got_down2 = lax.ppermute(down2, "ka", along_y(-2))

    total = (mine + got_up1 + got_down1 + got_up2 + got_down2).reshape(2, 128, 256)
    keep = jnp.where(core == 0, total[0], total[1])
    give = jnp.where(core == 0, total[1], total[0])
    got = lax.ppermute(give, "ka", CORES)
    return jnp.concatenate([jnp.where(core == 0, keep, got), jnp.where(core == 0, got, keep)], axis=1)


def solution(mesh):
    in_specs = (P("ma", "ka"), P(("ka", "ma"), "an"))
    out_specs = P(("ma", "ka"), "an")
    return jax.shard_map(shards, mesh=mesh, in_specs=in_specs, out_specs=out_specs, check_vma=False)
```

time: 161 us -> 107 us (0.66)
  waiting for transfers between devices: 128 us -> 30.3 us
  starting transfers between devices: 0.04 us -> 37.2 us
  Pallas kernels: 0 us -> 30.4 us
  matrix products: 17.5 us -> 0 us
  between operations: 13.4 us -> 0.22 us
  local copies, waits for them, and re-layouts: 0 us -> 6.55 us
    all_gather x1 -> x0, waiting for transfers between devices: 65 us -> none  [shards(): b_local = lax.all_gather(right_panel, 'ma', axis=0, tiled=True)]
    reduce_scatter x1 -> x0, waiting for transfers between devices: 62.6 us -> none  [shards(): lax.psum_scatter(partial_value, 'ka', scatter_dimension=0, tiled=True)]
    ppermute x0 -> x9, starting transfers between devices: none -> 33.5 us  [the longest x1 8.78 us: shards(): other = lax.ppermute(left_matrix, 'ka', CORES)]
    pallas_call x0 -> x5, Pallas kernels: none -> 30.4 us  [the longest x2 15.7 us: split(): pl.pallas_call(split_kernel, grid=(rows // 256,), in_specs=[spec], out_sp...]
    dot_general x1 -> x0, matrix products: 17.5 us -> none  [shards(): jnp.dot(left_matrix, b_local, preferred_element_type=jnp.float32, precisi...]
    all_to_all x0 -> x1, waiting for transfers between devices: none -> 17.3 us  [shards(): lax.all_to_all(sent, ('ma', 'ka'), 0, 0, axis_index_groups=PLANES)]
    ppermute x0 -> x9, waiting for transfers between devices: none -> 13 us  [the longest x1 8.8 us: shards(): got_up2 = lax.ppermute(up2, 'ka', along_y(2))]
    unnamed x0 -> x4, local copies, waits for them, and re-layouts: none -> 3.87 us
  transfers between devices with their start and end apart: 2 -> 10, of which waited for: 2 -> 4; matrix products, arithmetic and copies ran while one was open for 0% -> 3% of each run, Pallas kernels for 0% -> 16%
where the time goes in v1:
time: 107 us; the launch traced here: 106 us
  starting transfers between devices  37.2 us (35%)
  Pallas kernels  30.4 us (28%)
  waiting for transfers between devices  30.3 us (28%)
  local copies, waits for them, and re-layouts  6.55 us (6%)
    all_to_all x1, waiting for transfers between devices, shards(): lax.all_to_all(sent, ('ma', 'ka'), 0, 0, axis_index_groups=PLANES)  17.3 us
    pallas_call x2, Pallas kernels, split(): pl.pallas_call(split_kernel, grid=(rows // 256,), in_specs=[spec], out_sp...  15.7 us
    pallas_call x2, Pallas kernels, products(): pl.pallas_call(lambda *refs: product_kernel(count, *refs), grid_spec=pltp...  13.9 us
    ppermute x1, waiting for transfers between devices, shards(): got_up2 = lax.ppermute(up2, 'ka', along_y(2))  8.8 us
    ppermute x1, starting transfers between devices, shards(): other = lax.ppermute(left_matrix, 'ka', CORES)  8.78 us
    ppermute x1, starting transfers between devices, shards(): got_down2 = lax.ppermute(down2, 'ka', along_y(-2))  4.35 us
    unnamed x4, local copies, waits for them, and re-layouts  3.87 us
    all_to_all x1, starting transfers between devices, shards(): lax.all_to_all(sent, ('ma', 'ka'), 0, 0, axis_index_groups=PLANES)  3.61 us
  transfers between devices with their start and end apart: 10, of which 4 were waited for; matrix products, arithmetic and copies ran while one was open for 3% of the time, Pallas kernels for 16%

profile of v1, /device:TPU:1, one launch (start us, length us, event | category | flops | bytes accessed | tf_op | source)
XLA Modules:
  0.0 105.7 jit_solution(6284748390320099844)
XLA Ops:
  0.0 8.8 %collective-permute-start = (f32[2048,1024]{1,0:T(8,128)}, f32[2048,1024]{1,0:T(8,128)}, u32[]{:S(2)}, u32[]{:S(2)}) collective-permute-start(f32[2048,1024]{1,0:T(8,128)} %a_ref.1), channel_id=1, source_target_pairs={{0,4},{4,0},{8,12},{12,8},{16,20},{20,16},{24,28},{28,24},{32,36},... | collective-permute-start | bytes 25165832 | tf_op jit(solution)/shard_map/ppermute | solution.py:122
  8.8 1.1 %reshape.15 = f32[128,2,256]{2,1,0:T(2,128)S(1)} reshape(f32[128,512]{1,0:T(8,128)} %param.3) | data formatting | bytes 524288 | tf_op jit(solution)/shard_map/reshape | solution.py:119
  9.9 1.5 %broadcast_in_dim.11 = f32[8,2,128,256]{3,2,1,0:T(8,128)} broadcast(f32[2,128,256]{2,1,0:T(8,128)S(1)} %copy.3), dimensions={1,2,3} | broadcast | bytes 2359296 | tf_op jit(solution)/shard_map/broadcast_in_dim | solution.py:120
  11.5 3.6 %all-to-all-start = ((f32[16,128,256]{2,1,0:T(8,128)}), f32[16,128,256]{2,1,0:T(8,128)S(1)}, u32[]{:S(2)}, u32[]{:S(2)}) async-start(f32[16,128,256]{2,1,0:T(8,128)} %bitcast.6), calls=%async_computation | async-start | bytes 4194304 | tf_op jit(solution)/shard_map/all_to_all | solution.py:121
  15.1 7.8 %shard_map.28 = (bf16[2048,1024]{1,0:T(8,128)(2,1)S(1)}, bf16[2048,1024]{1,0:T(8,128)(2,1)}) custom-call(f32[2048,1024]{1,0:T(8,128)} %a_ref.1), custom_call_target="tpu_custom_call" | custom-call | flops 8388608 | bytes 16777216 | tf_op jit(solution)/shard_map/pallas_call | solution.py:28
  22.9 0.0 copy-start
  22.9 1.9 %copy-done = bf16[2048,1024]{1,0:T(8,128)(2,1)} copy-done((bf16[2048,1024]{1,0:T(8,128)(2,1)}, bf16[2048,1024]{1,0:T(8,128)(2,1)S(1)}, u32[]{:S(2)}) %copy-start) | copy-done | bytes 4194328
  24.8 0.1 pad_add_fusion.place.refs_0_
  24.9 17.3 %all-to-all-done = f32[16,128,256]{2,1,0:T(8,128)S(1)} async-done(((f32[16,128,256]{2,1,0:T(8,128)}), f32[16,128,256]{2,1,0:T(8,128)S(1)}, u32[]{:S(2)}, u32[]{:S(2)}) %all-to-all-start) | async-done | bytes 2097184 | tf_op jit(solution)/shard_map/all_to_all | solution.py:121
  42.2 0.8 shard_map.30
  43.0 0.0 collective-permute-done.a_ref
  43.0 7.9 %shard_map.29 = (bf16[2048,1024]{1,0:T(8,128)(2,1)S(1)}, bf16[2048,1024]{1,0:T(8,128)(2,1)}) custom-call(f32[2048,1024]{1,0:T(8,128)} %collective-permute-done.a_ref), custom_call_target="tpu_custom_call" | custom-call | flops 8388608 | bytes 16777216 | tf_op jit(solution)/shard_map/pallas_call | solution.py:28
  50.9 0.0 copy-start.1
  50.9 2.0 %copy-done.1 = bf16[2048,1024]{1,0:T(8,128)(2,1)} copy-done((bf16[2048,1024]{1,0:T(8,128)(2,1)}, bf16[2048,1024]{1,0:T(8,128)(2,1)S(1)}, u32[]{:S(2)}) %copy-start.1) | copy-done | bytes 4194328
  52.9 5.7 %shard_map.32 = (f32[256,256]{1,0:T(8,128)S(1)}, f32[256,256]{1,0:T(8,128)S(1)}, f32[256,256]{1,0:T(8,128)S(1)}) custom-call(s32[2]{0:T(128)S(1)} %pad_add_fusion.place.refs_0_, bf16[2048,1024]{1,0:T(8,128)(2,1)} %copy-done, bf16[2048,1024]{1,0:T(8,128)(2,1)} %get-tuple-element.20.refs_2_, bf16[2048,1024]{1,0:T(8,128)(2,1)} %copy-done.1, ...), custom_call_target="tpu_custom_call" | custom-call | flops 2415919104 | bytes 6291456 | tf_op jit(solution)/shard_map/pallas_call | solution.py:88
  58.6 1.9 %collective-permute-start.3 = (f32[256,256]{1,0:T(8,128)S(1)}, f32[256,256]{1,0:T(8,128)S(1)}, u32[]{:S(2)}, u32[]{:S(2)}) collective-permute-start(f32[256,256]{1,0:T(8,128)S(1)} %get-tuple-element.29), channel_id=1, source_target_pairs={{0,8},{4,12},{8,16},{12,20},{16,24},{20,28},{24,32},{28,36},{32,40... | collective-permute-start | bytes 786440 | tf_op jit(solution)/shard_map/ppermute | solution.py:128
  60.5 3.5 %collective-permute-start.4 = (f32[256,256]{1,0:T(8,128)S(1)}, f32[256,256]{1,0:T(8,128)S(1)}, u32[]{:S(2)}, u32[]{:S(2)}) collective-permute-start(f32[256,256]{1,0:T(8,128)S(1)} %get-tuple-element.30), channel_id=1, source_target_pairs={{0,16},{4,52},{8,24},{12,60},{16,32},{20,4},{24,40},{28,12},{32,48... | collective-permute-start | bytes 786440 | tf_op jit(solution)/shard_map/ppermute | solution.py:130
  64.0 3.0 %collective-permute-start.6 = (f32[256,256]{1,0:T(8,128)S(1)}, f32[256,256]{1,0:T(8,128)S(1)}, u32[]{:S(2)}, u32[]{:S(2)}) collective-permute-start(f32[256,256]{1,0:T(8,128)S(1)} %get-tuple-element.32), channel_id=1, source_target_pairs={{0,56},{4,60},{8,0},{12,4},{16,8},{20,12},{24,16},{28,20},{32,24},... | collective-permute-start | bytes 786440 | tf_op jit(solution)/shard_map/ppermute | solution.py:129
  67.0 8.3 %shard_map.31 = (f32[256,256]{1,0:T(8,128)S(1)}, f32[256,256]{1,0:T(8,128)S(1)}, f32[256,256]{1,0:T(8,128)S(1)}, f32[256,256]{1,0:T(8,128)S(1)}, f32[256,256]{1,0:T(8,128)S(1)}) custom-call(s32[2]{0:T(128)S(1)} %pad_add_fusion.place.refs_0_, bf16[2048,1024]{1,0:T(8,128)(2,1)} %copy-done, bf16[2048,1024]{1,0:T(8,128)(2,1)} %get-tuple-element.20.refs_2_, ...), custom_call_target="tpu_custom_call" | custom-call | flops 4026531840 | bytes 10485760 | tf_op jit(solution)/shard_map/pallas_call | solution.py:88
  75.3 3.1 %collective-permute-start.1 = (f32[256,256]{1,0:T(8,128)S(1)}, f32[256,256]{1,0:T(8,128)S(1)}, u32[]{:S(2)}, u32[]{:S(2)}) collective-permute-start(f32[256,256]{1,0:T(8,128)S(1)} %get-tuple-element.26), channel_id=1, source_target_pairs={{0,8},{4,12},{8,16},{12,20},{16,24},{20,28},{24,32},{28,36},{32,40... | collective-permute-start | bytes 786440 | tf_op jit(solution)/shard_map/ppermute | solution.py:132
  78.4 3.4 %collective-permute-start.2 = (f32[256,256]{1,0:T(8,128)S(1)}, f32[256,256]{1,0:T(8,128)S(1)}, u32[]{:S(2)}, u32[]{:S(2)}) collective-permute-start(f32[256,256]{1,0:T(8,128)S(1)} %get-tuple-element.27), channel_id=1, source_target_pairs={{0,56},{4,60},{8,0},{12,4},{16,8},{20,12},{24,16},{28,20},{32,24},... | collective-permute-start | bytes 786440 | tf_op jit(solution)/shard_map/ppermute | solution.py:133
  81.8 0.0 collective-permute-done.3
  81.8 0.0 collective-permute-done.4
  81.8 0.0 collective-permute-done.6
  81.8 0.1 select_add_fusion.1
  81.9 3.0 %collective-permute-start.5 = (f32[256,256]{1,0:T(8,128)S(1)}, f32[256,256]{1,0:T(8,128)S(1)}, u32[]{:S(2)}, u32[]{:S(2)}) collective-permute-start(f32[256,256]{1,0:T(8,128)S(1)} %get-tuple-element.35), channel_id=1, source_target_pairs={{0,16},{4,20},{8,24},{12,28},{16,32},{20,36},{24,40},{28,44},{32,4... | collective-permute-start | bytes 786440 | tf_op jit(solution)/shard_map/ppermute | solution.py:137
  85.0 4.3 %collective-permute-start.7 = (f32[256,256]{1,0:T(8,128)S(1)}, f32[256,256]{1,0:T(8,128)S(1)}, u32[]{:S(2)}, u32[]{:S(2)}) collective-permute-start(f32[256,256]{1,0:T(8,128)S(1)} %get-tuple-element.36), channel_id=1, source_target_pairs={{0,48},{4,52},{8,56},{12,60},{16,0},{20,4},{24,8},{28,12},{32,16},... | collective-permute-start | bytes 786440 | tf_op jit(solution)/shard_map/ppermute | solution.py:138
  89.3 0.0 collective-permute-done.1
  89.3 0.0 collective-permute-done.2
  89.3 8.8 %collective-permute-done.5 = f32[256,256]{1,0:T(8,128)S(1)} collective-permute-done((f32[256,256]{1,0:T(8,128)S(1)}, f32[256,256]{1,0:T(8,128)S(1)}, u32[]{:S(2)}, u32[]{:S(2)}) %collective-permute-start.5) | collective-permute-done | bytes 262176 | tf_op jit(solution)/shard_map/ppermute | solution.py:137
  98.1 3.2 %collective-permute-done.7 = f32[256,256]{1,0:T(8,128)S(1)} collective-permute-done((f32[256,256]{1,0:T(8,128)S(1)}, f32[256,256]{1,0:T(8,128)S(1)}, u32[]{:S(2)}, u32[]{:S(2)}) %collective-permute-start.7) | collective-permute-done | bytes 262176 | tf_op jit(solution)/shard_map/ppermute | solution.py:138
  101.4 0.1 add_add_fusion
  101.5 2.5 %collective-permute-start.8 = (f32[128,256]{1,0:T(8,128)S(1)}, f32[128,256]{1,0:T(8,128)S(1)}, u32[]{:S(2)}, u32[]{:S(2)}) collective-permute-start(f32[128,256]{1,0:T(8,128)S(1)} %slice_select_fusion), channel_id=1, source_target_pairs={{0,4},{4,0},{8,12},{12,8},{16,20},{20,16},{24,28},{28,24},{32,36},... | collective-permute-start | bytes 393224 | tf_op jit(solution)/shard_map/ppermute | solution.py:143
  104.0 1.0 collective-permute-done.8
  105.0 0.7 pad_maximum_fusion
  (3 shorter events, 0.1 us)
Async XLA Ops:
  0.0 43.0 %collective-permute-start = (f32[2048,1024]{1,0:T(8,128)}, f32[2048,1024]{1,0:T(8,128)}, u32[]{:S(2)}, u32[]{:S(2)}) collective-permute-start(f32[2048,1024]{1,0:T(8,128)} %a_ref.1), channel_id=1, source_target_pairs={{0,4},{4,0},{8,12},{12,8},{16,20},{20,16},{24,28},{28,24},{32,36},... | collective-permute-start | bytes 25165832 | tf_op jit(solution)/shard_map/ppermute | solution.py:122
  11.5 30.7 %all-to-all-start = ((f32[16,128,256]{2,1,0:T(8,128)}), f32[16,128,256]{2,1,0:T(8,128)S(1)}, u32[]{:S(2)}, u32[]{:S(2)}) async-start(f32[16,128,256]{2,1,0:T(8,128)} %bitcast.6), calls=%async_computation | async-start | bytes 4194304 | tf_op jit(solution)/shard_map/all_to_all | solution.py:121
  22.9 1.9 %copy-start = (bf16[2048,1024]{1,0:T(8,128)(2,1)}, bf16[2048,1024]{1,0:T(8,128)(2,1)S(1)}, u32[]{:S(2)}) copy-start(bf16[2048,1024]{1,0:T(8,128)(2,1)S(1)} %get-tuple-element.19.refs_1_) | copy-start | bytes 12582916
  50.9 2.0 %copy-start.1 = (bf16[2048,1024]{1,0:T(8,128)(2,1)}, bf16[2048,1024]{1,0:T(8,128)(2,1)S(1)}, u32[]{:S(2)}) copy-start(bf16[2048,1024]{1,0:T(8,128)(2,1)S(1)} %get-tuple-element.21.refs_3_) | copy-start | bytes 12582916
  58.6 23.2 %collective-permute-start.3 = (f32[256,256]{1,0:T(8,128)S(1)}, f32[256,256]{1,0:T(8,128)S(1)}, u32[]{:S(2)}, u32[]{:S(2)}) collective-permute-start(f32[256,256]{1,0:T(8,128)S(1)} %get-tuple-element.29), channel_id=1, source_target_pairs={{0,8},{4,12},{8,16},{12,20},{16,24},{20,28},{24,32},{28,36},{32,40... | collective-permute-start | bytes 786440 | tf_op jit(solution)/shard_map/ppermute | solution.py:128
  60.5 21.3 %collective-permute-start.4 = (f32[256,256]{1,0:T(8,128)S(1)}, f32[256,256]{1,0:T(8,128)S(1)}, u32[]{:S(2)}, u32[]{:S(2)}) collective-permute-start(f32[256,256]{1,0:T(8,128)S(1)} %get-tuple-element.30), channel_id=1, source_target_pairs={{0,16},{4,52},{8,24},{12,60},{16,32},{20,4},{24,40},{28,12},{32,48... | collective-permute-start | bytes 786440 | tf_op jit(solution)/shard_map/ppermute | solution.py:130
  64.0 17.8 %collective-permute-start.6 = (f32[256,256]{1,0:T(8,128)S(1)}, f32[256,256]{1,0:T(8,128)S(1)}, u32[]{:S(2)}, u32[]{:S(2)}) collective-permute-start(f32[256,256]{1,0:T(8,128)S(1)} %get-tuple-element.32), channel_id=1, source_target_pairs={{0,56},{4,60},{8,0},{12,4},{16,8},{20,12},{24,16},{28,20},{32,24},... | collective-permute-start | bytes 786440 | tf_op jit(solution)/shard_map/ppermute | solution.py:129
  75.3 14.0 %collective-permute-start.1 = (f32[256,256]{1,0:T(8,128)S(1)}, f32[256,256]{1,0:T(8,128)S(1)}, u32[]{:S(2)}, u32[]{:S(2)}) collective-permute-start(f32[256,256]{1,0:T(8,128)S(1)} %get-tuple-element.26), channel_id=1, source_target_pairs={{0,8},{4,12},{8,16},{12,20},{16,24},{20,28},{24,32},{28,36},{32,40... | collective-permute-start | bytes 786440 | tf_op jit(solution)/shard_map/ppermute | solution.py:132
  78.4 11.0 %collective-permute-start.2 = (f32[256,256]{1,0:T(8,128)S(1)}, f32[256,256]{1,0:T(8,128)S(1)}, u32[]{:S(2)}, u32[]{:S(2)}) collective-permute-start(f32[256,256]{1,0:T(8,128)S(1)} %get-tuple-element.27), channel_id=1, source_target_pairs={{0,56},{4,60},{8,0},{12,4},{16,8},{20,12},{24,16},{28,20},{32,24},... | collective-permute-start | bytes 786440 | tf_op jit(solution)/shard_map/ppermute | solution.py:133
  81.9 16.2 %collective-permute-start.5 = (f32[256,256]{1,0:T(8,128)S(1)}, f32[256,256]{1,0:T(8,128)S(1)}, u32[]{:S(2)}, u32[]{:S(2)}) collective-permute-start(f32[256,256]{1,0:T(8,128)S(1)} %get-tuple-element.35), channel_id=1, source_target_pairs={{0,16},{4,20},{8,24},{12,28},{16,32},{20,36},{24,40},{28,44},{32,4... | collective-permute-start | bytes 786440 | tf_op jit(solution)/shard_map/ppermute | solution.py:137
  85.0 16.4 %collective-permute-start.7 = (f32[256,256]{1,0:T(8,128)S(1)}, f32[256,256]{1,0:T(8,128)S(1)}, u32[]{:S(2)}, u32[]{:S(2)}) collective-permute-start(f32[256,256]{1,0:T(8,128)S(1)} %get-tuple-element.36), channel_id=1, source_target_pairs={{0,48},{4,52},{8,56},{12,60},{16,0},{20,4},{24,8},{28,12},{32,16},... | collective-permute-start | bytes 786440 | tf_op jit(solution)/shard_map/ppermute | solution.py:138
  101.5 3.4 %collective-permute-start.8 = (f32[128,256]{1,0:T(8,128)S(1)}, f32[128,256]{1,0:T(8,128)S(1)}, u32[]{:S(2)}, u32[]{:S(2)}) collective-permute-start(f32[128,256]{1,0:T(8,128)S(1)} %slice_select_fusion), channel_id=1, source_target_pairs={{0,4},{4,0},{8,12},{12,8},{16,20},{20,16},{24,28},{28,24},{32,36},... | collective-permute-start | bytes 393224 | tf_op jit(solution)/shard_map/ppermute | solution.py:143

commit v2 on v0

v2 whole, which is shorter than its diff:
```python
import jax
import jax.numpy as jnp
from jax import lax
from jax.experimental import pallas as pl
from jax.experimental.pallas import tpu as pltpu
from jax.sharding import PartitionSpec as P

F32, BF16 = jnp.float32, jnp.bfloat16
VMEM = pl.BlockSpec(memory_space=pltpu.VMEM)
MIB = 1024 * 1024


def two_parts(value):
    high = value.astype(BF16)
    return high, (value - high.astype(F32)).astype(BF16)


def place():
    ka, ma = lax.axis_index("ka"), lax.axis_index("ma")
    return ka // 2, ka % 2, ma % 2, ma // 2


def dot(a, b):
    return jnp.dot(a, b, preferred_element_type=F32)


def early_kernel(a_ref, b0, b1, b2, b3, sums, high_out, low_out, b_high, b_low):
    _, _, half, own_x = place()
    for index, b_ref in enumerate((b0, b1, b2, b3)):
        rows = slice(128 * index, 128 * index + 128)
        b_high[rows, :], b_low[rows, :] = two_parts(b_ref[...])

    def body(a_block, sums_block, high_block, low_block):
        def parts(z):
            starts = [pl.multiple_of((2 * ((own_x + offset) % 4) + z) * 128, 128) for offset in OFFSETS]
            return two_parts(jnp.concatenate([a_block[:, pl.ds(start, 128)] for start in starts], axis=1))

        high, low = parts(half)
        sums_block[...] = dot(high, b_low[...]) + dot(low, b_high[...]) + dot(high, b_high[...])
        high_block[...], low_block[...] = parts(1 - half)

    spec = pl.BlockSpec((256, 512), lambda i: (i, 0))
    pltpu.emit_pipeline(
        body, grid=(8,), in_specs=[pl.BlockSpec((256, 1024), lambda i: (i, 0))], out_specs=[spec] * 3
    )(a_ref, sums, high_out, low_out)


def early(a, near_b):
    return pl.pallas_call(
        early_kernel,
        in_specs=[pl.BlockSpec(memory_space=pltpu.HBM)] + [VMEM] * 4,
        out_specs=[pl.BlockSpec(memory_space=pl.ANY)] * 3,
        out_shape=[jax.ShapeDtypeStruct((2048, 512), kind) for kind in (F32, BF16, BF16)],
        scratch_shapes=[pltpu.VMEM((512, 512), BF16)] * 2,
        compiler_params=pltpu.CompilerParams(vmem_limit_bytes=12 * MIB),
        cost_estimate=pl.CostEstimate(flops=2 * 3 * 2048 * 512 * 512, bytes_accessed=16 * MIB, transcendentals=0),
    )(a, *near_b)


def late_kernel(shifts, mine, a_high, a_low, early_ref, b0, b1, b2, b3, out, b_high, b_low):
    y, core, _, _ = place()
    side = core if mine else 1 - core
    for index, b_ref in enumerate((b0, b1, b2, b3)):
        rows = slice(128 * index, 128 * index + 128)
        b_high[rows, :], b_low[rows, :] = two_parts(b_ref[...])
    at = 0
    for shift in shifts:
        if shift in (0, 4):
            start, count = ((y + shift) % 8) * 256 + side * 128, 128
        else:
            start, count = ((y + jnp.where(side == 0, shift, 8 - shift)) % 8) * 256, 256
        rows = pl.ds(pl.multiple_of(start, 128), count)
        high, low = a_high[rows, :], a_low[rows, :]
        total = dot(high, b_low[...]) + dot(low, b_high[...]) + dot(high, b_high[...])
        out[at : at + count, :] = early_ref[rows, :] + total
        at += count


def late(shifts, mine, a_high, a_low, sums, far_b):
    count = sum(128 if shift in (0, 4) else 256 for shift in shifts)
    return pl.pallas_call(
        lambda *refs: late_kernel(shifts, mine, *refs),
        in_specs=[VMEM] * 7,
        out_specs=VMEM,
        out_shape=jax.ShapeDtypeStruct((count, 512), F32),
        scratch_shapes=[pltpu.VMEM((512, 512), BF16)] * 2,
        compiler_params=pltpu.CompilerParams(vmem_limit_bytes=14 * MIB),
        cost_estimate=pl.CostEstimate(flops=2 * 3 * count * 512 * 512, bytes_accessed=10 * MIB, transcendentals=0),
    )(a_high, a_low, sums, *far_b)


def add_kernel(first, second, *outs):
    at = 0
    for out in outs:
        rows = slice(at, at + out.shape[0])
        out[...] = first[rows, :] + second[rows, :]
        at += out.shape[0]


def add(first, second, *counts):
    return pl.pallas_call(
        add_kernel,
        in_specs=[VMEM] * 2,
        out_specs=[VMEM] * len(counts),
        out_shape=[jax.ShapeDtypeStruct((count, 512), F32) for count in counts],
        compiler_params=pltpu.CompilerParams(vmem_limit_bytes=6 * MIB),
        cost_estimate=pl.CostEstimate(flops=MIB, bytes_accessed=4 * MIB, transcendentals=0),
    )(first, second)


def pass_on_kernel(two, got_three, got_four, own, other):
    _, core, _, _ = place()
    for index, out in ((core, own), (1 - core, other)):
        rows = pl.ds(pl.multiple_of(index * 128, 128), 128)
        total = two[rows, :] + got_three[rows, :]
        out[...] = total + got_four[...] if out is own else total


def here_kernel(zero, got_one, keep, give):
    _, core, _, _ = place()
    keep[...] = zero[...] + got_one[pl.ds(pl.multiple_of(core * 128, 128), 128), :]
    give[...] = got_one[pl.ds(pl.multiple_of((1 - core) * 128, 128), 128), :]


def halves(kernel, *args):
    return pl.pallas_call(
        kernel,
        in_specs=[VMEM] * len(args),
        out_specs=[VMEM] * 2,
        out_shape=[jax.ShapeDtypeStruct((128, 512), F32)] * 2,
        compiler_params=pltpu.CompilerParams(vmem_limit_bytes=4 * MIB),
        cost_estimate=pl.CostEstimate(flops=MIB, bytes_accessed=2 * MIB, transcendentals=0),
    )(*args)


def along_y(distance, cross=0):
    return [(i, ((i + (2 * distance if i % 2 == 0 else -2 * distance)) % 16) ^ cross) for i in range(16)]


CORES = [(i, i ^ 1) for i in range(16)]
HALVES = [(i, i ^ 1) for i in range(8)]


FAR, NEAR = (3, 1, 4), (2, 0)
OFFSETS = (0, -1, 1, 2)


def by_x(offset):
    pairs = []
    for ma in range(8):
        for ka in range(16):
            step = 2 if offset == 2 and ka % 2 == 0 else -offset
            pairs.append((ma * 16 + ka, ((ma + 2 * step) % 8) * 16 + ka))
    return pairs


def shards(left_matrix, right_panel):
    def from_row(b):
        return [b] + [lax.ppermute(b, ("ma", "ka"), by_x(offset)) for offset in OFFSETS[1:]]

    far_b = from_row(lax.ppermute(right_panel, "ma", HALVES))
    sums, a_high, a_low = early(left_matrix, from_row(right_panel))

    def rest(shifts, mine, sums):
        return late(shifts, mine, a_high, a_low, sums, far_b)

    three, one, four = add(lax.ppermute(rest(FAR, False, sums), "ka", CORES), rest(FAR, True, sums), 256, 256, 128)
    sent = rest(NEAR, False, sums)
    three, four, one, sent, sums = lax.optimization_barrier((three, four, one, sent, sums))
    got_three = lax.ppermute(three, "ka", along_y(1))
    got_four = lax.ppermute(four, "ka", along_y(2))
    got_one = lax.ppermute(one, "ka", along_y(1))
    two, zero = add(lax.ppermute(sent, "ka", CORES), rest(NEAR, True, sums), 256, 128)

    own, other = halves(pass_on_kernel, two, got_three, got_four)
    got_own = lax.ppermute(own, "ka", along_y(2))
    got_other = lax.ppermute(other, "ka", along_y(2, 1))

    keep, give = halves(here_kernel, zero, got_one)
    got_give = lax.ppermute(give, "ka", CORES)
    return keep + got_give + got_own + got_other


def solution(mesh):
    in_specs = (P("ma", "ka"), P(("ka", "ma"), "an"))
    out_specs = P(("ma", "ka"), "an")
    return jax.shard_map(shards, mesh=mesh, in_specs=in_specs, out_specs=out_specs, check_vma=False)
```

time: 161 us -> 87.9 us (0.55)
  waiting for transfers between devices: 128 us -> 16.8 us
  starting transfers between devices: 0.04 us -> 53.3 us
  matrix products: 17.5 us -> 0 us
  between operations: 13.4 us -> 0.27 us
  Pallas kernels: 0 us -> 11.6 us
  local copies, waits for them, and re-layouts: 0 us -> 4.32 us
    all_gather x1 -> x0, waiting for transfers between devices: 65 us -> none  [shards(): b_local = lax.all_gather(right_panel, 'ma', axis=0, tiled=True)]
    reduce_scatter x1 -> x0, waiting for transfers between devices: 62.6 us -> none  [shards(): lax.psum_scatter(partial_value, 'ka', scatter_dimension=0, tiled=True)]
    ppermute x0 -> x15, starting transfers between devices: none -> 53.3 us  [the longest x6 18.6 us: from_row(): lax.ppermute(b, ('ma', 'ka'), by_x(offset))]
    dot_general x1 -> x0, matrix products: 17.5 us -> none  [shards(): jnp.dot(left_matrix, b_local, preferred_element_type=jnp.float32, precisi...]
    ppermute x0 -> x15, waiting for transfers between devices: none -> 16.8 us  [the longest x1 9.8 us: shards(): got_four = lax.ppermute(four, 'ka', along_y(2))]
    pallas_call x0 -> x9, Pallas kernels: none -> 11.6 us  [the longest x1 7.26 us: early(): pl.pallas_call(early_kernel, in_specs=[pl.BlockSpec(memory_space=pltpu.HB...]
    unnamed x0 -> x4, local copies, waits for them, and re-layouts: none -> 4.32 us
  transfers between devices with their start and end apart: 2 -> 15, of which waited for: 2 -> 3; matrix products, arithmetic and copies ran while one was open for 0% -> 0% of each run, Pallas kernels for 0% -> 12%
where the time goes in v2:
time: 87.9 us; the launch traced here: 87.1 us
  starting transfers between devices  53.3 us (61%)
  waiting for transfers between devices  16.8 us (19%)
  Pallas kernels  11.6 us (13%)
  local copies, waits for them, and re-layouts  4.32 us (5%)
    ppermute x6, starting transfers between devices, from_row(): lax.ppermute(b, ('ma', 'ka'), by_x(offset))  18.6 us
    ppermute x1, waiting for transfers between devices, shards(): got_four = lax.ppermute(four, 'ka', along_y(2))  9.8 us
    ppermute x1, starting transfers between devices, shards(): lax.ppermute(rest(FAR, False, sums), 'ka', CORES)  7.56 us
    pallas_call x1, Pallas kernels, early(): pl.pallas_call(early_kernel, in_specs=[pl.BlockSpec(memory_space=pltpu.HB...  7.26 us
    ppermute x1, waiting for transfers between devices, shards(): got_own = lax.ppermute(own, 'ka', along_y(2))  6.31 us
    ppermute x1, starting transfers between devices, shards(): got_own = lax.ppermute(own, 'ka', along_y(2))  5.51 us
    ppermute x1, starting transfers between devices, shards(): far_b = from_row(lax.ppermute(right_panel, 'ma', HALVES))  4.82 us
    unnamed x4, local copies, waits for them, and re-layouts  4.32 us
  transfers between devices with their start and end apart: 15, of which 3 were waited for; matrix products, arithmetic and copies ran while one was open for 0% of the time, Pallas kernels for 12%

profile of v2, /device:TPU:1, one launch (start us, length us, event | category | flops | bytes accessed | tf_op | source)
XLA Modules:
  0.0 87.1 jit_solution(14262380279229545454)
XLA Ops:
  0.0 4.8 %collective-permute-start.3 = (f32[128,512]{1,0:T(8,128)}, f32[128,512]{1,0:T(8,128)S(1)}, u32[]{:S(2)}, u32[]{:S(2)}) collective-permute-start(f32[128,512]{1,0:T(8,128)} %b0.1), channel_id=1, source_target_pairs={{0,64},{64,0},{128,192},{192,128},{256,320},{320,256},{384,448},{4... | collective-permute-start | bytes 786440 | tf_op jit(solution)/shard_map/ppermute | solution.py:161
  4.8 3.1 %collective-permute-start = (f32[128,512]{1,0:T(8,128)}, f32[128,512]{1,0:T(8,128)S(1)}, u32[]{:S(2)}, u32[]{:S(2)}) collective-permute-start(f32[128,512]{1,0:T(8,128)} %b0.1), channel_id=1, source_target_pairs={{0,128},{4,132},{8,136},{12,140},{16,144},{20,148},{24,152},{28,15... | collective-permute-start | bytes 786440 | tf_op jit(solution)/shard_map/ppermute | solution.py:159
  8.0 3.4 %collective-permute-start.1 = (f32[128,512]{1,0:T(8,128)}, f32[128,512]{1,0:T(8,128)S(1)}, u32[]{:S(2)}, u32[]{:S(2)}) collective-permute-start(f32[128,512]{1,0:T(8,128)} %b0.1), channel_id=1, source_target_pairs={{0,384},{4,388},{8,392},{12,396},{16,400},{20,404},{24,408},{28,41... | collective-permute-start | bytes 786440 | tf_op jit(solution)/shard_map/ppermute | solution.py:159
  11.3 3.4 %collective-permute-start.2 = (f32[128,512]{1,0:T(8,128)}, f32[128,512]{1,0:T(8,128)S(1)}, u32[]{:S(2)}, u32[]{:S(2)}) collective-permute-start(f32[128,512]{1,0:T(8,128)} %b0.1), channel_id=1, source_target_pairs={{0,256},{4,260},{8,264},{12,268},{16,272},{20,276},{24,280},{28,28... | collective-permute-start | bytes 786440 | tf_op jit(solution)/shard_map/ppermute | solution.py:159
  14.8 0.0 collective-permute-done.3.refs_3_
  14.8 2.2 %collective-permute-start.4 = (f32[128,512]{1,0:T(8,128)S(1)}, f32[128,512]{1,0:T(8,128)S(1)}, u32[]{:S(2)}, u32[]{:S(2)}) collective-permute-start(f32[128,512]{1,0:T(8,128)S(1)} %collective-permute-done.3.refs_3_), channel_id=1, source_target_pairs={{0,128},{4,132},{8,136},{12,140},{16,144},{20,148},{24,152},{28,15... | collective-permute-start | bytes 786440 | tf_op jit(solution)/shard_map/ppermute | solution.py:159
  17.0 4.3 %collective-permute-start.5 = (f32[128,512]{1,0:T(8,128)S(1)}, f32[128,512]{1,0:T(8,128)S(1)}, u32[]{:S(2)}, u32[]{:S(2)}) collective-permute-start(f32[128,512]{1,0:T(8,128)S(1)} %collective-permute-done.3.refs_3_), channel_id=1, source_target_pairs={{0,384},{4,388},{8,392},{12,396},{16,400},{20,404},{24,408},{28,41... | collective-permute-start | bytes 786440 | tf_op jit(solution)/shard_map/ppermute | solution.py:159
  21.3 0.0 collective-permute-done.b1
  21.3 2.1 %collective-permute-start.6 = (f32[128,512]{1,0:T(8,128)S(1)}, f32[128,512]{1,0:T(8,128)S(1)}, u32[]{:S(2)}, u32[]{:S(2)}) collective-permute-start(f32[128,512]{1,0:T(8,128)S(1)} %collective-permute-done.3.refs_3_), channel_id=1, source_target_pairs={{0,256},{4,260},{8,264},{12,268},{16,272},{20,276},{24,280},{28,28... | collective-permute-start | bytes 786440 | tf_op jit(solution)/shard_map/ppermute | solution.py:159
  23.5 0.0 collective-permute-done.1.b2
  23.5 0.0 collective-permute-done.2.b3
  23.5 0.0 copy-start
  23.5 3.4 %copy-done = f32[2048,1024]{1,0:T(8,128)S(1)} copy-done((f32[2048,1024]{1,0:T(8,128)S(1)}, f32[2048,1024]{1,0:T(8,128)}, u32[]{:S(2)}) %copy-start) | copy-done | bytes 8388632
  26.9 0.0 copy-start.1
  26.9 0.9 %copy-done.1 = f32[128,512]{1,0:T(8,128)S(1)} copy-done((f32[128,512]{1,0:T(8,128)S(1)}, f32[128,512]{1,0:T(8,128)}, u32[]{:S(2)}) %copy-start.1) | copy-done | bytes 262168
  27.8 7.3 %shard_map.28 = (f32[2048,512]{1,0:T(8,128)S(1)}, bf16[2048,512]{1,0:T(8,128)(2,1)S(1)}, bf16[2048,512]{1,0:T(8,128)(2,1)S(1)}) custom-call(f32[2048,1024]{1,0:T(8,128)S(1)} %copy-done, f32[128,512]{1,0:T(8,128)S(1)} %copy-done.1, f32[128,512]{1,0:T(8,128)S(1)} %collective-permute-done.b1, f32[128,512]{1,0:T(8,128)S(1)} %collective-permute-done.1.b2, ...), custom_call_target="tpu_custom_call" | custom-call | flops 3221225472 | bytes 16777216 | tf_op jit(solution)/shard_map/pallas_call | solution.py:49
  35.1 0.0 collective-permute-done.4.refs_4_
  35.1 0.0 collective-permute-done.5.refs_5_
  35.1 0.0 collective-permute-done.6.refs_6_
  35.1 1.2 %shard_map.29 = f32[640,512]{1,0:T(8,128)S(1)} custom-call(bf16[2048,512]{1,0:T(8,128)(2,1)S(1)} %get-tuple-element.22.refs_0_, bf16[2048,512]{1,0:T(8,128)(2,1)S(1)} %get-tuple-element.23.refs_1_, f32[2048,512]{1,0:T(8,128)S(1)} %get-tuple-element.29.refs_2_, f32[128,512]{1,0:T(8,128)S(1)} %collective-permute-done.3.refs_3_, ...), custom_call_target="tpu_custom_call" | custom-call | flops 1006632960 | bytes 10485760 | tf_op jit(solution)/shard_map/pallas_call | solution.py:81
  36.3 7.6 %collective-permute-start.7 = (f32[640,512]{1,0:T(8,128)S(1)}, f32[640,512]{1,0:T(8,128)S(1)}, u32[]{:S(2)}, u32[]{:S(2)}) collective-permute-start(f32[640,512]{1,0:T(8,128)S(1)} %shard_map.29), channel_id=1, source_target_pairs={{0,4},{4,0},{8,12},{12,8},{16,20},{20,16},{24,28},{28,24},{32,36},... | collective-permute-start | bytes 3932168 | tf_op jit(solution)/shard_map/ppermute | solution.py:167
  43.9 0.8 shard_map.32
  44.7 1.2 %shard_map.30.second = f32[640,512]{1,0:T(8,128)S(1)} custom-call(bf16[2048,512]{1,0:T(8,128)(2,1)S(1)} %get-tuple-element.22.refs_0_, bf16[2048,512]{1,0:T(8,128)(2,1)S(1)} %get-tuple-element.23.refs_1_, f32[2048,512]{1,0:T(8,128)S(1)} %get-tuple-element.29.refs_2_, f32[128,512]{1,0:T(8,128)S(1)} %collective-permute-done.3.refs_3_, ...), custom_call_target="tpu_custom_call" | custom-call | flops 1006632960 | bytes 10485760 | tf_op jit(solution)/shard_map/pallas_call | solution.py:81
  45.9 0.6 collective-permute-done.7.first
  46.5 0.1 shard_map.31
  46.7 2.3 %collective-permute-start.8 = (f32[384,512]{1,0:T(8,128)S(1)}, f32[384,512]{1,0:T(8,128)S(1)}, u32[]{:S(2)}, u32[]{:S(2)}) collective-permute-start(f32[384,512]{1,0:T(8,128)S(1)} %shard_map.32), channel_id=1, source_target_pairs={{0,4},{4,0},{8,12},{12,8},{16,20},{20,16},{24,28},{28,24},{32,36},... | collective-permute-start | bytes 2359304 | tf_op jit(solution)/shard_map/ppermute | solution.py:173
  48.9 2.1 %collective-permute-start.11 = (f32[256,512]{1,0:T(8,128)S(1)}, f32[256,512]{1,0:T(8,128)S(1)}, u32[]{:S(2)}, u32[]{:S(2)}) collective-permute-start(f32[256,512]{1,0:T(8,128)S(1)} %get-tuple-element.35), channel_id=1, source_target_pairs={{0,8},{4,60},{8,16},{12,4},{16,24},{20,12},{24,32},{28,20},{32,40}... | collective-permute-start | bytes 1572872 | tf_op jit(solution)/shard_map/ppermute | solution.py:170
  51.0 3.0 %collective-permute-start.9 = (f32[256,512]{1,0:T(8,128)S(1)}, f32[256,512]{1,0:T(8,128)S(1)}, u32[]{:S(2)}, u32[]{:S(2)}) collective-permute-start(f32[256,512]{1,0:T(8,128)S(1)} %get-tuple-element.31), channel_id=1, source_target_pairs={{0,8},{4,60},{8,16},{12,4},{16,24},{20,12},{24,32},{28,20},{32,40}... | collective-permute-start | bytes 1572872 | tf_op jit(solution)/shard_map/ppermute | solution.py:172
  54.0 3.8 %collective-permute-start.12 = (f32[128,512]{1,0:T(8,128)S(1)}, f32[128,512]{1,0:T(8,128)S(1)}, u32[]{:S(2)}, u32[]{:S(2)}) collective-permute-start(f32[128,512]{1,0:T(8,128)S(1)} %get-tuple-element.36), channel_id=1, source_target_pairs={{0,16},{4,52},{8,24},{12,60},{16,32},{20,4},{24,40},{28,12},{32,48... | collective-permute-start | bytes 786440 | tf_op jit(solution)/shard_map/ppermute | solution.py:171
  57.8 0.8 shard_map.33.second
  58.6 0.0 collective-permute-done.8.first
  58.6 0.1 shard_map.34
  58.7 9.8 %collective-permute-done.12.got_four = f32[128,512]{1,0:T(8,128)S(1)} collective-permute-done((f32[128,512]{1,0:T(8,128)S(1)}, f32[128,512]{1,0:T(8,128)S(1)}, u32[]{:S(2)}, u32[]{:S(2)}) %collective-permute-start.12) | collective-permute-done | bytes 262176 | tf_op jit(solution)/shard_map/ppermute | solution.py:171
  68.5 0.0 collective-permute-done.11.got_three
  68.5 0.1 shard_map.36
  68.6 3.8 %collective-permute-start.14 = (f32[128,512]{1,0:T(8,128)S(1)}, f32[128,512]{1,0:T(8,128)S(1)}, u32[]{:S(2)}, u32[]{:S(2)}) collective-permute-start(f32[128,512]{1,0:T(8,128)S(1)} %get-tuple-element.38), channel_id=1, source_target_pairs={{0,20},{4,48},{8,28},{12,56},{16,36},{20,0},{24,44},{28,8},{32,52}... | collective-permute-start | bytes 786440 | tf_op jit(solution)/shard_map/ppermute | solution.py:177
  72.4 5.5 %collective-permute-start.13 = (f32[128,512]{1,0:T(8,128)S(1)}, f32[128,512]{1,0:T(8,128)S(1)}, u32[]{:S(2)}, u32[]{:S(2)}) collective-permute-start(f32[128,512]{1,0:T(8,128)S(1)} %get-tuple-element.37), channel_id=1, source_target_pairs={{0,16},{4,52},{8,24},{12,60},{16,32},{20,4},{24,40},{28,12},{32,48... | collective-permute-start | bytes 786440 | tf_op jit(solution)/shard_map/ppermute | solution.py:176
  77.9 0.0 collective-permute-done.9.got_one
  77.9 0.1 shard_map.35
  78.0 1.9 %collective-permute-start.10 = (f32[128,512]{1,0:T(8,128)S(1)}, f32[128,512]{1,0:T(8,128)S(1)}, u32[]{:S(2)}, u32[]{:S(2)}) collective-permute-start(f32[128,512]{1,0:T(8,128)S(1)} %get-tuple-element.33), channel_id=1, source_target_pairs={{0,4},{4,0},{8,12},{12,8},{16,20},{20,16},{24,28},{28,24},{32,36},... | collective-permute-start | bytes 786440 | tf_op jit(solution)/shard_map/ppermute | solution.py:180
  79.9 0.0 collective-permute-done.14
  79.9 6.3 %collective-permute-done.13 = f32[128,512]{1,0:T(8,128)S(1)} collective-permute-done((f32[128,512]{1,0:T(8,128)S(1)}, f32[128,512]{1,0:T(8,128)S(1)}, u32[]{:S(2)}, u32[]{:S(2)}) %collective-permute-start.13) | collective-permute-done | bytes 262176 | tf_op jit(solution)/shard_map/ppermute | solution.py:176
  86.3 0.0 collective-permute-done.10
  86.3 0.8 add_add_fusion
Async XLA Ops:
  0.0 14.8 %collective-permute-start.3 = (f32[128,512]{1,0:T(8,128)}, f32[128,512]{1,0:T(8,128)S(1)}, u32[]{:S(2)}, u32[]{:S(2)}) collective-permute-start(f32[128,512]{1,0:T(8,128)} %b0.1), channel_id=1, source_target_pairs={{0,64},{64,0},{128,192},{192,128},{256,320},{320,256},{384,448},{4... | collective-permute-start | bytes 786440 | tf_op jit(solution)/shard_map/ppermute | solution.py:161
  4.8 16.5 %collective-permute-start = (f32[128,512]{1,0:T(8,128)}, f32[128,512]{1,0:T(8,128)S(1)}, u32[]{:S(2)}, u32[]{:S(2)}) collective-permute-start(f32[128,512]{1,0:T(8,128)} %b0.1), channel_id=1, source_target_pairs={{0,128},{4,132},{8,136},{12,140},{16,144},{20,148},{24,152},{28,15... | collective-permute-start | bytes 786440 | tf_op jit(solution)/shard_map/ppermute | solution.py:159
  8.0 15.5 %collective-permute-start.1 = (f32[128,512]{1,0:T(8,128)}, f32[128,512]{1,0:T(8,128)S(1)}, u32[]{:S(2)}, u32[]{:S(2)}) collective-permute-start(f32[128,512]{1,0:T(8,128)} %b0.1), channel_id=1, source_target_pairs={{0,384},{4,388},{8,392},{12,396},{16,400},{20,404},{24,408},{28,41... | collective-permute-start | bytes 786440 | tf_op jit(solution)/shard_map/ppermute | solution.py:159
  11.3 12.1 %collective-permute-start.2 = (f32[128,512]{1,0:T(8,128)}, f32[128,512]{1,0:T(8,128)S(1)}, u32[]{:S(2)}, u32[]{:S(2)}) collective-permute-start(f32[128,512]{1,0:T(8,128)} %b0.1), channel_id=1, source_target_pairs={{0,256},{4,260},{8,264},{12,268},{16,272},{20,276},{24,280},{28,28... | collective-permute-start | bytes 786440 | tf_op jit(solution)/shard_map/ppermute | solution.py:159
  14.8 20.3 %collective-permute-start.4 = (f32[128,512]{1,0:T(8,128)S(1)}, f32[128,512]{1,0:T(8,128)S(1)}, u32[]{:S(2)}, u32[]{:S(2)}) collective-permute-start(f32[128,512]{1,0:T(8,128)S(1)} %collective-permute-done.3.refs_3_), channel_id=1, source_target_pairs={{0,128},{4,132},{8,136},{12,140},{16,144},{20,148},{24,152},{28,15... | collective-permute-start | bytes 786440 | tf_op jit(solution)/shard_map/ppermute | solution.py:159
  17.0 18.1 %collective-permute-start.5 = (f32[128,512]{1,0:T(8,128)S(1)}, f32[128,512]{1,0:T(8,128)S(1)}, u32[]{:S(2)}, u32[]{:S(2)}) collective-permute-start(f32[128,512]{1,0:T(8,128)S(1)} %collective-permute-done.3.refs_3_), channel_id=1, source_target_pairs={{0,384},{4,388},{8,392},{12,396},{16,400},{20,404},{24,408},{28,41... | collective-permute-start | bytes 786440 | tf_op jit(solution)/shard_map/ppermute | solution.py:159
  21.3 13.8 %collective-permute-start.6 = (f32[128,512]{1,0:T(8,128)S(1)}, f32[128,512]{1,0:T(8,128)S(1)}, u32[]{:S(2)}, u32[]{:S(2)}) collective-permute-start(f32[128,512]{1,0:T(8,128)S(1)} %collective-permute-done.3.refs_3_), channel_id=1, source_target_pairs={{0,256},{4,260},{8,264},{12,268},{16,272},{20,276},{24,280},{28,28... | collective-permute-start | bytes 786440 | tf_op jit(solution)/shard_map/ppermute | solution.py:159
  23.5 3.4 %copy-start = (f32[2048,1024]{1,0:T(8,128)S(1)}, f32[2048,1024]{1,0:T(8,128)}, u32[]{:S(2)}) copy-start(f32[2048,1024]{1,0:T(8,128)} %a_ref.1) | copy-start | bytes 25165828
  26.9 0.9 %copy-start.1 = (f32[128,512]{1,0:T(8,128)S(1)}, f32[128,512]{1,0:T(8,128)}, u32[]{:S(2)}) copy-start(f32[128,512]{1,0:T(8,128)} %b0.1) | copy-start | bytes 786436
  36.3 10.2 %collective-permute-start.7 = (f32[640,512]{1,0:T(8,128)S(1)}, f32[640,512]{1,0:T(8,128)S(1)}, u32[]{:S(2)}, u32[]{:S(2)}) collective-permute-start(f32[640,512]{1,0:T(8,128)S(1)} %shard_map.29), channel_id=1, source_target_pairs={{0,4},{4,0},{8,12},{12,8},{16,20},{20,16},{24,28},{28,24},{32,36},... | collective-permute-start | bytes 3932168 | tf_op jit(solution)/shard_map/ppermute | solution.py:167
  46.7 11.9 %collective-permute-start.8 = (f32[384,512]{1,0:T(8,128)S(1)}, f32[384,512]{1,0:T(8,128)S(1)}, u32[]{:S(2)}, u32[]{:S(2)}) collective-permute-start(f32[384,512]{1,0:T(8,128)S(1)} %shard_map.32), channel_id=1, source_target_pairs={{0,4},{4,0},{8,12},{12,8},{16,20},{20,16},{24,28},{28,24},{32,36},... | collective-permute-start | bytes 2359304 | tf_op jit(solution)/shard_map/ppermute | solution.py:173
  48.9 19.5 %collective-permute-start.11 = (f32[256,512]{1,0:T(8,128)S(1)}, f32[256,512]{1,0:T(8,128)S(1)}, u32[]{:S(2)}, u32[]{:S(2)}) collective-permute-start(f32[256,512]{1,0:T(8,128)S(1)} %get-tuple-element.35), channel_id=1, source_target_pairs={{0,8},{4,60},{8,16},{12,4},{16,24},{20,12},{24,32},{28,20},{32,40}... | collective-permute-start | bytes 1572872 | tf_op jit(solution)/shard_map/ppermute | solution.py:170
  51.0 26.9 %collective-permute-start.9 = (f32[256,512]{1,0:T(8,128)S(1)}, f32[256,512]{1,0:T(8,128)S(1)}, u32[]{:S(2)}, u32[]{:S(2)}) collective-permute-start(f32[256,512]{1,0:T(8,128)S(1)} %get-tuple-element.31), channel_id=1, source_target_pairs={{0,8},{4,60},{8,16},{12,4},{16,24},{20,12},{24,32},{28,20},{32,40}... | collective-permute-start | bytes 1572872 | tf_op jit(solution)/shard_map/ppermute | solution.py:172
  54.0 14.5 %collective-permute-start.12 = (f32[128,512]{1,0:T(8,128)S(1)}, f32[128,512]{1,0:T(8,128)S(1)}, u32[]{:S(2)}, u32[]{:S(2)}) collective-permute-start(f32[128,512]{1,0:T(8,128)S(1)} %get-tuple-element.36), channel_id=1, source_target_pairs={{0,16},{4,52},{8,24},{12,60},{16,32},{20,4},{24,40},{28,12},{32,48... | collective-permute-start | bytes 786440 | tf_op jit(solution)/shard_map/ppermute | solution.py:171
  68.6 11.4 %collective-permute-start.14 = (f32[128,512]{1,0:T(8,128)S(1)}, f32[128,512]{1,0:T(8,128)S(1)}, u32[]{:S(2)}, u32[]{:S(2)}) collective-permute-start(f32[128,512]{1,0:T(8,128)S(1)} %get-tuple-element.38), channel_id=1, source_target_pairs={{0,20},{4,48},{8,28},{12,56},{16,36},{20,0},{24,44},{28,8},{32,52}... | collective-permute-start | bytes 786440 | tf_op jit(solution)/shard_map/ppermute | solution.py:177
  72.4 13.8 %collective-permute-start.13 = (f32[128,512]{1,0:T(8,128)S(1)}, f32[128,512]{1,0:T(8,128)S(1)}, u32[]{:S(2)}, u32[]{:S(2)}) collective-permute-start(f32[128,512]{1,0:T(8,128)S(1)} %get-tuple-element.37), channel_id=1, source_target_pairs={{0,16},{4,52},{8,24},{12,60},{16,32},{20,4},{24,40},{28,12},{32,48... | collective-permute-start | bytes 786440 | tf_op jit(solution)/shard_map/ppermute | solution.py:176
  78.0 8.3 %collective-permute-start.10 = (f32[128,512]{1,0:T(8,128)S(1)}, f32[128,512]{1,0:T(8,128)S(1)}, u32[]{:S(2)}, u32[]{:S(2)}) collective-permute-start(f32[128,512]{1,0:T(8,128)S(1)} %get-tuple-element.33), channel_id=1, source_target_pairs={{0,4},{4,0},{8,12},{12,8},{16,20},{20,16},{24,28},{28,24},{32,36},... | collective-permute-start | bytes 786440 | tf_op jit(solution)/shard_map/ppermute | solution.py:180

commit v3 on v2

v3 whole, which is shorter than its diff:
```python
import jax
import jax.numpy as jnp
from jax import lax
from jax.experimental import pallas as pl
from jax.experimental.pallas import tpu as pltpu
from jax.sharding import PartitionSpec as P

F32, BF16 = jnp.float32, jnp.bfloat16
VMEM = pl.BlockSpec(memory_space=pltpu.VMEM)
MIB = 1024 * 1024


def two_parts(value):
    high = value.astype(BF16)
    return high, (value - high.astype(F32)).astype(BF16)


def place():
    ka, ma = lax.axis_index("ka"), lax.axis_index("ma")
    return ka // 2, ka % 2, ma % 2, ma // 2


def dot(a, b):
    return jnp.dot(a, b, preferred_element_type=F32)


def place_parts(pieces, high, low):
    _, _, _, own_x = place()
    for offset, piece in zip(OFFSETS, pieces):
        rows = pl.ds(pl.multiple_of(((own_x + offset) % 4) * 128, 128), 128)
        high[rows, :], low[rows, :] = two_parts(piece[...])


def early_kernel(a_hbm, b0_hbm, b1, b2, b3, sums, high_out, low_out, a_ref, b0, b_high, b_low, a_sems, b_sem):
    _, _, half, _ = place()

    def load(step):
        return pltpu.make_async_copy(a_hbm.at[pl.ds(256 * step, 256)], a_ref.at[step], a_sems.at[step])

    b_load = pltpu.make_async_copy(b0_hbm, b0, b_sem)
    b_load.start()
    for step in range(8):
        load(step).start()
    b_load.wait()
    place_parts((b0, b1, b2, b3), b_high, b_low)
    for z in range(2):

        @pl.when(half == z)
        def _(z=z):
            @pl.loop(0, 8)
            def _(step):
                load(step).wait()

                def parts(z):
                    blocks = [a_ref[step, :, 256 * x + 128 * z : 256 * x + 128 * z + 128] for x in range(4)]
                    return two_parts(jnp.concatenate(blocks, axis=1))

                rows = pl.ds(pl.multiple_of(256 * step, 256), 256)
                high, low = parts(z)
                sums[rows, :] = dot(high, b_low[...]) + dot(low, b_high[...]) + dot(high, b_high[...])
                high_out[rows, :], low_out[rows, :] = parts(1 - z)


def early(a, near_b):
    kept = pl.BlockSpec(memory_space=pl.ANY)
    return pl.pallas_call(
        early_kernel,
        in_specs=[kept] * 2 + [VMEM] * 3,
        out_specs=[VMEM] * 3,
        out_shape=[jax.ShapeDtypeStruct((2048, 512), kind) for kind in (F32, BF16, BF16)],
        scratch_shapes=[
            pltpu.VMEM((8, 256, 1024), F32),
            pltpu.VMEM((128, 512), F32),
            pltpu.VMEM((512, 512), BF16),
            pltpu.VMEM((512, 512), BF16),
            pltpu.SemaphoreType.DMA((8,)),
            pltpu.SemaphoreType.DMA,
        ],
        compiler_params=pltpu.CompilerParams(vmem_limit_bytes=42 * MIB),
        cost_estimate=pl.CostEstimate(flops=2 * 3 * 2048 * 512 * 512, bytes_accessed=16 * MIB, transcendentals=0),
    )(a, *near_b)


def late_kernel(shifts, mine, a_high, a_low, early_ref, b0, b1, b2, b3, out, b_high, b_low):
    y, core, _, _ = place()
    side = core if mine else 1 - core
    place_parts((b0, b1, b2, b3), b_high, b_low)
    at = 0
    for shift in shifts:
        if shift in (0, 4):
            start, count = ((y + shift) % 8) * 256 + side * 128, 128
        else:
            start, count = ((y + jnp.where(side == 0, shift, 8 - shift)) % 8) * 256, 256
        rows = pl.ds(pl.multiple_of(start, 128), count)
        high, low = a_high[rows, :], a_low[rows, :]
        total = dot(high, b_low[...]) + dot(low, b_high[...]) + dot(high, b_high[...])
        out[at : at + count, :] = early_ref[rows, :] + total
        at += count


def late(shifts, mine, a_high, a_low, sums, far_b):
    count = sum(128 if shift in (0, 4) else 256 for shift in shifts)
    return pl.pallas_call(
        lambda *refs: late_kernel(shifts, mine, *refs),
        in_specs=[VMEM] * 7,
        out_specs=VMEM,
        out_shape=jax.ShapeDtypeStruct((count, 512), F32),
        scratch_shapes=[pltpu.VMEM((512, 512), BF16)] * 2,
        compiler_params=pltpu.CompilerParams(vmem_limit_bytes=14 * MIB),
        cost_estimate=pl.CostEstimate(flops=2 * 3 * count * 512 * 512, bytes_accessed=10 * MIB, transcendentals=0),
    )(a_high, a_low, sums, *far_b)


def add_kernel(first, second, three, four, one_own, one_other, two, zero):
    _, core, _, _ = place()
    own, other = (pl.multiple_of(256 + side * 128, 128) for side in (core, 1 - core))
    for start, out in ((0, three), (own, one_own), (other, one_other), (512, four), (640, two), (896, zero)):
        rows = pl.ds(start, out.shape[0])
        out[...] = first[rows, :] + second[rows, :]


def add(first, second):
    counts = (256, 128, 128, 128, 256, 128)
    return pl.pallas_call(
        add_kernel,
        in_specs=[VMEM] * 2,
        out_specs=[VMEM] * len(counts),
        out_shape=[jax.ShapeDtypeStruct((count, 512), F32) for count in counts],
        compiler_params=pltpu.CompilerParams(vmem_limit_bytes=8 * MIB),
        cost_estimate=pl.CostEstimate(flops=MIB, bytes_accessed=4 * MIB, transcendentals=0),
    )(first, second)


def pass_on_kernel(two, got_three, got_four, own, other):
    _, core, _, _ = place()
    for index, out in ((core, own), (1 - core, other)):
        rows = pl.ds(pl.multiple_of(index * 128, 128), 128)
        total = two[rows, :] + got_three[rows, :]
        out[...] = total + got_four[...] if out is own else total


def halves(kernel, *args):
    return pl.pallas_call(
        kernel,
        in_specs=[VMEM] * len(args),
        out_specs=[VMEM] * 2,
        out_shape=[jax.ShapeDtypeStruct((128, 512), F32)] * 2,
        compiler_params=pltpu.CompilerParams(vmem_limit_bytes=4 * MIB),
        cost_estimate=pl.CostEstimate(flops=MIB, bytes_accessed=2 * MIB, transcendentals=0),
    )(*args)


def along_y(distance, cross=0):
    return [(i, ((i + (2 * distance if i % 2 == 0 else -2 * distance)) % 16) ^ cross) for i in range(16)]


CORES = [(i, i ^ 1) for i in range(16)]
HALVES = [(i, i ^ 1) for i in range(8)]


SHIFTS = (3, 1, 4, 2, 0)
OFFSETS = (0, 2, 1, -1)


def by_x(offset):
    pairs = []
    for ma in range(8):
        for ka in range(16):
            step = 2 if offset == 2 and ka % 2 == 0 else -offset
            pairs.append((ma * 16 + ka, ((ma + 2 * step) % 8) * 16 + ka))
    return pairs


def shards(left_matrix, right_panel):
    def from_row(b):
        return [b] + [lax.ppermute(b, ("ma", "ka"), by_x(offset)) for offset in OFFSETS[1:]]

    far_b = from_row(lax.ppermute(right_panel, "ma", HALVES))
    sums, a_high, a_low = early(left_matrix, from_row(right_panel))

    def rest(mine):
        return late(SHIFTS, mine, a_high, a_low, sums, far_b)

    three, four, one_own, one_other, two, zero = add(lax.ppermute(rest(False), "ka", CORES), rest(True))
    got_three = lax.ppermute(three, "ka", along_y(1))
    got_four = lax.ppermute(four, "ka", along_y(2))
    near_own = lax.ppermute(one_own, "ka", along_y(1))
    near_other = lax.ppermute(one_other, "ka", along_y(1, 1))

    own, other = halves(pass_on_kernel, two, got_three, got_four)
    far_own = lax.ppermute(own, "ka", along_y(2))
    far_other = lax.ppermute(other, "ka", along_y(2, 1))
    return zero + near_own + near_other + far_own + far_other


def solution(mesh):
    in_specs = (P("ma", "ka"), P(("ka", "ma"), "an"))
    out_specs = P(("ma", "ka"), "an")
    return jax.shard_map(shards, mesh=mesh, in_specs=in_specs, out_specs=out_specs, check_vma=False)
```

time: 87.9 us -> 82.9 us (0.943)
  local copies, waits for them, and re-layouts: 4.32 us -> 0.94 us
  starting transfers between devices: 53.3 us -> 51.8 us
  Pallas kernels: 11.6 us -> 10.7 us
    ppermute x1, waiting for transfers between devices: 9.8 us -> 1.89 us  [shards(): got_four = lax.ppermute(four, 'ka', along_y(2))]
    ppermute x6 -> x5, waiting for transfers between devices: 6.97 us -> 14.3 us  [the longest x1 7.94 us: shards(): far_other = lax.ppermute(other, 'ka', along_y(2, 1))]
    unnamed x4 -> x2, local copies, waits for them, and re-layouts: 4.32 us -> 0.94 us
    ppermute x6 -> x5, starting transfers between devices: 24.1 us -> 21.2 us  [the longest x1 6.35 us: shards(): lax.ppermute(rest(False), 'ka', CORES)]
    ppermute x1, starting transfers between devices: 2.09 us -> 3.44 us  [shards(): got_three = lax.ppermute(three, 'ka', along_y(1))]
    ppermute x6, waiting for transfers between devices: 0.02 us -> 1.23 us  [from_row(): lax.ppermute(b, ('ma', 'ka'), by_x(offset))]
    pallas_call x4 -> x2, Pallas kernels: 3.95 us -> 3.97 us  [late(): pl.pallas_call(lambda *refs: late_kernel(shifts, mine, *refs), in_specs=[...]
  transfers between devices with their start and end apart: 15 -> 14, of which waited for: 3 -> 5; matrix products, arithmetic and copies ran while one was open for 0% -> 0% of each run, Pallas kernels for 12% -> 10%
where the time goes in v3:
time: 82.9 us; the launch traced here: 81.9 us
  starting transfers between devices  51.8 us (62%)
  waiting for transfers between devices  17.4 us (21%)
  Pallas kernels  10.7 us (13%)
  local copies, waits for them, and re-layouts  0.94 us (1%)
  other arithmetic  0.83 us (1%)
    ppermute x6, starting transfers between devices, from_row(): lax.ppermute(b, ('ma', 'ka'), by_x(offset))  18.6 us
    ppermute x1, waiting for transfers between devices, shards(): far_other = lax.ppermute(other, 'ka', along_y(2, 1))  7.94 us
    pallas_call x1, Pallas kernels, early(): pl.pallas_call(early_kernel, in_specs=[kept] * 2 + [VMEM] * 3, out_specs=...  6.45 us
    ppermute x1, starting transfers between devices, shards(): lax.ppermute(rest(False), 'ka', CORES)  6.35 us
    ppermute x1, starting transfers between devices, shards(): far_own = lax.ppermute(own, 'ka', along_y(2))  5.92 us
    ppermute x1, starting transfers between devices, shards(): far_b = from_row(lax.ppermute(right_panel, 'ma', HALVES))  4.82 us
    ppermute x1, waiting for transfers between devices, shards(): far_own = lax.ppermute(own, 'ka', along_y(2))  4.61 us
    pallas_call x2, Pallas kernels, late(): pl.pallas_call(lambda *refs: late_kernel(shifts, mine, *refs), in_specs=[...  3.97 us
  transfers between devices with their start and end apart: 14, of which 5 were waited for; matrix products, arithmetic and copies ran while one was open for 0% of the time, Pallas kernels for 10%

profile of v3, /device:TPU:1, one launch (start us, length us, event | category | flops | bytes accessed | tf_op | source)
XLA Modules:
  0.0 81.9 jit_solution(3251720941935151181)
XLA Ops:
  0.0 4.8 %collective-permute-start.3 = (f32[128,512]{1,0:T(8,128)}, f32[128,512]{1,0:T(8,128)S(1)}, u32[]{:S(2)}, u32[]{:S(2)}) collective-permute-start(f32[128,512]{1,0:T(8,128)} %b0_hbm.1), channel_id=1, source_target_pairs={{0,64},{64,0},{128,192},{192,128},{256,320},{320,256},{384,448},{4... | collective-permute-start | bytes 786440 | tf_op jit(solution)/shard_map/ppermute | solution.py:178
  4.8 3.1 %collective-permute-start.2 = (f32[128,512]{1,0:T(8,128)}, f32[128,512]{1,0:T(8,128)S(1)}, u32[]{:S(2)}, u32[]{:S(2)}) collective-permute-start(f32[128,512]{1,0:T(8,128)} %b0_hbm.1), channel_id=1, source_target_pairs={{0,128},{4,132},{8,136},{12,140},{16,144},{20,148},{24,152},{28,15... | collective-permute-start | bytes 786440 | tf_op jit(solution)/shard_map/ppermute | solution.py:176
  8.0 3.4 %collective-permute-start.1 = (f32[128,512]{1,0:T(8,128)}, f32[128,512]{1,0:T(8,128)S(1)}, u32[]{:S(2)}, u32[]{:S(2)}) collective-permute-start(f32[128,512]{1,0:T(8,128)} %b0_hbm.1), channel_id=1, source_target_pairs={{0,384},{4,388},{8,392},{12,396},{16,400},{20,404},{24,408},{28,41... | collective-permute-start | bytes 786440 | tf_op jit(solution)/shard_map/ppermute | solution.py:176
  11.3 3.4 %collective-permute-start = (f32[128,512]{1,0:T(8,128)}, f32[128,512]{1,0:T(8,128)S(1)}, u32[]{:S(2)}, u32[]{:S(2)}) collective-permute-start(f32[128,512]{1,0:T(8,128)} %b0_hbm.1), channel_id=1, source_target_pairs={{0,256},{4,260},{8,264},{12,268},{16,272},{20,276},{24,280},{28,28... | collective-permute-start | bytes 786440 | tf_op jit(solution)/shard_map/ppermute | solution.py:176
  14.8 0.0 collective-permute-done.3.refs_3_
  14.8 2.2 %collective-permute-start.6 = (f32[128,512]{1,0:T(8,128)S(1)}, f32[128,512]{1,0:T(8,128)S(1)}, u32[]{:S(2)}, u32[]{:S(2)}) collective-permute-start(f32[128,512]{1,0:T(8,128)S(1)} %collective-permute-done.3.refs_3_), channel_id=1, source_target_pairs={{0,128},{4,132},{8,136},{12,140},{16,144},{20,148},{24,152},{28,15... | collective-permute-start | bytes 786440 | tf_op jit(solution)/shard_map/ppermute | solution.py:176
  17.0 4.3 %collective-permute-start.5 = (f32[128,512]{1,0:T(8,128)S(1)}, f32[128,512]{1,0:T(8,128)S(1)}, u32[]{:S(2)}, u32[]{:S(2)}) collective-permute-start(f32[128,512]{1,0:T(8,128)S(1)} %collective-permute-done.3.refs_3_), channel_id=1, source_target_pairs={{0,384},{4,388},{8,392},{12,396},{16,400},{20,404},{24,408},{28,41... | collective-permute-start | bytes 786440 | tf_op jit(solution)/shard_map/ppermute | solution.py:176
  21.3 0.0 collective-permute-done.2.b3
  21.3 2.1 %collective-permute-start.4 = (f32[128,512]{1,0:T(8,128)S(1)}, f32[128,512]{1,0:T(8,128)S(1)}, u32[]{:S(2)}, u32[]{:S(2)}) collective-permute-start(f32[128,512]{1,0:T(8,128)S(1)} %collective-permute-done.3.refs_3_), channel_id=1, source_target_pairs={{0,256},{4,260},{8,264},{12,268},{16,272},{20,276},{24,280},{28,28... | collective-permute-start | bytes 786440 | tf_op jit(solution)/shard_map/ppermute | solution.py:176
  23.5 0.0 collective-permute-done.1.b2
  23.5 0.0 collective-permute-done.b1
  23.5 0.0 copy-start
  23.5 0.9 %copy-done = f32[128,512]{1,0:T(8,128)S(1)} copy-done((f32[128,512]{1,0:T(8,128)S(1)}, f32[128,512]{1,0:T(8,128)}, u32[]{:S(2)}) %copy-start) | copy-done | bytes 262168
  24.4 6.4 %shard_map.28 = (f32[2048,512]{1,0:T(8,128)S(1)}, bf16[2048,512]{1,0:T(8,128)(2,1)S(1)}, bf16[2048,512]{1,0:T(8,128)(2,1)S(1)}) custom-call(f32[2048,1024]{1,0:T(8,128)} %a_hbm.1, f32[128,512]{1,0:T(8,128)S(1)} %copy-done, f32[128,512]{1,0:T(8,128)S(1)} %collective-permute-done.b1, f32[128,512]{1,0:T(8,128)S(1)} %collective-permute-done.1.b2, ...), custom_call_target="tpu_custom_call" | custom-call | flops 3221225472 | bytes 16777216 | tf_op jit(solution)/shard_map/pallas_call | solution.py:66
  30.9 0.0 collective-permute-done.6.refs_6_
  30.9 0.0 collective-permute-done.5.refs_5_
  30.9 1.2 %collective-permute-done.4.refs_4_ = f32[128,512]{1,0:T(8,128)S(1)} collective-permute-done((f32[128,512]{1,0:T(8,128)S(1)}, f32[128,512]{1,0:T(8,128)S(1)}, u32[]{:S(2)}, u32[]{:S(2)}) %collective-permute-start.4) | collective-permute-done | bytes 262176 | tf_op jit(solution)/shard_map/ppermute | solution.py:176
  32.1 2.0 %shard_map.29 = f32[1024,512]{1,0:T(8,128)S(1)} custom-call(bf16[2048,512]{1,0:T(8,128)(2,1)S(1)} %get-tuple-element.16.refs_0_, bf16[2048,512]{1,0:T(8,128)(2,1)S(1)} %get-tuple-element.17.refs_1_, f32[2048,512]{1,0:T(8,128)S(1)} %get-tuple-element.18.refs_2_, f32[128,512]{1,0:T(8,128)S(1)} %collective-permute-done.3.refs_3_, ...), custom_call_target="tpu_custom_call" | custom-call | flops 1610612736 | bytes 10485760 | tf_op jit(solution)/shard_map/pallas_call | solution.py:103
  34.1 6.3 %collective-permute-start.7 = (f32[1024,512]{1,0:T(8,128)S(1)}, f32[1024,512]{1,0:T(8,128)S(1)}, u32[]{:S(2)}, u32[]{:S(2)}) collective-permute-start(f32[1024,512]{1,0:T(8,128)S(1)} %shard_map.29), channel_id=1, source_target_pairs={{0,4},{4,0},{8,12},{12,8},{16,20},{20,16},{24,28},{28,24},{32,36},... | collective-permute-start | bytes 6291464 | tf_op jit(solution)/shard_map/ppermute | solution.py:184
  40.5 2.0 %shard_map.30.second = f32[1024,512]{1,0:T(8,128)S(1)} custom-call(bf16[2048,512]{1,0:T(8,128)(2,1)S(1)} %get-tuple-element.16.refs_0_, bf16[2048,512]{1,0:T(8,128)(2,1)S(1)} %get-tuple-element.17.refs_1_, f32[2048,512]{1,0:T(8,128)S(1)} %get-tuple-element.18.refs_2_, f32[128,512]{1,0:T(8,128)S(1)} %collective-permute-done.3.refs_3_, ...), custom_call_target="tpu_custom_call" | custom-call | flops 1610612736 | bytes 10485760 | tf_op jit(solution)/shard_map/pallas_call | solution.py:103
  42.5 1.8 %collective-permute-done.7.first = f32[1024,512]{1,0:T(8,128)S(1)} collective-permute-done((f32[1024,512]{1,0:T(8,128)S(1)}, f32[1024,512]{1,0:T(8,128)S(1)}, u32[]{:S(2)}, u32[]{:S(2)}) %collective-permute-start.7) | collective-permute-done | bytes 2097184 | tf_op jit(solution)/shard_map/ppermute | solution.py:184
  44.2 0.2 shard_map.31
  44.4 3.4 %collective-permute-start.10 = (f32[256,512]{1,0:T(8,128)S(1)}, f32[256,512]{1,0:T(8,128)S(1)}, u32[]{:S(2)}, u32[]{:S(2)}) collective-permute-start(f32[256,512]{1,0:T(8,128)S(1)} %get-tuple-element.23), channel_id=1, source_target_pairs={{0,8},{4,60},{8,16},{12,4},{16,24},{20,12},{24,32},{28,20},{32,40}... | collective-permute-start | bytes 1572872 | tf_op jit(solution)/shard_map/ppermute | solution.py:185
  47.9 3.8 %collective-permute-start.11 = (f32[128,512]{1,0:T(8,128)S(1)}, f32[128,512]{1,0:T(8,128)S(1)}, u32[]{:S(2)}, u32[]{:S(2)}) collective-permute-start(f32[128,512]{1,0:T(8,128)S(1)} %get-tuple-element.24), channel_id=1, source_target_pairs={{0,16},{4,52},{8,24},{12,60},{16,32},{20,4},{24,40},{28,12},{32,48... | collective-permute-start | bytes 786440 | tf_op jit(solution)/shard_map/ppermute | solution.py:186
  51.7 3.0 %collective-permute-start.8 = (f32[128,512]{1,0:T(8,128)S(1)}, f32[128,512]{1,0:T(8,128)S(1)}, u32[]{:S(2)}, u32[]{:S(2)}) collective-permute-start(f32[128,512]{1,0:T(8,128)S(1)} %get-tuple-element.20), channel_id=1, source_target_pairs={{0,8},{4,60},{8,16},{12,4},{16,24},{20,12},{24,32},{28,20},{32,40}... | collective-permute-start | bytes 786440 | tf_op jit(solution)/shard_map/ppermute | solution.py:187
  54.6 3.2 %collective-permute-start.9 = (f32[128,512]{1,0:T(8,128)S(1)}, f32[128,512]{1,0:T(8,128)S(1)}, u32[]{:S(2)}, u32[]{:S(2)}) collective-permute-start(f32[128,512]{1,0:T(8,128)S(1)} %get-tuple-element.21), channel_id=1, source_target_pairs={{0,12},{4,56},{8,20},{12,0},{16,28},{20,8},{24,36},{28,16},{32,44}... | collective-permute-start | bytes 786440 | tf_op jit(solution)/shard_map/ppermute | solution.py:188
  57.8 1.9 %collective-permute-done.11.got_four = f32[128,512]{1,0:T(8,128)S(1)} collective-permute-done((f32[128,512]{1,0:T(8,128)S(1)}, f32[128,512]{1,0:T(8,128)S(1)}, u32[]{:S(2)}, u32[]{:S(2)}) %collective-permute-start.11) | collective-permute-done | bytes 262176 | tf_op jit(solution)/shard_map/ppermute | solution.py:186
  59.7 0.0 collective-permute-done.10.got_three
  59.7 0.1 shard_map.32
  59.8 5.9 %collective-permute-start.12 = (f32[128,512]{1,0:T(8,128)S(1)}, f32[128,512]{1,0:T(8,128)S(1)}, u32[]{:S(2)}, u32[]{:S(2)}) collective-permute-start(f32[128,512]{1,0:T(8,128)S(1)} %get-tuple-element.25), channel_id=1, source_target_pairs={{0,16},{4,52},{8,24},{12,60},{16,32},{20,4},{24,40},{28,12},{32,48... | collective-permute-start | bytes 786440 | tf_op jit(solution)/shard_map/ppermute | solution.py:191
  65.7 2.7 %collective-permute-start.13 = (f32[128,512]{1,0:T(8,128)S(1)}, f32[128,512]{1,0:T(8,128)S(1)}, u32[]{:S(2)}, u32[]{:S(2)}) collective-permute-start(f32[128,512]{1,0:T(8,128)S(1)} %get-tuple-element.26), channel_id=1, source_target_pairs={{0,20},{4,48},{8,28},{12,56},{16,36},{20,0},{24,44},{28,8},{32,52}... | collective-permute-start | bytes 786440 | tf_op jit(solution)/shard_map/ppermute | solution.py:192
  68.5 0.0 collective-permute-done.8
  68.5 0.0 collective-permute-done.9
  68.5 4.6 %collective-permute-done.12 = f32[128,512]{1,0:T(8,128)S(1)} collective-permute-done((f32[128,512]{1,0:T(8,128)S(1)}, f32[128,512]{1,0:T(8,128)S(1)}, u32[]{:S(2)}, u32[]{:S(2)}) %collective-permute-start.12) | collective-permute-done | bytes 262176 | tf_op jit(solution)/shard_map/ppermute | solution.py:191
  73.1 7.9 %collective-permute-done.13 = f32[128,512]{1,0:T(8,128)S(1)} collective-permute-done((f32[128,512]{1,0:T(8,128)S(1)}, f32[128,512]{1,0:T(8,128)S(1)}, u32[]{:S(2)}, u32[]{:S(2)}) %collective-permute-start.13) | collective-permute-done | bytes 262176 | tf_op jit(solution)/shard_map/ppermute | solution.py:192
  81.0 0.8 %add_add_fusion = f32[128,512]{1,0:T(8,128)} fusion(f32[128,512]{1,0:T(8,128)S(1)} %collective-permute-done.13, f32[128,512]{1,0:T(8,128)S(1)} %collective-permute-done.12, f32[128,512]{1,0:T(8,128)S(1)} %collective-permute-done.9, f32[128,512]{1,0:T(8,128)S(1)} %get-tuple-element.19, f32[128,512]{1,0:T(8,128)S(1)} %collective-permute-done.8), kind=kLoop, calls=%fused_computation | loop fusion | flops 262144 | bytes 1572864 | tf_op jit(solution)/shard_map/add | solution.py:193
Async XLA Ops:
  0.0 14.8 %collective-permute-start.3 = (f32[128,512]{1,0:T(8,128)}, f32[128,512]{1,0:T(8,128)S(1)}, u32[]{:S(2)}, u32[]{:S(2)}) collective-permute-start(f32[128,512]{1,0:T(8,128)} %b0_hbm.1), channel_id=1, source_target_pairs={{0,64},{64,0},{128,192},{192,128},{256,320},{320,256},{384,448},{4... | collective-permute-start | bytes 786440 | tf_op jit(solution)/shard_map/ppermute | solution.py:178
  4.8 16.5 %collective-permute-start.2 = (f32[128,512]{1,0:T(8,128)}, f32[128,512]{1,0:T(8,128)S(1)}, u32[]{:S(2)}, u32[]{:S(2)}) collective-permute-start(f32[128,512]{1,0:T(8,128)} %b0_hbm.1), channel_id=1, source_target_pairs={{0,128},{4,132},{8,136},{12,140},{16,144},{20,148},{24,152},{28,15... | collective-permute-start | bytes 786440 | tf_op jit(solution)/shard_map/ppermute | solution.py:176
  8.0 15.5 %collective-permute-start.1 = (f32[128,512]{1,0:T(8,128)}, f32[128,512]{1,0:T(8,128)S(1)}, u32[]{:S(2)}, u32[]{:S(2)}) collective-permute-start(f32[128,512]{1,0:T(8,128)} %b0_hbm.1), channel_id=1, source_target_pairs={{0,384},{4,388},{8,392},{12,396},{16,400},{20,404},{24,408},{28,41... | collective-permute-start | bytes 786440 | tf_op jit(solution)/shard_map/ppermute | solution.py:176
  11.3 12.1 %collective-permute-start = (f32[128,512]{1,0:T(8,128)}, f32[128,512]{1,0:T(8,128)S(1)}, u32[]{:S(2)}, u32[]{:S(2)}) collective-permute-start(f32[128,512]{1,0:T(8,128)} %b0_hbm.1), channel_id=1, source_target_pairs={{0,256},{4,260},{8,264},{12,268},{16,272},{20,276},{24,280},{28,28... | collective-permute-start | bytes 786440 | tf_op jit(solution)/shard_map/ppermute | solution.py:176
  14.8 16.1 %collective-permute-start.6 = (f32[128,512]{1,0:T(8,128)S(1)}, f32[128,512]{1,0:T(8,128)S(1)}, u32[]{:S(2)}, u32[]{:S(2)}) collective-permute-start(f32[128,512]{1,0:T(8,128)S(1)} %collective-permute-done.3.refs_3_), channel_id=1, source_target_pairs={{0,128},{4,132},{8,136},{12,140},{16,144},{20,148},{24,152},{28,15... | collective-permute-start | bytes 786440 | tf_op jit(solution)/shard_map/ppermute | solution.py:176
  17.0 13.9 %collective-permute-start.5 = (f32[128,512]{1,0:T(8,128)S(1)}, f32[128,512]{1,0:T(8,128)S(1)}, u32[]{:S(2)}, u32[]{:S(2)}) collective-permute-start(f32[128,512]{1,0:T(8,128)S(1)} %collective-permute-done.3.refs_3_), channel_id=1, source_target_pairs={{0,384},{4,388},{8,392},{12,396},{16,400},{20,404},{24,408},{28,41... | collective-permute-start | bytes 786440 | tf_op jit(solution)/shard_map/ppermute | solution.py:176
  21.3 10.8 %collective-permute-start.4 = (f32[128,512]{1,0:T(8,128)S(1)}, f32[128,512]{1,0:T(8,128)S(1)}, u32[]{:S(2)}, u32[]{:S(2)}) collective-permute-start(f32[128,512]{1,0:T(8,128)S(1)} %collective-permute-done.3.refs_3_), channel_id=1, source_target_pairs={{0,256},{4,260},{8,264},{12,268},{16,272},{20,276},{24,280},{28,28... | collective-permute-start | bytes 786440 | tf_op jit(solution)/shard_map/ppermute | solution.py:176
  23.5 1.0 %copy-start = (f32[128,512]{1,0:T(8,128)S(1)}, f32[128,512]{1,0:T(8,128)}, u32[]{:S(2)}) copy-start(f32[128,512]{1,0:T(8,128)} %b0_hbm.1) | copy-start | bytes 786436
  34.1 10.1 %collective-permute-start.7 = (f32[1024,512]{1,0:T(8,128)S(1)}, f32[1024,512]{1,0:T(8,128)S(1)}, u32[]{:S(2)}, u32[]{:S(2)}) collective-permute-start(f32[1024,512]{1,0:T(8,128)S(1)} %shard_map.29), channel_id=1, source_target_pairs={{0,4},{4,0},{8,12},{12,8},{16,20},{20,16},{24,28},{28,24},{32,36},... | collective-permute-start | bytes 6291464 | tf_op jit(solution)/shard_map/ppermute | solution.py:184
  44.4 15.3 %collective-permute-start.10 = (f32[256,512]{1,0:T(8,128)S(1)}, f32[256,512]{1,0:T(8,128)S(1)}, u32[]{:S(2)}, u32[]{:S(2)}) collective-permute-start(f32[256,512]{1,0:T(8,128)S(1)} %get-tuple-element.23), channel_id=1, source_target_pairs={{0,8},{4,60},{8,16},{12,4},{16,24},{20,12},{24,32},{28,20},{32,40}... | collective-permute-start | bytes 1572872 | tf_op jit(solution)/shard_map/ppermute | solution.py:185
  47.9 11.8 %collective-permute-start.11 = (f32[128,512]{1,0:T(8,128)S(1)}, f32[128,512]{1,0:T(8,128)S(1)}, u32[]{:S(2)}, u32[]{:S(2)}) collective-permute-start(f32[128,512]{1,0:T(8,128)S(1)} %get-tuple-element.24), channel_id=1, source_target_pairs={{0,16},{4,52},{8,24},{12,60},{16,32},{20,4},{24,40},{28,12},{32,48... | collective-permute-start | bytes 786440 | tf_op jit(solution)/shard_map/ppermute | solution.py:186
  51.7 16.8 %collective-permute-start.8 = (f32[128,512]{1,0:T(8,128)S(1)}, f32[128,512]{1,0:T(8,128)S(1)}, u32[]{:S(2)}, u32[]{:S(2)}) collective-permute-start(f32[128,512]{1,0:T(8,128)S(1)} %get-tuple-element.20), channel_id=1, source_target_pairs={{0,8},{4,60},{8,16},{12,4},{16,24},{20,12},{24,32},{28,20},{32,40}... | collective-permute-start | bytes 786440 | tf_op jit(solution)/shard_map/ppermute | solution.py:187
  54.6 13.8 %collective-permute-start.9 = (f32[128,512]{1,0:T(8,128)S(1)}, f32[128,512]{1,0:T(8,128)S(1)}, u32[]{:S(2)}, u32[]{:S(2)}) collective-permute-start(f32[128,512]{1,0:T(8,128)S(1)} %get-tuple-element.21), channel_id=1, source_target_pairs={{0,12},{4,56},{8,20},{12,0},{16,28},{20,8},{24,36},{28,16},{32,44}... | collective-permute-start | bytes 786440 | tf_op jit(solution)/shard_map/ppermute | solution.py:188
  59.8 13.3 %collective-permute-start.12 = (f32[128,512]{1,0:T(8,128)S(1)}, f32[128,512]{1,0:T(8,128)S(1)}, u32[]{:S(2)}, u32[]{:S(2)}) collective-permute-start(f32[128,512]{1,0:T(8,128)S(1)} %get-tuple-element.25), channel_id=1, source_target_pairs={{0,16},{4,52},{8,24},{12,60},{16,32},{20,4},{24,40},{28,12},{32,48... | collective-permute-start | bytes 786440 | tf_op jit(solution)/shard_map/ppermute | solution.py:191
  65.7 15.3 %collective-permute-start.13 = (f32[128,512]{1,0:T(8,128)S(1)}, f32[128,512]{1,0:T(8,128)S(1)}, u32[]{:S(2)}, u32[]{:S(2)}) collective-permute-start(f32[128,512]{1,0:T(8,128)S(1)} %get-tuple-element.26), channel_id=1, source_target_pairs={{0,20},{4,48},{8,28},{12,56},{16,36},{20,0},{24,44},{28,8},{32,52}... | collective-permute-start | bytes 786440 | tf_op jit(solution)/shard_map/ppermute | solution.py:192

commit v4 on v3

v4 whole, which is shorter than its diff:
```python
import jax
import jax.numpy as jnp
from jax import lax
from jax.experimental import pallas as pl
from jax.experimental.pallas import tpu as pltpu
from jax.sharding import PartitionSpec as P

F32, BF16 = jnp.float32, jnp.bfloat16
VMEM = pl.BlockSpec(memory_space=pltpu.VMEM)
MIB = 1024 * 1024


def two_parts(value):
    high = value.astype(BF16)
    return high, (value - high.astype(F32)).astype(BF16)


def place():
    ka, ma = lax.axis_index("ka"), lax.axis_index("ma")
    return ka // 2, ka % 2, ma % 2, ma // 2


def dot(a, b):
    return jnp.dot(a, b, preferred_element_type=F32)


def place_parts(pieces, high, low):
    _, _, _, own_x = place()
    for offset, piece in zip(OFFSETS, pieces):
        rows = pl.ds(pl.multiple_of(((own_x + offset) % 4) * 128, 128), 128)
        high[rows, :], low[rows, :] = two_parts(piece[...])


def row_copies(a_hbm, a_ref, sems, mine):
    y, core, _, _ = place()
    side = core if mine else 1 - core
    copies, at = [], 0
    for index, shift in enumerate(SHIFTS):
        if shift in (0, 4):
            start, count = ((y + shift) % 8) * 256 + side * 128, 128
        else:
            start, count = ((y + jnp.where(side == 0, shift, 8 - shift)) % 8) * 256, 256
        rows = pl.ds(pl.multiple_of(start, 128), count)
        copies.append(pltpu.make_async_copy(a_hbm.at[rows], a_ref.at[pl.ds(at, count)], sems.at[index]))
        at += count
    return copies


def parts_of(a_ref, rows, z):
    return two_parts(jnp.concatenate([a_ref[rows, 256 * x + 128 * z : 256 * x + 128 * z + 128] for x in range(4)], axis=1))


def three_dots(high, low, b_high, b_low):
    return dot(high, b_low[...]) + dot(low, b_high[...]) + dot(high, b_high[...])


def for_each_tile(body, copies=None):
    _, _, half, _ = place()
    for z in range(2):

        @pl.when(half == z)
        def _(z=z):
            for step, needed in enumerate(((0,), (1,), (2,), (3, 4))):
                for index in needed if copies else ():
                    copies[index].wait()
                body(z, slice(256 * step, 256 * step + 256))


def early_kernel(a_hbm, b0, b1, b2, b3, sums, high_out, low_out, b_high, b_low, a_kept, a_ref, sems, kept_sems):
    copies, kept_copies = row_copies(a_hbm, a_ref, sems, False), row_copies(a_hbm, a_kept, kept_sems, True)
    for copy in copies + kept_copies:
        copy.start()
    place_parts((b0, b1, b2, b3), b_high, b_low)

    def body(z, rows):
        sums[rows, :] = three_dots(*parts_of(a_ref, rows, z), b_high, b_low)
        high_out[rows, :], low_out[rows, :] = parts_of(a_ref, rows, 1 - z)

    for_each_tile(body, copies)
    for copy in kept_copies:
        copy.wait()


def late_kernel(sums, a_high, a_low, b0, b1, b2, b3, out, b_high, b_low):
    place_parts((b0, b1, b2, b3), b_high, b_low)
    for step in range(4):
        rows = slice(256 * step, 256 * step + 256)
        out[rows, :] = sums[rows, :] + three_dots(a_high[rows, :], a_low[rows, :], b_high, b_low)


def whole_kernel(a_ref, near_high, near_low, far_high, far_low, out):
    def body(z, rows):
        near = three_dots(*parts_of(a_ref, rows, z), near_high, near_low)
        out[rows, :] = near + three_dots(*parts_of(a_ref, rows, 1 - z), far_high, far_low)

    for_each_tile(body)


def product(kernel, outs, reads_a, limit, *args):
    return pl.pallas_call(
        kernel,
        in_specs=[pl.BlockSpec(memory_space=pl.ANY) if reads_a else VMEM] + [VMEM] * (len(args) - 1),
        out_specs=[VMEM] * len(outs),
        out_shape=[jax.ShapeDtypeStruct(shape, kind) for shape, kind in outs],
        scratch_shapes=[pltpu.VMEM((1024, 1024), F32)] + [pltpu.SemaphoreType.DMA((5,))] * 2 if reads_a else [],
        compiler_params=pltpu.CompilerParams(vmem_limit_bytes=limit * MIB),
        cost_estimate=pl.CostEstimate(flops=2 * 3 * 1024 * 512 * 512, bytes_accessed=8 * MIB, transcendentals=0),
    )(*args)


def add_kernel(first, second, three, four, one_own, one_other, two, zero):
    _, core, _, _ = place()
    own, other = (pl.multiple_of(256 + side * 128, 128) for side in (core, 1 - core))
    for start, out in ((0, three), (own, one_own), (other, one_other), (512, two), (768, four), (896, zero)):
        rows = pl.ds(start, out.shape[0])
        out[...] = first[rows, :] + second[rows, :]


def add(first, second):
    counts = (256, 128, 128, 128, 256, 128)
    return pl.pallas_call(
        add_kernel,
        in_specs=[VMEM] * 2,
        out_specs=[VMEM] * len(counts),
        out_shape=[jax.ShapeDtypeStruct((count, 512), F32) for count in counts],
        compiler_params=pltpu.CompilerParams(vmem_limit_bytes=8 * MIB),
        cost_estimate=pl.CostEstimate(flops=MIB, bytes_accessed=4 * MIB, transcendentals=0),
    )(first, second)


def pass_on_kernel(two, got_three, got_four, own, other):
    _, core, _, _ = place()
    for index, out in ((core, own), (1 - core, other)):
        rows = pl.ds(pl.multiple_of(index * 128, 128), 128)
        total = two[rows, :] + got_three[rows, :]
        out[...] = total + got_four[...] if out is own else total


def halves(kernel, *args):
    return pl.pallas_call(
        kernel,
        in_specs=[VMEM] * len(args),
        out_specs=[VMEM] * 2,
        out_shape=[jax.ShapeDtypeStruct((128, 512), F32)] * 2,
        compiler_params=pltpu.CompilerParams(vmem_limit_bytes=4 * MIB),
        cost_estimate=pl.CostEstimate(flops=MIB, bytes_accessed=2 * MIB, transcendentals=0),
    )(*args)


def along_y(distance, cross=0):
    return [(i, ((i + (2 * distance if i % 2 == 0 else -2 * distance)) % 16) ^ cross) for i in range(16)]


CORES = [(i, i ^ 1) for i in range(16)]
HALVES = [(i, i ^ 1) for i in range(8)]


SHIFTS = (3, 1, 2, 4, 0)
OFFSETS = (0, 2, 1, -1)


def by_x(offset):
    pairs = []
    for ma in range(8):
        for ka in range(16):
            step = 2 if offset == 2 and ka % 2 == 0 else -offset
            pairs.append((ma * 16 + ka, ((ma + 2 * step) % 8) * 16 + ka))
    return pairs


def shards(left_matrix, right_panel):
    def other_half(b):
        return lax.ppermute(b, "ma", HALVES)

    def from_row(b, offsets):
        return [lax.ppermute(b, ("ma", "ka"), by_x(offset)) for offset in offsets]

    near_b = [right_panel] + from_row(right_panel, OFFSETS[1:])
    swapped = other_half(right_panel)
    far_b = [swapped, other_half(near_b[1])] + from_row(swapped, OFFSETS[2:])
    sums, parts, b_parts = ((1024, 512), F32), [((1024, 512), BF16)] * 2, [((512, 512), BF16)] * 2
    outs = [sums] + parts + b_parts + [((1024, 1024), F32)]
    first, a_high, a_low, near_high, near_low, a_kept = product(early_kernel, outs, True, 40, left_matrix, *near_b)
    given, far_high, far_low = product(late_kernel, [sums] + b_parts, False, 14, first, a_high, a_low, *far_b)
    kept = product(whole_kernel, [sums], False, 14, a_kept, near_high, near_low, far_high, far_low)[0]

    three, four, one_own, one_other, two, zero = add(lax.ppermute(given, "ka", CORES), kept)
    got_three = lax.ppermute(three, "ka", along_y(1))
    got_four = lax.ppermute(four, "ka", along_y(2))
    near_own = lax.ppermute(one_own, "ka", along_y(1))
    near_other = lax.ppermute(one_other, "ka", along_y(1, 1))

    own, other = halves(pass_on_kernel, two, got_three, got_four)
    far_own = lax.ppermute(own, "ka", along_y(2))
    far_other = lax.ppermute(other, "ka", along_y(2, 1))
    return zero + near_own + near_other + far_own + far_other


def solution(mesh):
    in_specs = (P("ma", "ka"), P(("ka", "ma"), "an"))
    out_specs = P(("ma", "ka"), "an")
    return jax.shard_map(shards, mesh=mesh, in_specs=in_specs, out_specs=out_specs, check_vma=False)
```

time: 82.9 us -> 78.6 us (0.948)
  the two profiles are of different devices: /device:TPU:1 before, /device:TPU:129 now
where the time goes in v4:
time: 78.6 us; the launch traced here: 78.1 us
  starting transfers between devices  51.5 us (66%)
  waiting for transfers between devices  14.8 us (19%)
  Pallas kernels  9.82 us (12%)
  local copies, waits for them, and re-layouts  0.94 us (1%)
  other arithmetic  0.83 us (1%)
    ppermute x5, starting transfers between devices, from_row(): return [lax.ppermute(b, ('ma', 'ka'), by_x(offset)) for offset in offsets]  17.6 us
    pallas_call x3, Pallas kernels, product(): pl.pallas_call(kernel, in_specs=[pl.BlockSpec(memory_space=pl.ANY) if rea...  9.54 us
    ppermute x1, waiting for transfers between devices, shards(): far_other = lax.ppermute(other, 'ka', along_y(2, 1))  8 us
    ppermute x1, starting transfers between devices, shards(): far_own = lax.ppermute(own, 'ka', along_y(2))  5.93 us
    ppermute x2, starting transfers between devices, other_half(): return lax.ppermute(b, 'ma', HALVES)  5.92 us
    ppermute x1, starting transfers between devices, shards(): got_three = lax.ppermute(three, 'ka', along_y(1))  5.12 us
    ppermute x1, waiting for transfers between devices, shards(): far_own = lax.ppermute(own, 'ka', along_y(2))  4.54 us
    ppermute x1, starting transfers between devices, shards(): lax.ppermute(given, 'ka', CORES)  4.27 us
  transfers between devices with their start and end apart: 14, of which 4 were waited for; matrix products, arithmetic and copies ran while one was open for 0% of the time, Pallas kernels for 10%

profile of v4, /device:TPU:129, one launch (start us, length us, event | category | flops | bytes accessed | tf_op | source)
XLA Modules:
  0.0 78.1 jit_solution(13029047039170854441)
XLA Ops:
  0.0 4.6 %collective-permute-start = (f32[128,512]{1,0:T(8,128)}, f32[128,512]{1,0:T(8,128)S(1)}, u32[]{:S(2)}, u32[]{:S(2)}) collective-permute-start(f32[128,512]{1,0:T(8,128)} %b0.1), channel_id=1, source_target_pairs={{0,256},{4,260},{8,264},{12,268},{16,272},{20,276},{24,280},{28,28... | collective-permute-start | bytes 786440 | tf_op jit(solution)/shard_map/ppermute | solution.py:176
  4.6 4.0 %collective-permute-start.3 = (f32[128,512]{1,0:T(8,128)}, f32[128,512]{1,0:T(8,128)S(1)}, u32[]{:S(2)}, u32[]{:S(2)}) collective-permute-start(f32[128,512]{1,0:T(8,128)} %b0.1), channel_id=1, source_target_pairs={{0,64},{64,0},{128,192},{192,128},{256,320},{320,256},{384,448},{4... | collective-permute-start | bytes 786440 | tf_op jit(solution)/shard_map/ppermute | solution.py:173
  8.7 2.2 %collective-permute-start.2 = (f32[128,512]{1,0:T(8,128)}, f32[128,512]{1,0:T(8,128)S(1)}, u32[]{:S(2)}, u32[]{:S(2)}) collective-permute-start(f32[128,512]{1,0:T(8,128)} %b0.1), channel_id=1, source_target_pairs={{0,128},{4,132},{8,136},{12,140},{16,144},{20,148},{24,152},{28,15... | collective-permute-start | bytes 786440 | tf_op jit(solution)/shard_map/ppermute | solution.py:176
  10.9 4.3 %collective-permute-start.1 = (f32[128,512]{1,0:T(8,128)}, f32[128,512]{1,0:T(8,128)S(1)}, u32[]{:S(2)}, u32[]{:S(2)}) collective-permute-start(f32[128,512]{1,0:T(8,128)} %b0.1), channel_id=1, source_target_pairs={{0,384},{4,388},{8,392},{12,396},{16,400},{20,404},{24,408},{28,41... | collective-permute-start | bytes 786440 | tf_op jit(solution)/shard_map/ppermute | solution.py:176
  15.2 0.0 collective-permute-done.b1
  15.2 1.9 %collective-permute-start.4 = (f32[128,512]{1,0:T(8,128)S(1)}, f32[128,512]{1,0:T(8,128)S(1)}, u32[]{:S(2)}, u32[]{:S(2)}) collective-permute-start(f32[128,512]{1,0:T(8,128)S(1)} %collective-permute-done.b1), channel_id=1, source_target_pairs={{0,64},{64,0},{128,192},{192,128},{256,320},{320,256},{384,448},{4... | collective-permute-start | bytes 786440 | tf_op jit(solution)/shard_map/ppermute | solution.py:173
  17.1 0.0 collective-permute-done.3.b0
  17.1 1.9 %collective-permute-start.6 = (f32[128,512]{1,0:T(8,128)S(1)}, f32[128,512]{1,0:T(8,128)S(1)}, u32[]{:S(2)}, u32[]{:S(2)}) collective-permute-start(f32[128,512]{1,0:T(8,128)S(1)} %collective-permute-done.3.b0), channel_id=1, source_target_pairs={{0,128},{4,132},{8,136},{12,140},{16,144},{20,148},{24,152},{28,15... | collective-permute-start | bytes 786440 | tf_op jit(solution)/shard_map/ppermute | solution.py:176
  19.0 4.6 %collective-permute-start.5 = (f32[128,512]{1,0:T(8,128)S(1)}, f32[128,512]{1,0:T(8,128)S(1)}, u32[]{:S(2)}, u32[]{:S(2)}) collective-permute-start(f32[128,512]{1,0:T(8,128)S(1)} %collective-permute-done.3.b0), channel_id=1, source_target_pairs={{0,384},{4,388},{8,392},{12,396},{16,400},{20,404},{24,408},{28,41... | collective-permute-start | bytes 786440 | tf_op jit(solution)/shard_map/ppermute | solution.py:176
  23.6 0.0 collective-permute-done.2.b3
  23.6 0.0 collective-permute-done.1.b2
  23.6 0.0 copy-start
  23.7 0.9 %copy-done = f32[128,512]{1,0:T(8,128)S(1)} copy-done((f32[128,512]{1,0:T(8,128)S(1)}, f32[128,512]{1,0:T(8,128)}, u32[]{:S(2)}) %copy-start) | copy-done | bytes 262168
  24.6 4.1 %shard_map.28 = (f32[1024,512]{1,0:T(8,128)S(1)}, bf16[1024,512]{1,0:T(8,128)(2,1)S(1)}, bf16[1024,512]{1,0:T(8,128)(2,1)S(1)}, bf16[512,512]{1,0:T(8,128)(2,1)S...) custom-call(f32[2048,1024]{1,0:T(8,128)} %a_hbm.1, f32[128,512]{1,0:T(8,128)S(1)} %copy-done, ...), custom_call_target="tpu_custom_call" | custom-call | flops 1610612736 | bytes 8388608 | tf_op jit(solution)/shard_map/pallas_call | solution.py:100
  28.7 0.0 collective-permute-done.4.b1
  28.7 0.0 collective-permute-done.6.b3
  28.7 0.0 collective-permute-done.5.b2
  28.7 2.0 %shard_map.29 = (f32[1024,512]{1,0:T(8,128)S(1)}, bf16[512,512]{1,0:T(8,128)(2,1)S(1)}, bf16[512,512]{1,0:T(8,128)(2,1)S(1)}) custom-call(f32[1024,512]{1,0:T(8,128)S(1)} %get-tuple-element.22.sums, bf16[1024,512]{1,0:T(8,128)(2,1)S(1)} %get-tuple-element.23.a_high, bf16[1024,512]{1,0:T(8,128)(2,1)S(1)} %get-tuple-element.24.a_low, ...), custom_call_target="tpu_custom_call" | custom-call | flops 1610612736 | bytes 8388608 | tf_op jit(solution)/shard_map/pallas_call | solution.py:100
  30.8 4.3 %collective-permute-start.7 = (f32[1024,512]{1,0:T(8,128)S(1)}, f32[1024,512]{1,0:T(8,128)S(1)}, u32[]{:S(2)}, u32[]{:S(2)}) collective-permute-start(f32[1024,512]{1,0:T(8,128)S(1)} %get-tuple-element.25), channel_id=1, source_target_pairs={{0,4},{4,0},{8,12},{12,8},{16,20},{20,16},{24,28},{28,24},{32,36},... | collective-permute-start | bytes 6291464 | tf_op jit(solution)/shard_map/ppermute | solution.py:187
  35.0 3.4 %shard_map.30.second = f32[1024,512]{1,0:T(8,128)S(1)} custom-call(f32[1024,1024]{1,0:T(8,128)S(1)} %get-tuple-element.26.a_ref, bf16[512,512]{1,0:T(8,128)(2,1)S(1)} %get-tuple-element.27.near_high, bf16[512,512]{1,0:T(8,128)(2,1)S(1)} %get-tuple-element.28.near_low, bf16[512,512]{1,0:T(8,128)(2,1)S(1)} %get-tuple-element.29.far_high, ...), custom_call_target="tpu_custom_call" | custom-call | flops 1610612736 | bytes 8388608 | tf_op jit(solution)/shard_map/pallas_call | solution.py:100
  38.5 0.3 collective-permute-done.7.first
  38.8 0.2 shard_map.31
  39.0 5.1 %collective-permute-start.10 = (f32[256,512]{1,0:T(8,128)S(1)}, f32[256,512]{1,0:T(8,128)S(1)}, u32[]{:S(2)}, u32[]{:S(2)}) collective-permute-start(f32[256,512]{1,0:T(8,128)S(1)} %get-tuple-element.35), channel_id=1, source_target_pairs={{0,8},{4,60},{8,16},{12,4},{16,24},{20,12},{24,32},{28,20},{32,40}... | collective-permute-start | bytes 1572872 | tf_op jit(solution)/shard_map/ppermute | solution.py:188
  44.1 3.7 %collective-permute-start.11 = (f32[128,512]{1,0:T(8,128)S(1)}, f32[128,512]{1,0:T(8,128)S(1)}, u32[]{:S(2)}, u32[]{:S(2)}) collective-permute-start(f32[128,512]{1,0:T(8,128)S(1)} %get-tuple-element.36), channel_id=1, source_target_pairs={{0,16},{4,52},{8,24},{12,60},{16,32},{20,4},{24,40},{28,12},{32,48... | collective-permute-start | bytes 786440 | tf_op jit(solution)/shard_map/ppermute | solution.py:189
  47.9 3.0 %collective-permute-start.8 = (f32[128,512]{1,0:T(8,128)S(1)}, f32[128,512]{1,0:T(8,128)S(1)}, u32[]{:S(2)}, u32[]{:S(2)}) collective-permute-start(f32[128,512]{1,0:T(8,128)S(1)} %get-tuple-element.32), channel_id=1, source_target_pairs={{0,8},{4,60},{8,16},{12,4},{16,24},{20,12},{24,32},{28,20},{32,40}... | collective-permute-start | bytes 786440 | tf_op jit(solution)/shard_map/ppermute | solution.py:190
  50.9 3.2 %collective-permute-start.9 = (f32[128,512]{1,0:T(8,128)S(1)}, f32[128,512]{1,0:T(8,128)S(1)}, u32[]{:S(2)}, u32[]{:S(2)}) collective-permute-start(f32[128,512]{1,0:T(8,128)S(1)} %get-tuple-element.33), channel_id=1, source_target_pairs={{0,12},{4,56},{8,20},{12,0},{16,28},{20,8},{24,36},{28,16},{32,44}... | collective-permute-start | bytes 786440 | tf_op jit(solution)/shard_map/ppermute | solution.py:191
  54.1 1.9 %collective-permute-done.11.got_four = f32[128,512]{1,0:T(8,128)S(1)} collective-permute-done((f32[128,512]{1,0:T(8,128)S(1)}, f32[128,512]{1,0:T(8,128)S(1)}, u32[]{:S(2)}, u32[]{:S(2)}) %collective-permute-start.11) | collective-permute-done | bytes 262176 | tf_op jit(solution)/shard_map/ppermute | solution.py:189
  56.0 0.0 collective-permute-done.10.got_three
  56.0 0.1 shard_map.32
  56.0 5.9 %collective-permute-start.12 = (f32[128,512]{1,0:T(8,128)S(1)}, f32[128,512]{1,0:T(8,128)S(1)}, u32[]{:S(2)}, u32[]{:S(2)}) collective-permute-start(f32[128,512]{1,0:T(8,128)S(1)} %get-tuple-element.37), channel_id=1, source_target_pairs={{0,16},{4,52},{8,24},{12,60},{16,32},{20,4},{24,40},{28,12},{32,48... | collective-permute-start | bytes 786440 | tf_op jit(solution)/shard_map/ppermute | solution.py:194
  62.0 2.8 %collective-permute-start.13 = (f32[128,512]{1,0:T(8,128)S(1)}, f32[128,512]{1,0:T(8,128)S(1)}, u32[]{:S(2)}, u32[]{:S(2)}) collective-permute-start(f32[128,512]{1,0:T(8,128)S(1)} %get-tuple-element.38), channel_id=1, source_target_pairs={{0,20},{4,48},{8,28},{12,56},{16,36},{20,0},{24,44},{28,8},{32,52}... | collective-permute-start | bytes 786440 | tf_op jit(solution)/shard_map/ppermute | solution.py:195
  64.7 0.0 collective-permute-done.8
  64.7 0.0 collective-permute-done.9
  64.7 4.5 %collective-permute-done.12 = f32[128,512]{1,0:T(8,128)S(1)} collective-permute-done((f32[128,512]{1,0:T(8,128)S(1)}, f32[128,512]{1,0:T(8,128)S(1)}, u32[]{:S(2)}, u32[]{:S(2)}) %collective-permute-start.12) | collective-permute-done | bytes 262176 | tf_op jit(solution)/shard_map/ppermute | solution.py:194
  69.3 8.0 %collective-permute-done.13 = f32[128,512]{1,0:T(8,128)S(1)} collective-permute-done((f32[128,512]{1,0:T(8,128)S(1)}, f32[128,512]{1,0:T(8,128)S(1)}, u32[]{:S(2)}, u32[]{:S(2)}) %collective-permute-start.13) | collective-permute-done | bytes 262176 | tf_op jit(solution)/shard_map/ppermute | solution.py:195
  77.3 0.8 %add_add_fusion = f32[128,512]{1,0:T(8,128)} fusion(f32[128,512]{1,0:T(8,128)S(1)} %collective-permute-done.13, f32[128,512]{1,0:T(8,128)S(1)} %collective-permute-done.12, f32[128,512]{1,0:T(8,128)S(1)} %collective-permute-done.9, f32[128,512]{1,0:T(8,128)S(1)} %get-tuple-element.31, f32[128,512]{1,0:T(8,128)S(1)} %collective-permute-done.8), kind=kLoop, calls=%fused_computation | loop fusion | flops 262144 | bytes 1572864 | tf_op jit(solution)/shard_map/add | solution.py:196
Async XLA Ops:
  0.0 15.2 %collective-permute-start = (f32[128,512]{1,0:T(8,128)}, f32[128,512]{1,0:T(8,128)S(1)}, u32[]{:S(2)}, u32[]{:S(2)}) collective-permute-start(f32[128,512]{1,0:T(8,128)} %b0.1), channel_id=1, source_target_pairs={{0,256},{4,260},{8,264},{12,268},{16,272},{20,276},{24,280},{28,28... | collective-permute-start | bytes 786440 | tf_op jit(solution)/shard_map/ppermute | solution.py:176
  4.6 12.5 %collective-permute-start.3 = (f32[128,512]{1,0:T(8,128)}, f32[128,512]{1,0:T(8,128)S(1)}, u32[]{:S(2)}, u32[]{:S(2)}) collective-permute-start(f32[128,512]{1,0:T(8,128)} %b0.1), channel_id=1, source_target_pairs={{0,64},{64,0},{128,192},{192,128},{256,320},{320,256},{384,448},{4... | collective-permute-start | bytes 786440 | tf_op jit(solution)/shard_map/ppermute | solution.py:173
  8.7 15.0 %collective-permute-start.2 = (f32[128,512]{1,0:T(8,128)}, f32[128,512]{1,0:T(8,128)S(1)}, u32[]{:S(2)}, u32[]{:S(2)}) collective-permute-start(f32[128,512]{1,0:T(8,128)} %b0.1), channel_id=1, source_target_pairs={{0,128},{4,132},{8,136},{12,140},{16,144},{20,148},{24,152},{28,15... | collective-permute-start | bytes 786440 | tf_op jit(solution)/shard_map/ppermute | solution.py:176
  10.9 12.8 %collective-permute-start.1 = (f32[128,512]{1,0:T(8,128)}, f32[128,512]{1,0:T(8,128)S(1)}, u32[]{:S(2)}, u32[]{:S(2)}) collective-permute-start(f32[128,512]{1,0:T(8,128)} %b0.1), channel_id=1, source_target_pairs={{0,384},{4,388},{8,392},{12,396},{16,400},{20,404},{24,408},{28,41... | collective-permute-start | bytes 786440 | tf_op jit(solution)/shard_map/ppermute | solution.py:176
  15.2 13.5 %collective-permute-start.4 = (f32[128,512]{1,0:T(8,128)S(1)}, f32[128,512]{1,0:T(8,128)S(1)}, u32[]{:S(2)}, u32[]{:S(2)}) collective-permute-start(f32[128,512]{1,0:T(8,128)S(1)} %collective-permute-done.b1), channel_id=1, source_target_pairs={{0,64},{64,0},{128,192},{192,128},{256,320},{320,256},{384,448},{4... | collective-permute-start | bytes 786440 | tf_op jit(solution)/shard_map/ppermute | solution.py:173
  17.1 11.6 %collective-permute-start.6 = (f32[128,512]{1,0:T(8,128)S(1)}, f32[128,512]{1,0:T(8,128)S(1)}, u32[]{:S(2)}, u32[]{:S(2)}) collective-permute-start(f32[128,512]{1,0:T(8,128)S(1)} %collective-permute-done.3.b0), channel_id=1, source_target_pairs={{0,128},{4,132},{8,136},{12,140},{16,144},{20,148},{24,152},{28,15... | collective-permute-start | bytes 786440 | tf_op jit(solution)/shard_map/ppermute | solution.py:176
  19.0 9.7 %collective-permute-start.5 = (f32[128,512]{1,0:T(8,128)S(1)}, f32[128,512]{1,0:T(8,128)S(1)}, u32[]{:S(2)}, u32[]{:S(2)}) collective-permute-start(f32[128,512]{1,0:T(8,128)S(1)} %collective-permute-done.3.b0), channel_id=1, source_target_pairs={{0,384},{4,388},{8,392},{12,396},{16,400},{20,404},{24,408},{28,41... | collective-permute-start | bytes 786440 | tf_op jit(solution)/shard_map/ppermute | solution.py:176
  23.6 1.0 %copy-start = (f32[128,512]{1,0:T(8,128)S(1)}, f32[128,512]{1,0:T(8,128)}, u32[]{:S(2)}) copy-start(f32[128,512]{1,0:T(8,128)} %b0.1) | copy-start | bytes 786436
  30.8 8.0 %collective-permute-start.7 = (f32[1024,512]{1,0:T(8,128)S(1)}, f32[1024,512]{1,0:T(8,128)S(1)}, u32[]{:S(2)}, u32[]{:S(2)}) collective-permute-start(f32[1024,512]{1,0:T(8,128)S(1)} %get-tuple-element.25), channel_id=1, source_target_pairs={{0,4},{4,0},{8,12},{12,8},{16,20},{20,16},{24,28},{28,24},{32,36},... | collective-permute-start | bytes 6291464 | tf_op jit(solution)/shard_map/ppermute | solution.py:187
  39.0 16.9 %collective-permute-start.10 = (f32[256,512]{1,0:T(8,128)S(1)}, f32[256,512]{1,0:T(8,128)S(1)}, u32[]{:S(2)}, u32[]{:S(2)}) collective-permute-start(f32[256,512]{1,0:T(8,128)S(1)} %get-tuple-element.35), channel_id=1, source_target_pairs={{0,8},{4,60},{8,16},{12,4},{16,24},{20,12},{24,32},{28,20},{32,40}... | collective-permute-start | bytes 1572872 | tf_op jit(solution)/shard_map/ppermute | solution.py:188
  44.1 11.8 %collective-permute-start.11 = (f32[128,512]{1,0:T(8,128)S(1)}, f32[128,512]{1,0:T(8,128)S(1)}, u32[]{:S(2)}, u32[]{:S(2)}) collective-permute-start(f32[128,512]{1,0:T(8,128)S(1)} %get-tuple-element.36), channel_id=1, source_target_pairs={{0,16},{4,52},{8,24},{12,60},{16,32},{20,4},{24,40},{28,12},{32,48... | collective-permute-start | bytes 786440 | tf_op jit(solution)/shard_map/ppermute | solution.py:189
  47.9 16.8 %collective-permute-start.8 = (f32[128,512]{1,0:T(8,128)S(1)}, f32[128,512]{1,0:T(8,128)S(1)}, u32[]{:S(2)}, u32[]{:S(2)}) collective-permute-start(f32[128,512]{1,0:T(8,128)S(1)} %get-tuple-element.32), channel_id=1, source_target_pairs={{0,8},{4,60},{8,16},{12,4},{16,24},{20,12},{24,32},{28,20},{32,40}... | collective-permute-start | bytes 786440 | tf_op jit(solution)/shard_map/ppermute | solution.py:190
  50.9 13.9 %collective-permute-start.9 = (f32[128,512]{1,0:T(8,128)S(1)}, f32[128,512]{1,0:T(8,128)S(1)}, u32[]{:S(2)}, u32[]{:S(2)}) collective-permute-start(f32[128,512]{1,0:T(8,128)S(1)} %get-tuple-element.33), channel_id=1, source_target_pairs={{0,12},{4,56},{8,20},{12,0},{16,28},{20,8},{24,36},{28,16},{32,44}... | collective-permute-start | bytes 786440 | tf_op jit(solution)/shard_map/ppermute | solution.py:191
  56.0 13.3 %collective-permute-start.12 = (f32[128,512]{1,0:T(8,128)S(1)}, f32[128,512]{1,0:T(8,128)S(1)}, u32[]{:S(2)}, u32[]{:S(2)}) collective-permute-start(f32[128,512]{1,0:T(8,128)S(1)} %get-tuple-element.37), channel_id=1, source_target_pairs={{0,16},{4,52},{8,24},{12,60},{16,32},{20,4},{24,40},{28,12},{32,48... | collective-permute-start | bytes 786440 | tf_op jit(solution)/shard_map/ppermute | solution.py:194
  62.0 15.3 %collective-permute-start.13 = (f32[128,512]{1,0:T(8,128)S(1)}, f32[128,512]{1,0:T(8,128)S(1)}, u32[]{:S(2)}, u32[]{:S(2)}) collective-permute-start(f32[128,512]{1,0:T(8,128)S(1)} %get-tuple-element.38), channel_id=1, source_target_pairs={{0,20},{4,48},{8,28},{12,56},{16,36},{20,0},{24,44},{28,8},{32,52}... | collective-permute-start | bytes 786440 | tf_op jit(solution)/shard_map/ppermute | solution.py:195

commit v5 on v4

--- a/solution.py
+++ b/solution.py
@@ -25,9 +25,10 @@
 
 
 def place_parts(pieces, high, low):
-    _, _, _, own_x = place()
+    _, core, _, own_x = place()
     for offset, piece in zip(OFFSETS, pieces):
-        rows = pl.ds(pl.multiple_of(((own_x + offset) % 4) * 128, 128), 128)
+        x = (own_x + jnp.where(core == 0, offset, 4 - offset)) % 4
+        rows = pl.ds(pl.multiple_of(x * 128, 128), 128)
         high[rows, :], low[rows, :] = two_parts(piece[...])
 
 
@@ -163,7 +164,7 @@
     pairs = []
     for ma in range(8):
         for ka in range(16):
-            step = 2 if offset == 2 and ka % 2 == 0 else -offset
+            step = -offset if ka % 2 == 0 else offset
             pairs.append((ma * 16 + ka, ((ma + 2 * step) % 8) * 16 + ka))
     return pairs
 

time: 78.6 us -> 78.6 us (level)
  starting transfers between devices: 51.5 us -> 48 us
  waiting for transfers between devices: 14.8 us -> 18.3 us
    ppermute x5, waiting for transfers between devices: 0.01 us -> 3.58 us  [from_row(): return [lax.ppermute(b, ('ma', 'ka'), by_x(offset)) for offset in offsets]]
    ppermute x5, starting transfers between devices: 17.6 us -> 15.8 us  [from_row(): return [lax.ppermute(b, ('ma', 'ka'), by_x(offset)) for offset in offsets]]
    ppermute x1, starting transfers between devices: 4.27 us -> 2.51 us  [shards(): lax.ppermute(given, 'ka', CORES)]
  transfers between devices with their start and end apart: 14 -> 14, of which waited for: 4 -> 5; matrix products, arithmetic and copies ran while one was open for 0% -> 0% of each run, Pallas kernels for 10% -> 10%
where the time goes in v5:
time: 78.6 us; the launch traced here: 78.1 us
  starting transfers between devices  48 us (61%)
  waiting for transfers between devices  18.3 us (23%)
  Pallas kernels  9.82 us (12%)
  local copies, waits for them, and re-layouts  0.94 us (1%)
  other arithmetic  0.83 us (1%)
    ppermute x5, starting transfers between devices, from_row(): return [lax.ppermute(b, ('ma', 'ka'), by_x(offset)) for offset in offsets]  15.8 us
    pallas_call x3, Pallas kernels, product(): pl.pallas_call(kernel, in_specs=[pl.BlockSpec(memory_space=pl.ANY) if rea...  9.55 us
    ppermute x1, waiting for transfers between devices, shards(): far_other = lax.ppermute(other, 'ka', along_y(2, 1))  7.96 us
    ppermute x2, starting transfers between devices, other_half(): return lax.ppermute(b, 'ma', HALVES)  5.92 us
    ppermute x1, starting transfers between devices, shards(): far_own = lax.ppermute(own, 'ka', along_y(2))  5.92 us
    ppermute x1, starting transfers between devices, shards(): got_three = lax.ppermute(three, 'ka', along_y(1))  5.1 us
    ppermute x1, waiting for transfers between devices, shards(): far_own = lax.ppermute(own, 'ka', along_y(2))  4.58 us
    ppermute x1, starting transfers between devices, shards(): got_four = lax.ppermute(four, 'ka', along_y(2))  3.79 us
  transfers between devices with their start and end apart: 14, of which 5 were waited for; matrix products, arithmetic and copies ran while one was open for 0% of the time, Pallas kernels for 10%

profile of v5, /device:TPU:129, one launch (start us, length us, event | category | flops | bytes accessed | tf_op | source)
XLA Modules:
  0.0 78.1 jit_solution(4483577764698647353)
XLA Ops:
  0.0 4.6 %collective-permute-start = (f32[128,512]{1,0:T(8,128)}, f32[128,512]{1,0:T(8,128)S(1)}, u32[]{:S(2)}, u32[]{:S(2)}) collective-permute-start(f32[128,512]{1,0:T(8,128)} %b0.1), channel_id=1, source_target_pairs={{0,256},{4,260},{8,264},{12,268},{16,272},{20,276},{24,280},{28,28... | collective-permute-start | bytes 786440 | tf_op jit(solution)/shard_map/ppermute | solution.py:177
  4.6 4.0 %collective-permute-start.3 = (f32[128,512]{1,0:T(8,128)}, f32[128,512]{1,0:T(8,128)S(1)}, u32[]{:S(2)}, u32[]{:S(2)}) collective-permute-start(f32[128,512]{1,0:T(8,128)} %b0.1), channel_id=1, source_target_pairs={{0,64},{64,0},{128,192},{192,128},{256,320},{320,256},{384,448},{4... | collective-permute-start | bytes 786440 | tf_op jit(solution)/shard_map/ppermute | solution.py:174
  8.7 2.8 %collective-permute-start.2 = (f32[128,512]{1,0:T(8,128)}, f32[128,512]{1,0:T(8,128)S(1)}, u32[]{:S(2)}, u32[]{:S(2)}) collective-permute-start(f32[128,512]{1,0:T(8,128)} %b0.1), channel_id=1, source_target_pairs={{0,128},{4,388},{8,136},{12,396},{16,144},{20,404},{24,152},{28,41... | collective-permute-start | bytes 786440 | tf_op jit(solution)/shard_map/ppermute | solution.py:177
  11.4 2.5 %collective-permute-start.1 = (f32[128,512]{1,0:T(8,128)}, f32[128,512]{1,0:T(8,128)S(1)}, u32[]{:S(2)}, u32[]{:S(2)}) collective-permute-start(f32[128,512]{1,0:T(8,128)} %b0.1), channel_id=1, source_target_pairs={{0,384},{4,132},{8,392},{12,140},{16,400},{20,148},{24,408},{28,15... | collective-permute-start | bytes 786440 | tf_op jit(solution)/shard_map/ppermute | solution.py:177
  14.0 0.0 collective-permute-done.b1
  14.0 1.9 %collective-permute-start.4 = (f32[128,512]{1,0:T(8,128)S(1)}, f32[128,512]{1,0:T(8,128)S(1)}, u32[]{:S(2)}, u32[]{:S(2)}) collective-permute-start(f32[128,512]{1,0:T(8,128)S(1)} %collective-permute-done.b1), channel_id=1, source_target_pairs={{0,64},{64,0},{128,192},{192,128},{256,320},{320,256},{384,448},{4... | collective-permute-start | bytes 786440 | tf_op jit(solution)/shard_map/ppermute | solution.py:174
  15.9 0.0 collective-permute-done.3.b0
  15.9 4.0 %collective-permute-start.6 = (f32[128,512]{1,0:T(8,128)S(1)}, f32[128,512]{1,0:T(8,128)S(1)}, u32[]{:S(2)}, u32[]{:S(2)}) collective-permute-start(f32[128,512]{1,0:T(8,128)S(1)} %collective-permute-done.3.b0), channel_id=1, source_target_pairs={{0,128},{4,388},{8,136},{12,396},{16,144},{20,404},{24,152},{28,41... | collective-permute-start | bytes 786440 | tf_op jit(solution)/shard_map/ppermute | solution.py:177
  19.9 1.9 %collective-permute-start.5 = (f32[128,512]{1,0:T(8,128)S(1)}, f32[128,512]{1,0:T(8,128)S(1)}, u32[]{:S(2)}, u32[]{:S(2)}) collective-permute-start(f32[128,512]{1,0:T(8,128)S(1)} %collective-permute-done.3.b0), channel_id=1, source_target_pairs={{0,384},{4,132},{8,392},{12,140},{16,400},{20,148},{24,408},{28,15... | collective-permute-start | bytes 786440 | tf_op jit(solution)/shard_map/ppermute | solution.py:177
  21.8 0.0 collective-permute-done.2.b3
  21.8 0.0 collective-permute-done.1.b2
  21.8 0.0 copy-start
  21.8 0.9 %copy-done = f32[128,512]{1,0:T(8,128)S(1)} copy-done((f32[128,512]{1,0:T(8,128)S(1)}, f32[128,512]{1,0:T(8,128)}, u32[]{:S(2)}) %copy-start) | copy-done | bytes 262168
  22.8 4.1 %shard_map.28 = (f32[1024,512]{1,0:T(8,128)S(1)}, bf16[1024,512]{1,0:T(8,128)(2,1)S(1)}, bf16[1024,512]{1,0:T(8,128)(2,1)S(1)}, bf16[512,512]{1,0:T(8,128)(2,1)S...) custom-call(f32[2048,1024]{1,0:T(8,128)} %a_hbm.1, f32[128,512]{1,0:T(8,128)S(1)} %copy-done, ...), custom_call_target="tpu_custom_call" | custom-call | flops 1610612736 | bytes 8388608 | tf_op jit(solution)/shard_map/pallas_call | solution.py:101
  26.9 0.0 collective-permute-done.4.b1
  26.9 0.0 collective-permute-done.6.b3
  26.9 3.6 %collective-permute-done.5.b2 = f32[128,512]{1,0:T(8,128)S(1)} collective-permute-done((f32[128,512]{1,0:T(8,128)S(1)}, f32[128,512]{1,0:T(8,128)S(1)}, u32[]{:S(2)}, u32[]{:S(2)}) %collective-permute-start.5) | collective-permute-done | bytes 262176 | tf_op jit(solution)/shard_map/ppermute | solution.py:177
  30.5 2.0 %shard_map.29 = (f32[1024,512]{1,0:T(8,128)S(1)}, bf16[512,512]{1,0:T(8,128)(2,1)S(1)}, bf16[512,512]{1,0:T(8,128)(2,1)S(1)}) custom-call(f32[1024,512]{1,0:T(8,128)S(1)} %get-tuple-element.22.sums, bf16[1024,512]{1,0:T(8,128)(2,1)S(1)} %get-tuple-element.23.a_high, bf16[1024,512]{1,0:T(8,128)(2,1)S(1)} %get-tuple-element.24.a_low, ...), custom_call_target="tpu_custom_call" | custom-call | flops 1610612736 | bytes 8388608 | tf_op jit(solution)/shard_map/pallas_call | solution.py:101
  32.5 2.5 %collective-permute-start.7 = (f32[1024,512]{1,0:T(8,128)S(1)}, f32[1024,512]{1,0:T(8,128)S(1)}, u32[]{:S(2)}, u32[]{:S(2)}) collective-permute-start(f32[1024,512]{1,0:T(8,128)S(1)} %get-tuple-element.25), channel_id=1, source_target_pairs={{0,4},{4,0},{8,12},{12,8},{16,20},{20,16},{24,28},{28,24},{32,36},... | collective-permute-start | bytes 6291464 | tf_op jit(solution)/shard_map/ppermute | solution.py:188
  35.0 3.4 %shard_map.30.second = f32[1024,512]{1,0:T(8,128)S(1)} custom-call(f32[1024,1024]{1,0:T(8,128)S(1)} %get-tuple-element.26.a_ref, bf16[512,512]{1,0:T(8,128)(2,1)S(1)} %get-tuple-element.27.near_high, bf16[512,512]{1,0:T(8,128)(2,1)S(1)} %get-tuple-element.28.near_low, bf16[512,512]{1,0:T(8,128)(2,1)S(1)} %get-tuple-element.29.far_high, ...), custom_call_target="tpu_custom_call" | custom-call | flops 1610612736 | bytes 8388608 | tf_op jit(solution)/shard_map/pallas_call | solution.py:101
  38.5 0.3 collective-permute-done.7.first
  38.8 0.2 shard_map.31
  39.0 5.1 %collective-permute-start.10 = (f32[256,512]{1,0:T(8,128)S(1)}, f32[256,512]{1,0:T(8,128)S(1)}, u32[]{:S(2)}, u32[]{:S(2)}) collective-permute-start(f32[256,512]{1,0:T(8,128)S(1)} %get-tuple-element.35), channel_id=1, source_target_pairs={{0,8},{4,60},{8,16},{12,4},{16,24},{20,12},{24,32},{28,20},{32,40}... | collective-permute-start | bytes 1572872 | tf_op jit(solution)/shard_map/ppermute | solution.py:189
  44.1 3.8 %collective-permute-start.11 = (f32[128,512]{1,0:T(8,128)S(1)}, f32[128,512]{1,0:T(8,128)S(1)}, u32[]{:S(2)}, u32[]{:S(2)}) collective-permute-start(f32[128,512]{1,0:T(8,128)S(1)} %get-tuple-element.36), channel_id=1, source_target_pairs={{0,16},{4,52},{8,24},{12,60},{16,32},{20,4},{24,40},{28,12},{32,48... | collective-permute-start | bytes 786440 | tf_op jit(solution)/shard_map/ppermute | solution.py:190
  47.9 3.0 %collective-permute-start.8 = (f32[128,512]{1,0:T(8,128)S(1)}, f32[128,512]{1,0:T(8,128)S(1)}, u32[]{:S(2)}, u32[]{:S(2)}) collective-permute-start(f32[128,512]{1,0:T(8,128)S(1)} %get-tuple-element.32), channel_id=1, source_target_pairs={{0,8},{4,60},{8,16},{12,4},{16,24},{20,12},{24,32},{28,20},{32,40}... | collective-permute-start | bytes 786440 | tf_op jit(solution)/shard_map/ppermute | solution.py:191
  50.9 3.2 %collective-permute-start.9 = (f32[128,512]{1,0:T(8,128)S(1)}, f32[128,512]{1,0:T(8,128)S(1)}, u32[]{:S(2)}, u32[]{:S(2)}) collective-permute-start(f32[128,512]{1,0:T(8,128)S(1)} %get-tuple-element.33), channel_id=1, source_target_pairs={{0,12},{4,56},{8,20},{12,0},{16,28},{20,8},{24,36},{28,16},{32,44}... | collective-permute-start | bytes 786440 | tf_op jit(solution)/shard_map/ppermute | solution.py:192
  54.1 1.9 %collective-permute-done.11.got_four = f32[128,512]{1,0:T(8,128)S(1)} collective-permute-done((f32[128,512]{1,0:T(8,128)S(1)}, f32[128,512]{1,0:T(8,128)S(1)}, u32[]{:S(2)}, u32[]{:S(2)}) %collective-permute-start.11) | collective-permute-done | bytes 262176 | tf_op jit(solution)/shard_map/ppermute | solution.py:190
  55.9 0.0 collective-permute-done.10.got_three
  56.0 0.1 shard_map.32
  56.0 5.9 %collective-permute-start.12 = (f32[128,512]{1,0:T(8,128)S(1)}, f32[128,512]{1,0:T(8,128)S(1)}, u32[]{:S(2)}, u32[]{:S(2)}) collective-permute-start(f32[128,512]{1,0:T(8,128)S(1)} %get-tuple-element.37), channel_id=1, source_target_pairs={{0,16},{4,52},{8,24},{12,60},{16,32},{20,4},{24,40},{28,12},{32,48... | collective-permute-start | bytes 786440 | tf_op jit(solution)/shard_map/ppermute | solution.py:195
  61.9 2.8 %collective-permute-start.13 = (f32[128,512]{1,0:T(8,128)S(1)}, f32[128,512]{1,0:T(8,128)S(1)}, u32[]{:S(2)}, u32[]{:S(2)}) collective-permute-start(f32[128,512]{1,0:T(8,128)S(1)} %get-tuple-element.38), channel_id=1, source_target_pairs={{0,20},{4,48},{8,28},{12,56},{16,36},{20,0},{24,44},{28,8},{32,52}... | collective-permute-start | bytes 786440 | tf_op jit(solution)/shard_map/ppermute | solution.py:196
  64.7 0.0 collective-permute-done.8
  64.7 0.0 collective-permute-done.9
  64.7 4.6 %collective-permute-done.12 = f32[128,512]{1,0:T(8,128)S(1)} collective-permute-done((f32[128,512]{1,0:T(8,128)S(1)}, f32[128,512]{1,0:T(8,128)S(1)}, u32[]{:S(2)}, u32[]{:S(2)}) %collective-permute-start.12) | collective-permute-done | bytes 262176 | tf_op jit(solution)/shard_map/ppermute | solution.py:195
  69.3 8.0 %collective-permute-done.13 = f32[128,512]{1,0:T(8,128)S(1)} collective-permute-done((f32[128,512]{1,0:T(8,128)S(1)}, f32[128,512]{1,0:T(8,128)S(1)}, u32[]{:S(2)}, u32[]{:S(2)}) %collective-permute-start.13) | collective-permute-done | bytes 262176 | tf_op jit(solution)/shard_map/ppermute | solution.py:196
  77.3 0.8 %add_add_fusion = f32[128,512]{1,0:T(8,128)} fusion(f32[128,512]{1,0:T(8,128)S(1)} %collective-permute-done.13, f32[128,512]{1,0:T(8,128)S(1)} %collective-permute-done.12, f32[128,512]{1,0:T(8,128)S(1)} %collective-permute-done.9, f32[128,512]{1,0:T(8,128)S(1)} %get-tuple-element.31, f32[128,512]{1,0:T(8,128)S(1)} %collective-permute-done.8), kind=kLoop, calls=%fused_computation | loop fusion | flops 262144 | bytes 1572864 | tf_op jit(solution)/shard_map/add | solution.py:197
Async XLA Ops:
  0.0 14.0 %collective-permute-start = (f32[128,512]{1,0:T(8,128)}, f32[128,512]{1,0:T(8,128)S(1)}, u32[]{:S(2)}, u32[]{:S(2)}) collective-permute-start(f32[128,512]{1,0:T(8,128)} %b0.1), channel_id=1, source_target_pairs={{0,256},{4,260},{8,264},{12,268},{16,272},{20,276},{24,280},{28,28... | collective-permute-start | bytes 786440 | tf_op jit(solution)/shard_map/ppermute | solution.py:177
  4.6 11.2 %collective-permute-start.3 = (f32[128,512]{1,0:T(8,128)}, f32[128,512]{1,0:T(8,128)S(1)}, u32[]{:S(2)}, u32[]{:S(2)}) collective-permute-start(f32[128,512]{1,0:T(8,128)} %b0.1), channel_id=1, source_target_pairs={{0,64},{64,0},{128,192},{192,128},{256,320},{320,256},{384,448},{4... | collective-permute-start | bytes 786440 | tf_op jit(solution)/shard_map/ppermute | solution.py:174
  8.7 13.2 %collective-permute-start.2 = (f32[128,512]{1,0:T(8,128)}, f32[128,512]{1,0:T(8,128)S(1)}, u32[]{:S(2)}, u32[]{:S(2)}) collective-permute-start(f32[128,512]{1,0:T(8,128)} %b0.1), channel_id=1, source_target_pairs={{0,128},{4,388},{8,136},{12,396},{16,144},{20,404},{24,152},{28,41... | collective-permute-start | bytes 786440 | tf_op jit(solution)/shard_map/ppermute | solution.py:177
  11.4 10.4 %collective-permute-start.1 = (f32[128,512]{1,0:T(8,128)}, f32[128,512]{1,0:T(8,128)S(1)}, u32[]{:S(2)}, u32[]{:S(2)}) collective-permute-start(f32[128,512]{1,0:T(8,128)} %b0.1), channel_id=1, source_target_pairs={{0,384},{4,132},{8,392},{12,140},{16,400},{20,148},{24,408},{28,15... | collective-permute-start | bytes 786440 | tf_op jit(solution)/shard_map/ppermute | solution.py:177
  14.0 13.0 %collective-permute-start.4 = (f32[128,512]{1,0:T(8,128)S(1)}, f32[128,512]{1,0:T(8,128)S(1)}, u32[]{:S(2)}, u32[]{:S(2)}) collective-permute-start(f32[128,512]{1,0:T(8,128)S(1)} %collective-permute-done.b1), channel_id=1, source_target_pairs={{0,64},{64,0},{128,192},{192,128},{256,320},{320,256},{384,448},{4... | collective-permute-start | bytes 786440 | tf_op jit(solution)/shard_map/ppermute | solution.py:174
  15.9 11.0 %collective-permute-start.6 = (f32[128,512]{1,0:T(8,128)S(1)}, f32[128,512]{1,0:T(8,128)S(1)}, u32[]{:S(2)}, u32[]{:S(2)}) collective-permute-start(f32[128,512]{1,0:T(8,128)S(1)} %collective-permute-done.3.b0), channel_id=1, source_target_pairs={{0,128},{4,388},{8,136},{12,396},{16,144},{20,404},{24,152},{28,41... | collective-permute-start | bytes 786440 | tf_op jit(solution)/shard_map/ppermute | solution.py:177
  19.9 10.6 %collective-permute-start.5 = (f32[128,512]{1,0:T(8,128)S(1)}, f32[128,512]{1,0:T(8,128)S(1)}, u32[]{:S(2)}, u32[]{:S(2)}) collective-permute-start(f32[128,512]{1,0:T(8,128)S(1)} %collective-permute-done.3.b0), channel_id=1, source_target_pairs={{0,384},{4,132},{8,392},{12,140},{16,400},{20,148},{24,408},{28,15... | collective-permute-start | bytes 786440 | tf_op jit(solution)/shard_map/ppermute | solution.py:177
  21.8 1.0 %copy-start = (f32[128,512]{1,0:T(8,128)S(1)}, f32[128,512]{1,0:T(8,128)}, u32[]{:S(2)}) copy-start(f32[128,512]{1,0:T(8,128)} %b0.1) | copy-start | bytes 786436
  32.5 6.3 %collective-permute-start.7 = (f32[1024,512]{1,0:T(8,128)S(1)}, f32[1024,512]{1,0:T(8,128)S(1)}, u32[]{:S(2)}, u32[]{:S(2)}) collective-permute-start(f32[1024,512]{1,0:T(8,128)S(1)} %get-tuple-element.25), channel_id=1, source_target_pairs={{0,4},{4,0},{8,12},{12,8},{16,20},{20,16},{24,28},{28,24},{32,36},... | collective-permute-start | bytes 6291464 | tf_op jit(solution)/shard_map/ppermute | solution.py:188
  39.0 16.9 %collective-permute-start.10 = (f32[256,512]{1,0:T(8,128)S(1)}, f32[256,512]{1,0:T(8,128)S(1)}, u32[]{:S(2)}, u32[]{:S(2)}) collective-permute-start(f32[256,512]{1,0:T(8,128)S(1)} %get-tuple-element.35), channel_id=1, source_target_pairs={{0,8},{4,60},{8,16},{12,4},{16,24},{20,12},{24,32},{28,20},{32,40}... | collective-permute-start | bytes 1572872 | tf_op jit(solution)/shard_map/ppermute | solution.py:189
  44.1 11.8 %collective-permute-start.11 = (f32[128,512]{1,0:T(8,128)S(1)}, f32[128,512]{1,0:T(8,128)S(1)}, u32[]{:S(2)}, u32[]{:S(2)}) collective-permute-start(f32[128,512]{1,0:T(8,128)S(1)} %get-tuple-element.36), channel_id=1, source_target_pairs={{0,16},{4,52},{8,24},{12,60},{16,32},{20,4},{24,40},{28,12},{32,48... | collective-permute-start | bytes 786440 | tf_op jit(solution)/shard_map/ppermute | solution.py:190
  47.9 16.8 %collective-permute-start.8 = (f32[128,512]{1,0:T(8,128)S(1)}, f32[128,512]{1,0:T(8,128)S(1)}, u32[]{:S(2)}, u32[]{:S(2)}) collective-permute-start(f32[128,512]{1,0:T(8,128)S(1)} %get-tuple-element.32), channel_id=1, source_target_pairs={{0,8},{4,60},{8,16},{12,4},{16,24},{20,12},{24,32},{28,20},{32,40}... | collective-permute-start | bytes 786440 | tf_op jit(solution)/shard_map/ppermute | solution.py:191
  50.9 13.8 %collective-permute-start.9 = (f32[128,512]{1,0:T(8,128)S(1)}, f32[128,512]{1,0:T(8,128)S(1)}, u32[]{:S(2)}, u32[]{:S(2)}) collective-permute-start(f32[128,512]{1,0:T(8,128)S(1)} %get-tuple-element.33), channel_id=1, source_target_pairs={{0,12},{4,56},{8,20},{12,0},{16,28},{20,8},{24,36},{28,16},{32,44}... | collective-permute-start | bytes 786440 | tf_op jit(solution)/shard_map/ppermute | solution.py:192
  56.0 13.3 %collective-permute-start.12 = (f32[128,512]{1,0:T(8,128)S(1)}, f32[128,512]{1,0:T(8,128)S(1)}, u32[]{:S(2)}, u32[]{:S(2)}) collective-permute-start(f32[128,512]{1,0:T(8,128)S(1)} %get-tuple-element.37), channel_id=1, source_target_pairs={{0,16},{4,52},{8,24},{12,60},{16,32},{20,4},{24,40},{28,12},{32,48... | collective-permute-start | bytes 786440 | tf_op jit(solution)/shard_map/ppermute | solution.py:195
  61.9 15.3 %collective-permute-start.13 = (f32[128,512]{1,0:T(8,128)S(1)}, f32[128,512]{1,0:T(8,128)S(1)}, u32[]{:S(2)}, u32[]{:S(2)}) collective-permute-start(f32[128,512]{1,0:T(8,128)S(1)} %get-tuple-element.38), channel_id=1, source_target_pairs={{0,20},{4,48},{8,28},{12,56},{16,36},{20,0},{24,44},{28,8},{32,52}... | collective-permute-start | bytes 786440 | tf_op jit(solution)/shard_map/ppermute | solution.py:196

commit v6 on v5

--- a/solution.py
+++ b/solution.py
@@ -82,17 +82,26 @@
         copy.wait()
 
 
-def late_kernel(sums, a_high, a_low, b0, b1, b2, b3, out, b_high, b_low):
+def store(rows, value, out, zero_out):
+    if rows.stop <= 896:
+        out[rows, :] = value
+    else:
+        out[rows.start : 896, :] = value[:128]
+        zero_out[...] = value[128:]
+
+
+def late_kernel(sums, a_high, a_low, b0, b1, b2, b3, out, zero_out, b_high, b_low):
     place_parts((b0, b1, b2, b3), b_high, b_low)
     for step in range(4):
         rows = slice(256 * step, 256 * step + 256)
-        out[rows, :] = sums[rows, :] + three_dots(a_high[rows, :], a_low[rows, :], b_high, b_low)
-
-
-def whole_kernel(a_ref, near_high, near_low, far_high, far_low, out):
+        value = sums[rows, :] + three_dots(a_high[rows, :], a_low[rows, :], b_high, b_low)
+        store(rows, value, out, zero_out)
+
+
+def whole_kernel(a_ref, near_high, near_low, far_high, far_low, out, zero_out):
     def body(z, rows):
         near = three_dots(*parts_of(a_ref, rows, z), near_high, near_low)
-        out[rows, :] = near + three_dots(*parts_of(a_ref, rows, 1 - z), far_high, far_low)
+        store(rows, near + three_dots(*parts_of(a_ref, rows, 1 - z), far_high, far_low), out, zero_out)
 
     for_each_tile(body)
 
@@ -109,16 +118,16 @@
     )(*args)
 
 
-def add_kernel(first, second, three, four, one_own, one_other, two, zero):
+def add_kernel(first, second, three, four, one_own, one_other, two):
     _, core, _, _ = place()
     own, other = (pl.multiple_of(256 + side * 128, 128) for side in (core, 1 - core))
-    for start, out in ((0, three), (own, one_own), (other, one_other), (512, two), (768, four), (896, zero)):
+    for start, out in ((0, three), (own, one_own), (other, one_other), (512, two), (768, four)):
         rows = pl.ds(start, out.shape[0])
         out[...] = first[rows, :] + second[rows, :]
 
 
 def add(first, second):
-    counts = (256, 128, 128, 128, 256, 128)
+    counts = (256, 128, 128, 128, 256)
     return pl.pallas_call(
         add_kernel,
         in_specs=[VMEM] * 2,
@@ -182,10 +191,11 @@
     sums, parts, b_parts = ((1024, 512), F32), [((1024, 512), BF16)] * 2, [((512, 512), BF16)] * 2
     outs = [sums] + parts + b_parts + [((1024, 1024), F32)]
     first, a_high, a_low, near_high, near_low, a_kept = product(early_kernel, outs, True, 40, left_matrix, *near_b)
-    given, far_high, far_low = product(late_kernel, [sums] + b_parts, False, 14, first, a_high, a_low, *far_b)
-    kept = product(whole_kernel, [sums], False, 14, a_kept, near_high, near_low, far_high, far_low)[0]
-
-    three, four, one_own, one_other, two, zero = add(lax.ppermute(given, "ka", CORES), kept)
+    swapped_sums = [((896, 512), F32), ((128, 512), F32)]
+    given, zero_given, far_high, far_low = product(late_kernel, swapped_sums + b_parts, False, 14, first, a_high, a_low, *far_b)
+    kept, zero = product(whole_kernel, swapped_sums, False, 14, a_kept, near_high, near_low, far_high, far_low)
+
+    three, four, one_own, one_other, two = add(lax.ppermute(given, "ka", CORES), kept)
     got_three = lax.ppermute(three, "ka", along_y(1))
     got_four = lax.ppermute(four, "ka", along_y(2))
     near_own = lax.ppermute(one_own, "ka", along_y(1))
@@ -194,7 +204,8 @@
     own, other = halves(pass_on_kernel, two, got_three, got_four)
     far_own = lax.ppermute(own, "ka", along_y(2))
     far_other = lax.ppermute(other, "ka", along_y(2, 1))
-    return zero + near_own + near_other + far_own + far_other
+    zero_got = lax.ppermute(zero_given, "ka", CORES)
+    return zero + zero_got + near_own + near_other + far_own + far_other
 
 
 def solution(mesh):

time: 78.6 us -> 78.3 us (level)
  waiting for transfers between devices: 18.3 us -> 16.2 us
  starting transfers between devices: 48 us -> 49.7 us
    ppermute x0 -> x1, starting transfers between devices: none -> 1.92 us  [shards(): zero_got = lax.ppermute(zero_given, 'ka', CORES)]
    ppermute x1, waiting for transfers between devices: 1.87 us -> 0.01 us  [shards(): got_four = lax.ppermute(four, 'ka', along_y(2))]
    ppermute x1, starting transfers between devices: 5.92 us -> 4.83 us  [shards(): far_own = lax.ppermute(own, 'ka', along_y(2))]
    ppermute x1, starting transfers between devices: 3.18 us -> 4.18 us  [shards(): near_other = lax.ppermute(one_other, 'ka', along_y(1, 1))]
  transfers between devices with their start and end apart: 14 -> 15, of which waited for: 5 -> 3; matrix products, arithmetic and copies ran while one was open for 0% -> 0% of each run, Pallas kernels for 10% -> 10%
where the time goes in v6:
time: 78.3 us; the launch traced here: 77.8 us
  starting transfers between devices  49.7 us (63%)
  waiting for transfers between devices  16.2 us (21%)
  Pallas kernels  9.81 us (13%)
  local copies, waits for them, and re-layouts  0.94 us (1%)
  other arithmetic  0.85 us (1%)
    ppermute x5, starting transfers between devices, from_row(): return [lax.ppermute(b, ('ma', 'ka'), by_x(offset)) for offset in offsets]  15.8 us
    pallas_call x3, Pallas kernels, product(): pl.pallas_call(kernel, in_specs=[pl.BlockSpec(memory_space=pl.ANY) if rea...  9.55 us
    ppermute x1, waiting for transfers between devices, shards(): far_other = lax.ppermute(other, 'ka', along_y(2, 1))  7.7 us
    ppermute x2, starting transfers between devices, other_half(): return lax.ppermute(b, 'ma', HALVES)  5.92 us
    ppermute x1, starting transfers between devices, shards(): got_three = lax.ppermute(three, 'ka', along_y(1))  5.1 us
    ppermute x1, waiting for transfers between devices, shards(): far_own = lax.ppermute(own, 'ka', along_y(2))  4.9 us
    ppermute x1, starting transfers between devices, shards(): far_own = lax.ppermute(own, 'ka', along_y(2))  4.83 us
    ppermute x1, starting transfers between devices, shards(): near_other = lax.ppermute(one_other, 'ka', along_y(1, 1))  4.18 us
  transfers between devices with their start and end apart: 15, of which 3 were waited for; matrix products, arithmetic and copies ran while one was open for 0% of the time, Pallas kernels for 10%

profile of v6, /device:TPU:129, one launch (start us, length us, event | category | flops | bytes accessed | tf_op | source)
XLA Modules:
  0.0 77.8 jit_solution(1731280574347258690)
XLA Ops:
  0.0 4.6 %collective-permute-start = (f32[128,512]{1,0:T(8,128)}, f32[128,512]{1,0:T(8,128)S(1)}, u32[]{:S(2)}, u32[]{:S(2)}) collective-permute-start(f32[128,512]{1,0:T(8,128)} %b0.1), channel_id=1, source_target_pairs={{0,256},{4,260},{8,264},{12,268},{16,272},{20,276},{24,280},{28,28... | collective-permute-start | bytes 786440 | tf_op jit(solution)/shard_map/ppermute | solution.py:186
  4.6 4.0 %collective-permute-start.3 = (f32[128,512]{1,0:T(8,128)}, f32[128,512]{1,0:T(8,128)S(1)}, u32[]{:S(2)}, u32[]{:S(2)}) collective-permute-start(f32[128,512]{1,0:T(8,128)} %b0.1), channel_id=1, source_target_pairs={{0,64},{64,0},{128,192},{192,128},{256,320},{320,256},{384,448},{4... | collective-permute-start | bytes 786440 | tf_op jit(solution)/shard_map/ppermute | solution.py:183
  8.7 2.8 %collective-permute-start.2 = (f32[128,512]{1,0:T(8,128)}, f32[128,512]{1,0:T(8,128)S(1)}, u32[]{:S(2)}, u32[]{:S(2)}) collective-permute-start(f32[128,512]{1,0:T(8,128)} %b0.1), channel_id=1, source_target_pairs={{0,128},{4,388},{8,136},{12,396},{16,144},{20,404},{24,152},{28,41... | collective-permute-start | bytes 786440 | tf_op jit(solution)/shard_map/ppermute | solution.py:186
  11.4 2.5 %collective-permute-start.1 = (f32[128,512]{1,0:T(8,128)}, f32[128,512]{1,0:T(8,128)S(1)}, u32[]{:S(2)}, u32[]{:S(2)}) collective-permute-start(f32[128,512]{1,0:T(8,128)} %b0.1), channel_id=1, source_target_pairs={{0,384},{4,132},{8,392},{12,140},{16,400},{20,148},{24,408},{28,15... | collective-permute-start | bytes 786440 | tf_op jit(solution)/shard_map/ppermute | solution.py:186
  14.0 0.0 collective-permute-done.b1
  14.0 1.9 %collective-permute-start.4 = (f32[128,512]{1,0:T(8,128)S(1)}, f32[128,512]{1,0:T(8,128)S(1)}, u32[]{:S(2)}, u32[]{:S(2)}) collective-permute-start(f32[128,512]{1,0:T(8,128)S(1)} %collective-permute-done.b1), channel_id=1, source_target_pairs={{0,64},{64,0},{128,192},{192,128},{256,320},{320,256},{384,448},{4... | collective-permute-start | bytes 786440 | tf_op jit(solution)/shard_map/ppermute | solution.py:183
  15.9 0.0 collective-permute-done.3.b0
  15.9 4.0 %collective-permute-start.6 = (f32[128,512]{1,0:T(8,128)S(1)}, f32[128,512]{1,0:T(8,128)S(1)}, u32[]{:S(2)}, u32[]{:S(2)}) collective-permute-start(f32[128,512]{1,0:T(8,128)S(1)} %collective-permute-done.3.b0), channel_id=1, source_target_pairs={{0,128},{4,388},{8,136},{12,396},{16,144},{20,404},{24,152},{28,41... | collective-permute-start | bytes 786440 | tf_op jit(solution)/shard_map/ppermute | solution.py:186
  19.9 1.9 %collective-permute-start.5 = (f32[128,512]{1,0:T(8,128)S(1)}, f32[128,512]{1,0:T(8,128)S(1)}, u32[]{:S(2)}, u32[]{:S(2)}) collective-permute-start(f32[128,512]{1,0:T(8,128)S(1)} %collective-permute-done.3.b0), channel_id=1, source_target_pairs={{0,384},{4,132},{8,392},{12,140},{16,400},{20,148},{24,408},{28,15... | collective-permute-start | bytes 786440 | tf_op jit(solution)/shard_map/ppermute | solution.py:186
  21.8 0.0 collective-permute-done.2.b3
  21.8 0.0 collective-permute-done.1.b2
  21.8 0.0 copy-start
  21.8 0.9 %copy-done = f32[128,512]{1,0:T(8,128)S(1)} copy-done((f32[128,512]{1,0:T(8,128)S(1)}, f32[128,512]{1,0:T(8,128)}, u32[]{:S(2)}) %copy-start) | copy-done | bytes 262168
  22.8 4.1 %shard_map.28 = (f32[1024,512]{1,0:T(8,128)S(1)}, bf16[1024,512]{1,0:T(8,128)(2,1)S(1)}, bf16[1024,512]{1,0:T(8,128)(2,1)S(1)}, bf16[512,512]{1,0:T(8,128)(2,1)S...) custom-call(f32[2048,1024]{1,0:T(8,128)} %a_hbm.1, f32[128,512]{1,0:T(8,128)S(1)} %copy-done, ...), custom_call_target="tpu_custom_call" | custom-call | flops 1610612736 | bytes 8388608 | tf_op jit(solution)/shard_map/pallas_call | solution.py:110
  26.9 0.0 collective-permute-done.4.b1
  26.9 0.0 collective-permute-done.6.b3
  26.9 3.6 %collective-permute-done.5.b2 = f32[128,512]{1,0:T(8,128)S(1)} collective-permute-done((f32[128,512]{1,0:T(8,128)S(1)}, f32[128,512]{1,0:T(8,128)S(1)}, u32[]{:S(2)}, u32[]{:S(2)}) %collective-permute-start.5) | collective-permute-done | bytes 262176 | tf_op jit(solution)/shard_map/ppermute | solution.py:186
  30.5 2.0 %shard_map.29 = (f32[896,512]{1,0:T(8,128)S(1)}, f32[128,512]{1,0:T(8,128)S(1)}, bf16[512,512]{1,0:T(8,128)(2,1)S(1)}, bf16[512,512]{1,0:T(8,128)(2,1)S(1)}) custom-call(f32[1024,512]{1,0:T(8,128)S(1)} %get-tuple-element.27.sums, bf16[1024,512]{1,0:T(8,128)(2,1)S(1)} %get-tuple-element.28.a_high, bf16[1024,512]{1,0:T(8,128)(2,1)S(1)} %get-tuple-element.29.a_low, ...), custom_call_target="tpu_custom_call" | custom-call | flops 1610612736 | bytes 8388608 | tf_op jit(solution)/shard_map/pallas_call | solution.py:110
  32.5 2.5 %collective-permute-start.8 = (f32[896,512]{1,0:T(8,128)S(1)}, f32[896,512]{1,0:T(8,128)S(1)}, u32[]{:S(2)}, u32[]{:S(2)}) collective-permute-start(f32[896,512]{1,0:T(8,128)S(1)} %get-tuple-element.34), channel_id=1, source_target_pairs={{0,4},{4,0},{8,12},{12,8},{16,20},{20,16},{24,28},{28,24},{32,36},... | collective-permute-start | bytes 5505032 | tf_op jit(solution)/shard_map/ppermute | solution.py:198
  35.0 3.4 %shard_map.30 = (f32[896,512]{1,0:T(8,128)S(1)}, f32[128,512]{1,0:T(8,128)S(1)}) custom-call(f32[1024,1024]{1,0:T(8,128)S(1)} %get-tuple-element.24.a_ref, bf16[512,512]{1,0:T(8,128)(2,1)S(1)} %get-tuple-element.25.near_high, bf16[512,512]{1,0:T(8,128)(2,1)S(1)} %get-tuple-element.26.near_low, bf16[512,512]{1,0:T(8,128)(2,1)S(1)} %get-tuple-element.30.far_high, ...), custom_call_target="tpu_custom_call" | custom-call | flops 1610612736 | bytes 8388608 | tf_op jit(solution)/shard_map/pallas_call | solution.py:110
  38.5 0.0 collective-permute-done.8.first
  38.5 0.2 shard_map.31
  38.7 5.1 %collective-permute-start.11 = (f32[256,512]{1,0:T(8,128)S(1)}, f32[256,512]{1,0:T(8,128)S(1)}, u32[]{:S(2)}, u32[]{:S(2)}) collective-permute-start(f32[256,512]{1,0:T(8,128)S(1)} %get-tuple-element.39), channel_id=1, source_target_pairs={{0,8},{4,60},{8,16},{12,4},{16,24},{20,12},{24,32},{28,20},{32,40}... | collective-permute-start | bytes 1572872 | tf_op jit(solution)/shard_map/ppermute | solution.py:199
  43.8 3.8 %collective-permute-start.12 = (f32[128,512]{1,0:T(8,128)S(1)}, f32[128,512]{1,0:T(8,128)S(1)}, u32[]{:S(2)}, u32[]{:S(2)}) collective-permute-start(f32[128,512]{1,0:T(8,128)S(1)} %get-tuple-element.40), channel_id=1, source_target_pairs={{0,16},{4,52},{8,24},{12,60},{16,32},{20,4},{24,40},{28,12},{32,48... | collective-permute-start | bytes 786440 | tf_op jit(solution)/shard_map/ppermute | solution.py:200
  47.6 1.9 %collective-permute-start.7 = (f32[128,512]{1,0:T(8,128)S(1)}, f32[128,512]{1,0:T(8,128)S(1)}, u32[]{:S(2)}, u32[]{:S(2)}) collective-permute-start(f32[128,512]{1,0:T(8,128)S(1)} %get-tuple-element.33), channel_id=1, source_target_pairs={{0,4},{4,0},{8,12},{12,8},{16,20},{20,16},{24,28},{28,24},{32,36},... | collective-permute-start | bytes 786440 | tf_op jit(solution)/shard_map/ppermute | solution.py:207
  49.5 3.0 %collective-permute-start.9 = (f32[128,512]{1,0:T(8,128)S(1)}, f32[128,512]{1,0:T(8,128)S(1)}, u32[]{:S(2)}, u32[]{:S(2)}) collective-permute-start(f32[128,512]{1,0:T(8,128)S(1)} %get-tuple-element.36), channel_id=1, source_target_pairs={{0,8},{4,60},{8,16},{12,4},{16,24},{20,12},{24,32},{28,20},{32,40}... | collective-permute-start | bytes 786440 | tf_op jit(solution)/shard_map/ppermute | solution.py:201
  52.5 4.2 %collective-permute-start.10 = (f32[128,512]{1,0:T(8,128)S(1)}, f32[128,512]{1,0:T(8,128)S(1)}, u32[]{:S(2)}, u32[]{:S(2)}) collective-permute-start(f32[128,512]{1,0:T(8,128)S(1)} %get-tuple-element.37), channel_id=1, source_target_pairs={{0,12},{4,56},{8,20},{12,0},{16,28},{20,8},{24,36},{28,16},{32,44}... | collective-permute-start | bytes 786440 | tf_op jit(solution)/shard_map/ppermute | solution.py:202
  56.7 0.0 collective-permute-done.12.got_four
  56.7 0.0 collective-permute-done.11.got_three
  56.7 0.1 shard_map.32
  56.8 4.8 %collective-permute-start.13 = (f32[128,512]{1,0:T(8,128)S(1)}, f32[128,512]{1,0:T(8,128)S(1)}, u32[]{:S(2)}, u32[]{:S(2)}) collective-permute-start(f32[128,512]{1,0:T(8,128)S(1)} %get-tuple-element.41), channel_id=1, source_target_pairs={{0,16},{4,52},{8,24},{12,60},{16,32},{20,4},{24,40},{28,12},{32,48... | collective-permute-start | bytes 786440 | tf_op jit(solution)/shard_map/ppermute | solution.py:205
  61.6 2.7 %collective-permute-start.14 = (f32[128,512]{1,0:T(8,128)S(1)}, f32[128,512]{1,0:T(8,128)S(1)}, u32[]{:S(2)}, u32[]{:S(2)}) collective-permute-start(f32[128,512]{1,0:T(8,128)S(1)} %get-tuple-element.42), channel_id=1, source_target_pairs={{0,20},{4,48},{8,28},{12,56},{16,36},{20,0},{24,44},{28,8},{32,52}... | collective-permute-start | bytes 786440 | tf_op jit(solution)/shard_map/ppermute | solution.py:206
  64.3 0.0 collective-permute-done.7
  64.3 0.0 collective-permute-done.9
  64.3 0.0 collective-permute-done.10
  64.3 4.9 %collective-permute-done.13 = f32[128,512]{1,0:T(8,128)S(1)} collective-permute-done((f32[128,512]{1,0:T(8,128)S(1)}, f32[128,512]{1,0:T(8,128)S(1)}, u32[]{:S(2)}, u32[]{:S(2)}) %collective-permute-start.13) | collective-permute-done | bytes 262176 | tf_op jit(solution)/shard_map/ppermute | solution.py:205
  69.2 7.7 %collective-permute-done.14 = f32[128,512]{1,0:T(8,128)S(1)} collective-permute-done((f32[128,512]{1,0:T(8,128)S(1)}, f32[128,512]{1,0:T(8,128)S(1)}, u32[]{:S(2)}, u32[]{:S(2)}) %collective-permute-start.14) | collective-permute-done | bytes 262176 | tf_op jit(solution)/shard_map/ppermute | solution.py:206
  76.9 0.8 %add_add_fusion = f32[128,512]{1,0:T(8,128)} fusion(f32[128,512]{1,0:T(8,128)S(1)} %collective-permute-done.14, f32[128,512]{1,0:T(8,128)S(1)} %collective-permute-done.13, f32[128,512]{1,0:T(8,128)S(1)} %collective-permute-done.10, f32[128,512]{1,0:T(8,128)S(1)} %collective-permute-done.9, f32[128,512]{1,0:T(8,128)S(1)} %get-tuple-element.32, ...), kind=kLoop, calls=%fused_computation | loop fusion | flops 327680 | bytes 1835008 | tf_op jit(solution)/shard_map/add | solution.py:208
Async XLA Ops:
  0.0 14.0 %collective-permute-start = (f32[128,512]{1,0:T(8,128)}, f32[128,512]{1,0:T(8,128)S(1)}, u32[]{:S(2)}, u32[]{:S(2)}) collective-permute-start(f32[128,512]{1,0:T(8,128)} %b0.1), channel_id=1, source_target_pairs={{0,256},{4,260},{8,264},{12,268},{16,272},{20,276},{24,280},{28,28... | collective-permute-start | bytes 786440 | tf_op jit(solution)/shard_map/ppermute | solution.py:186
  4.6 11.2 %collective-permute-start.3 = (f32[128,512]{1,0:T(8,128)}, f32[128,512]{1,0:T(8,128)S(1)}, u32[]{:S(2)}, u32[]{:S(2)}) collective-permute-start(f32[128,512]{1,0:T(8,128)} %b0.1), channel_id=1, source_target_pairs={{0,64},{64,0},{128,192},{192,128},{256,320},{320,256},{384,448},{4... | collective-permute-start | bytes 786440 | tf_op jit(solution)/shard_map/ppermute | solution.py:183
  8.7 13.2 %collective-permute-start.2 = (f32[128,512]{1,0:T(8,128)}, f32[128,512]{1,0:T(8,128)S(1)}, u32[]{:S(2)}, u32[]{:S(2)}) collective-permute-start(f32[128,512]{1,0:T(8,128)} %b0.1), channel_id=1, source_target_pairs={{0,128},{4,388},{8,136},{12,396},{16,144},{20,404},{24,152},{28,41... | collective-permute-start | bytes 786440 | tf_op jit(solution)/shard_map/ppermute | solution.py:186
  11.4 10.4 %collective-permute-start.1 = (f32[128,512]{1,0:T(8,128)}, f32[128,512]{1,0:T(8,128)S(1)}, u32[]{:S(2)}, u32[]{:S(2)}) collective-permute-start(f32[128,512]{1,0:T(8,128)} %b0.1), channel_id=1, source_target_pairs={{0,384},{4,132},{8,392},{12,140},{16,400},{20,148},{24,408},{28,15... | collective-permute-start | bytes 786440 | tf_op jit(solution)/shard_map/ppermute | solution.py:186
  14.0 13.0 %collective-permute-start.4 = (f32[128,512]{1,0:T(8,128)S(1)}, f32[128,512]{1,0:T(8,128)S(1)}, u32[]{:S(2)}, u32[]{:S(2)}) collective-permute-start(f32[128,512]{1,0:T(8,128)S(1)} %collective-permute-done.b1), channel_id=1, source_target_pairs={{0,64},{64,0},{128,192},{192,128},{256,320},{320,256},{384,448},{4... | collective-permute-start | bytes 786440 | tf_op jit(solution)/shard_map/ppermute | solution.py:183
  15.9 11.0 %collective-permute-start.6 = (f32[128,512]{1,0:T(8,128)S(1)}, f32[128,512]{1,0:T(8,128)S(1)}, u32[]{:S(2)}, u32[]{:S(2)}) collective-permute-start(f32[128,512]{1,0:T(8,128)S(1)} %collective-permute-done.3.b0), channel_id=1, source_target_pairs={{0,128},{4,388},{8,136},{12,396},{16,144},{20,404},{24,152},{28,41... | collective-permute-start | bytes 786440 | tf_op jit(solution)/shard_map/ppermute | solution.py:186
  19.9 10.6 %collective-permute-start.5 = (f32[128,512]{1,0:T(8,128)S(1)}, f32[128,512]{1,0:T(8,128)S(1)}, u32[]{:S(2)}, u32[]{:S(2)}) collective-permute-start(f32[128,512]{1,0:T(8,128)S(1)} %collective-permute-done.3.b0), channel_id=1, source_target_pairs={{0,384},{4,132},{8,392},{12,140},{16,400},{20,148},{24,408},{28,15... | collective-permute-start | bytes 786440 | tf_op jit(solution)/shard_map/ppermute | solution.py:186
  21.8 1.0 %copy-start = (f32[128,512]{1,0:T(8,128)S(1)}, f32[128,512]{1,0:T(8,128)}, u32[]{:S(2)}) copy-start(f32[128,512]{1,0:T(8,128)} %b0.1) | copy-start | bytes 786436
  32.5 6.0 %collective-permute-start.8 = (f32[896,512]{1,0:T(8,128)S(1)}, f32[896,512]{1,0:T(8,128)S(1)}, u32[]{:S(2)}, u32[]{:S(2)}) collective-permute-start(f32[896,512]{1,0:T(8,128)S(1)} %get-tuple-element.34), channel_id=1, source_target_pairs={{0,4},{4,0},{8,12},{12,8},{16,20},{20,16},{24,28},{28,24},{32,36},... | collective-permute-start | bytes 5505032 | tf_op jit(solution)/shard_map/ppermute | solution.py:198
  38.7 18.0 %collective-permute-start.11 = (f32[256,512]{1,0:T(8,128)S(1)}, f32[256,512]{1,0:T(8,128)S(1)}, u32[]{:S(2)}, u32[]{:S(2)}) collective-permute-start(f32[256,512]{1,0:T(8,128)S(1)} %get-tuple-element.39), channel_id=1, source_target_pairs={{0,8},{4,60},{8,16},{12,4},{16,24},{20,12},{24,32},{28,20},{32,40}... | collective-permute-start | bytes 1572872 | tf_op jit(solution)/shard_map/ppermute | solution.py:199
  43.8 12.9 %collective-permute-start.12 = (f32[128,512]{1,0:T(8,128)S(1)}, f32[128,512]{1,0:T(8,128)S(1)}, u32[]{:S(2)}, u32[]{:S(2)}) collective-permute-start(f32[128,512]{1,0:T(8,128)S(1)} %get-tuple-element.40), channel_id=1, source_target_pairs={{0,16},{4,52},{8,24},{12,60},{16,32},{20,4},{24,40},{28,12},{32,48... | collective-permute-start | bytes 786440 | tf_op jit(solution)/shard_map/ppermute | solution.py:200
  47.6 16.7 %collective-permute-start.7 = (f32[128,512]{1,0:T(8,128)S(1)}, f32[128,512]{1,0:T(8,128)S(1)}, u32[]{:S(2)}, u32[]{:S(2)}) collective-permute-start(f32[128,512]{1,0:T(8,128)S(1)} %get-tuple-element.33), channel_id=1, source_target_pairs={{0,4},{4,0},{8,12},{12,8},{16,20},{20,16},{24,28},{28,24},{32,36},... | collective-permute-start | bytes 786440 | tf_op jit(solution)/shard_map/ppermute | solution.py:207
  49.5 14.8 %collective-permute-start.9 = (f32[128,512]{1,0:T(8,128)S(1)}, f32[128,512]{1,0:T(8,128)S(1)}, u32[]{:S(2)}, u32[]{:S(2)}) collective-permute-start(f32[128,512]{1,0:T(8,128)S(1)} %get-tuple-element.36), channel_id=1, source_target_pairs={{0,8},{4,60},{8,16},{12,4},{16,24},{20,12},{24,32},{28,20},{32,40}... | collective-permute-start | bytes 786440 | tf_op jit(solution)/shard_map/ppermute | solution.py:201
  52.5 11.8 %collective-permute-start.10 = (f32[128,512]{1,0:T(8,128)S(1)}, f32[128,512]{1,0:T(8,128)S(1)}, u32[]{:S(2)}, u32[]{:S(2)}) collective-permute-start(f32[128,512]{1,0:T(8,128)S(1)} %get-tuple-element.37), channel_id=1, source_target_pairs={{0,12},{4,56},{8,20},{12,0},{16,28},{20,8},{24,36},{28,16},{32,44}... | collective-permute-start | bytes 786440 | tf_op jit(solution)/shard_map/ppermute | solution.py:202
  56.8 12.5 %collective-permute-start.13 = (f32[128,512]{1,0:T(8,128)S(1)}, f32[128,512]{1,0:T(8,128)S(1)}, u32[]{:S(2)}, u32[]{:S(2)}) collective-permute-start(f32[128,512]{1,0:T(8,128)S(1)} %get-tuple-element.41), channel_id=1, source_target_pairs={{0,16},{4,52},{8,24},{12,60},{16,32},{20,4},{24,40},{28,12},{32,48... | collective-permute-start | bytes 786440 | tf_op jit(solution)/shard_map/ppermute | solution.py:205
  61.6 15.3 %collective-permute-start.14 = (f32[128,512]{1,0:T(8,128)S(1)}, f32[128,512]{1,0:T(8,128)S(1)}, u32[]{:S(2)}, u32[]{:S(2)}) collective-permute-start(f32[128,512]{1,0:T(8,128)S(1)} %get-tuple-element.42), channel_id=1, source_target_pairs={{0,20},{4,48},{8,28},{12,56},{16,36},{20,0},{24,44},{28,8},{32,52}... | collective-permute-start | bytes 786440 | tf_op jit(solution)/shard_map/ppermute | solution.py:206

commit v7 on v5

--- a/solution.py
+++ b/solution.py
@@ -109,16 +109,16 @@
     )(*args)
 
 
-def add_kernel(first, second, three, four, one_own, one_other, two, zero):
+def add_kernel(first, second, *outs):
     _, core, _, _ = place()
-    own, other = (pl.multiple_of(256 + side * 128, 128) for side in (core, 1 - core))
-    for start, out in ((0, three), (own, one_own), (other, one_other), (512, two), (768, four), (896, zero)):
-        rows = pl.ds(start, out.shape[0])
+    starts = [pl.multiple_of(256 * block + side * 128, 128) for block in range(3) for side in (core, 1 - core)]
+    for start, out in zip(starts + [768, 896], outs):
+        rows = pl.ds(start, 128)
         out[...] = first[rows, :] + second[rows, :]
 
 
 def add(first, second):
-    counts = (256, 128, 128, 128, 256, 128)
+    counts = (128,) * 8
     return pl.pallas_call(
         add_kernel,
         in_specs=[VMEM] * 2,
@@ -127,25 +127,6 @@
         compiler_params=pltpu.CompilerParams(vmem_limit_bytes=8 * MIB),
         cost_estimate=pl.CostEstimate(flops=MIB, bytes_accessed=4 * MIB, transcendentals=0),
     )(first, second)
-
-
-def pass_on_kernel(two, got_three, got_four, own, other):
-    _, core, _, _ = place()
-    for index, out in ((core, own), (1 - core, other)):
-        rows = pl.ds(pl.multiple_of(index * 128, 128), 128)
-        total = two[rows, :] + got_three[rows, :]
-        out[...] = total + got_four[...] if out is own else total
-
-
-def halves(kernel, *args):
-    return pl.pallas_call(
-        kernel,
-        in_specs=[VMEM] * len(args),
-        out_specs=[VMEM] * 2,
-        out_shape=[jax.ShapeDtypeStruct((128, 512), F32)] * 2,
-        compiler_params=pltpu.CompilerParams(vmem_limit_bytes=4 * MIB),
-        cost_estimate=pl.CostEstimate(flops=MIB, bytes_accessed=2 * MIB, transcendentals=0),
-    )(*args)
 
 
 def along_y(distance, cross=0):
@@ -185,16 +166,17 @@
     given, far_high, far_low = product(late_kernel, [sums] + b_parts, False, 14, first, a_high, a_low, *far_b)
     kept = product(whole_kernel, [sums], False, 14, a_kept, near_high, near_low, far_high, far_low)[0]
 
-    three, four, one_own, one_other, two, zero = add(lax.ppermute(given, "ka", CORES), kept)
-    got_three = lax.ppermute(three, "ka", along_y(1))
+    three_own, three_other, one_own, one_other, two_own, two_other, four, zero = add(
+        lax.ppermute(given, "ka", CORES), kept
+    )
+    got_three_other = lax.ppermute(three_other, "ka", along_y(1))
     got_four = lax.ppermute(four, "ka", along_y(2))
+    got_three_own = lax.ppermute(three_own, "ka", along_y(1))
+    got_two_other = lax.ppermute(two_other + got_three_other, "ka", along_y(1))
     near_own = lax.ppermute(one_own, "ka", along_y(1))
-    near_other = lax.ppermute(one_other, "ka", along_y(1, 1))
-
-    own, other = halves(pass_on_kernel, two, got_three, got_four)
-    far_own = lax.ppermute(own, "ka", along_y(2))
-    far_other = lax.ppermute(other, "ka", along_y(2, 1))
-    return zero + near_own + near_other + far_own + far_other
+    far_own = lax.ppermute(two_own + got_three_own + got_four, "ka", along_y(2))
+    far_other = lax.ppermute(one_other + got_two_other, "ka", along_y(1, 1))
+    return zero + near_own + far_own + far_other
 
 
 def solution(mesh):

time: 78.6 us -> 76.6 us (0.975)
  the two profiles are of different devices: /device:TPU:129 before, /device:TPU:1 now
where the time goes in v7:
time: 76.6 us; the launch traced here: 76 us
  starting transfers between devices  50.2 us (66%)
  waiting for transfers between devices  14 us (18%)
  Pallas kernels  9.77 us (13%)
  local copies, waits for them, and re-layouts  0.94 us (1%)
  other arithmetic  0.92 us (1%)
    ppermute x5, starting transfers between devices, from_row(): return [lax.ppermute(b, ('ma', 'ka'), by_x(offset)) for offset in offsets]  16.6 us
    pallas_call x3, Pallas kernels, product(): pl.pallas_call(kernel, in_specs=[pl.BlockSpec(memory_space=pl.ANY) if rea...  9.56 us
    ppermute x2, starting transfers between devices, other_half(): return lax.ppermute(b, 'ma', HALVES)  5.92 us
    ppermute x1, starting transfers between devices, shards(): lax.ppermute(given, 'ka', CORES)  5.25 us
    ppermute x1, waiting for transfers between devices, shards(): far_other = lax.ppermute(one_other + got_two_other, 'ka', along_y(1, 1))  4.91 us
    ppermute x1, starting transfers between devices, shards(): far_own = lax.ppermute(two_own + got_three_own + got_four, 'ka', along_y(2))  4.76 us
    ppermute x1, starting transfers between devices, shards(): got_four = lax.ppermute(four, 'ka', along_y(2))  3.79 us
    ppermute x1, starting transfers between devices, shards(): far_other = lax.ppermute(one_other + got_two_other, 'ka', along_y(1, 1))  3.58 us
  transfers between devices with their start and end apart: 15, of which 5 were waited for; matrix products, arithmetic and copies ran while one was open for 0% of the time, Pallas kernels for 10%

profile of v7, /device:TPU:1, one launch (start us, length us, event | category | flops | bytes accessed | tf_op | source)
XLA Modules:
  0.0 76.0 jit_solution(14427172448272044926)
XLA Ops:
  0.0 5.5 %collective-permute-start = (f32[128,512]{1,0:T(8,128)}, f32[128,512]{1,0:T(8,128)S(1)}, u32[]{:S(2)}, u32[]{:S(2)}) collective-permute-start(f32[128,512]{1,0:T(8,128)} %b0.1), channel_id=1, source_target_pairs={{0,256},{4,260},{8,264},{12,268},{16,272},{20,276},{24,280},{28,28... | collective-permute-start | bytes 786440 | tf_op jit(solution)/shard_map/ppermute | solution.py:158
  5.5 4.0 %collective-permute-start.3 = (f32[128,512]{1,0:T(8,128)}, f32[128,512]{1,0:T(8,128)S(1)}, u32[]{:S(2)}, u32[]{:S(2)}) collective-permute-start(f32[128,512]{1,0:T(8,128)} %b0.1), channel_id=1, source_target_pairs={{0,64},{64,0},{128,192},{192,128},{256,320},{320,256},{384,448},{4... | collective-permute-start | bytes 786440 | tf_op jit(solution)/shard_map/ppermute | solution.py:155
  9.5 2.8 %collective-permute-start.2 = (f32[128,512]{1,0:T(8,128)}, f32[128,512]{1,0:T(8,128)S(1)}, u32[]{:S(2)}, u32[]{:S(2)}) collective-permute-start(f32[128,512]{1,0:T(8,128)} %b0.1), channel_id=1, source_target_pairs={{0,128},{4,388},{8,136},{12,396},{16,144},{20,404},{24,152},{28,41... | collective-permute-start | bytes 786440 | tf_op jit(solution)/shard_map/ppermute | solution.py:158
  12.3 2.5 %collective-permute-start.1 = (f32[128,512]{1,0:T(8,128)}, f32[128,512]{1,0:T(8,128)S(1)}, u32[]{:S(2)}, u32[]{:S(2)}) collective-permute-start(f32[128,512]{1,0:T(8,128)} %b0.1), channel_id=1, source_target_pairs={{0,384},{4,132},{8,392},{12,140},{16,400},{20,148},{24,408},{28,15... | collective-permute-start | bytes 786440 | tf_op jit(solution)/shard_map/ppermute | solution.py:158
  14.8 0.0 collective-permute-done.b1
  14.8 1.9 %collective-permute-start.4 = (f32[128,512]{1,0:T(8,128)S(1)}, f32[128,512]{1,0:T(8,128)S(1)}, u32[]{:S(2)}, u32[]{:S(2)}) collective-permute-start(f32[128,512]{1,0:T(8,128)S(1)} %collective-permute-done.b1), channel_id=1, source_target_pairs={{0,64},{64,0},{128,192},{192,128},{256,320},{320,256},{384,448},{4... | collective-permute-start | bytes 786440 | tf_op jit(solution)/shard_map/ppermute | solution.py:155
  16.7 0.0 collective-permute-done.3.b0
  16.7 4.0 %collective-permute-start.6 = (f32[128,512]{1,0:T(8,128)S(1)}, f32[128,512]{1,0:T(8,128)S(1)}, u32[]{:S(2)}, u32[]{:S(2)}) collective-permute-start(f32[128,512]{1,0:T(8,128)S(1)} %collective-permute-done.3.b0), channel_id=1, source_target_pairs={{0,128},{4,388},{8,136},{12,396},{16,144},{20,404},{24,152},{28,41... | collective-permute-start | bytes 786440 | tf_op jit(solution)/shard_map/ppermute | solution.py:158
  20.7 1.9 %collective-permute-start.5 = (f32[128,512]{1,0:T(8,128)S(1)}, f32[128,512]{1,0:T(8,128)S(1)}, u32[]{:S(2)}, u32[]{:S(2)}) collective-permute-start(f32[128,512]{1,0:T(8,128)S(1)} %collective-permute-done.3.b0), channel_id=1, source_target_pairs={{0,384},{4,132},{8,392},{12,140},{16,400},{20,148},{24,408},{28,15... | collective-permute-start | bytes 786440 | tf_op jit(solution)/shard_map/ppermute | solution.py:158
  22.6 0.0 collective-permute-done.2.b3
  22.7 0.0 collective-permute-done.1.b2
  22.7 0.0 copy-start
  22.7 0.9 %copy-done = f32[128,512]{1,0:T(8,128)S(1)} copy-done((f32[128,512]{1,0:T(8,128)S(1)}, f32[128,512]{1,0:T(8,128)}, u32[]{:S(2)}) %copy-start) | copy-done | bytes 262168
  23.6 4.1 %shard_map.28 = (f32[1024,512]{1,0:T(8,128)S(1)}, bf16[1024,512]{1,0:T(8,128)(2,1)S(1)}, bf16[1024,512]{1,0:T(8,128)(2,1)S(1)}, bf16[512,512]{1,0:T(8,128)(2,1)S...) custom-call(f32[2048,1024]{1,0:T(8,128)} %a_hbm.1, f32[128,512]{1,0:T(8,128)S(1)} %copy-done, ...), custom_call_target="tpu_custom_call" | custom-call | flops 1610612736 | bytes 8388608 | tf_op jit(solution)/shard_map/pallas_call | solution.py:101
  27.8 0.0 collective-permute-done.4.b1
  27.8 0.0 collective-permute-done.6.b3
  27.8 2.8 %collective-permute-done.5.b2 = f32[128,512]{1,0:T(8,128)S(1)} collective-permute-done((f32[128,512]{1,0:T(8,128)S(1)}, f32[128,512]{1,0:T(8,128)S(1)}, u32[]{:S(2)}, u32[]{:S(2)}) %collective-permute-start.5) | collective-permute-done | bytes 262176 | tf_op jit(solution)/shard_map/ppermute | solution.py:158
  30.6 2.0 %shard_map.29 = (f32[1024,512]{1,0:T(8,128)S(1)}, bf16[512,512]{1,0:T(8,128)(2,1)S(1)}, bf16[512,512]{1,0:T(8,128)(2,1)S(1)}) custom-call(f32[1024,512]{1,0:T(8,128)S(1)} %get-tuple-element.22.sums, bf16[1024,512]{1,0:T(8,128)(2,1)S(1)} %get-tuple-element.23.a_high, bf16[1024,512]{1,0:T(8,128)(2,1)S(1)} %get-tuple-element.24.a_low, ...), custom_call_target="tpu_custom_call" | custom-call | flops 1610612736 | bytes 8388608 | tf_op jit(solution)/shard_map/pallas_call | solution.py:101
  32.6 5.3 %collective-permute-start.7 = (f32[1024,512]{1,0:T(8,128)S(1)}, f32[1024,512]{1,0:T(8,128)S(1)}, u32[]{:S(2)}, u32[]{:S(2)}) collective-permute-start(f32[1024,512]{1,0:T(8,128)S(1)} %get-tuple-element.25), channel_id=1, source_target_pairs={{0,4},{4,0},{8,12},{12,8},{16,20},{20,16},{24,28},{28,24},{32,36},... | collective-permute-start | bytes 6291464 | tf_op jit(solution)/shard_map/ppermute | solution.py:170
  37.9 3.4 %shard_map.30.second = f32[1024,512]{1,0:T(8,128)S(1)} custom-call(f32[1024,1024]{1,0:T(8,128)S(1)} %get-tuple-element.26.a_ref, bf16[512,512]{1,0:T(8,128)(2,1)S(1)} %get-tuple-element.27.near_high, bf16[512,512]{1,0:T(8,128)(2,1)S(1)} %get-tuple-element.28.near_low, bf16[512,512]{1,0:T(8,128)(2,1)S(1)} %get-tuple-element.29.far_high, ...), custom_call_target="tpu_custom_call" | custom-call | flops 1610612736 | bytes 8388608 | tf_op jit(solution)/shard_map/pallas_call | solution.py:101
  41.3 0.3 collective-permute-done.7.first
  41.6 0.2 shard_map.31
  41.8 3.1 %collective-permute-start.12 = (f32[128,512]{1,0:T(8,128)S(1)}, f32[128,512]{1,0:T(8,128)S(1)}, u32[]{:S(2)}, u32[]{:S(2)}) collective-permute-start(f32[128,512]{1,0:T(8,128)S(1)} %get-tuple-element.38), channel_id=1, source_target_pairs={{0,8},{4,60},{8,16},{12,4},{16,24},{20,12},{24,32},{28,20},{32,40}... | collective-permute-start | bytes 786440 | tf_op jit(solution)/shard_map/ppermute | solution.py:172
  44.9 3.0 %collective-permute-start.9 = (f32[128,512]{1,0:T(8,128)S(1)}, f32[128,512]{1,0:T(8,128)S(1)}, u32[]{:S(2)}, u32[]{:S(2)}) collective-permute-start(f32[128,512]{1,0:T(8,128)S(1)} %get-tuple-element.34), channel_id=1, source_target_pairs={{0,8},{4,60},{8,16},{12,4},{16,24},{20,12},{24,32},{28,20},{32,40}... | collective-permute-start | bytes 786440 | tf_op jit(solution)/shard_map/ppermute | solution.py:174
  47.9 3.8 %collective-permute-start.10 = (f32[128,512]{1,0:T(8,128)S(1)}, f32[128,512]{1,0:T(8,128)S(1)}, u32[]{:S(2)}, u32[]{:S(2)}) collective-permute-start(f32[128,512]{1,0:T(8,128)S(1)} %get-tuple-element.35), channel_id=1, source_target_pairs={{0,16},{4,52},{8,24},{12,60},{16,32},{20,4},{24,40},{28,12},{32,48... | collective-permute-start | bytes 786440 | tf_op jit(solution)/shard_map/ppermute | solution.py:173
  51.7 0.0 collective-permute-done.12
  51.8 2.1 %collective-permute-start.13 = (f32[128,512]{1,0:T(8,128)S(1)}, f32[128,512]{1,0:T(8,128)S(1)}, u32[]{:S(2)}, u32[]{:S(2)}) collective-permute-start(f32[128,512]{1,0:T(8,128)S(1)} %add.25), channel_id=1, source_target_pairs={{0,8},{4,60},{8,16},{12,4},{16,24},{20,12},{24,32},{28,20},{32,40}... | collective-permute-start | bytes 786440 | tf_op jit(solution)/shard_map/ppermute | solution.py:175
  53.8 2.1 %collective-permute-start.8 = (f32[128,512]{1,0:T(8,128)S(1)}, f32[128,512]{1,0:T(8,128)S(1)}, u32[]{:S(2)}, u32[]{:S(2)}) collective-permute-start(f32[128,512]{1,0:T(8,128)S(1)} %get-tuple-element.32), channel_id=1, source_target_pairs={{0,8},{4,60},{8,16},{12,4},{16,24},{20,12},{24,32},{28,20},{32,40}... | collective-permute-start | bytes 786440 | tf_op jit(solution)/shard_map/ppermute | solution.py:176
  55.9 0.0 collective-permute-done.9
  55.9 3.2 %collective-permute-done.10 = f32[128,512]{1,0:T(8,128)S(1)} collective-permute-done((f32[128,512]{1,0:T(8,128)S(1)}, f32[128,512]{1,0:T(8,128)S(1)}, u32[]{:S(2)}, u32[]{:S(2)}) %collective-permute-start.10) | collective-permute-done | bytes 262176 | tf_op jit(solution)/shard_map/ppermute | solution.py:173
  59.1 0.1 add_add_fusion.1
  59.2 4.8 %collective-permute-start.11 = (f32[128,512]{1,0:T(8,128)S(1)}, f32[128,512]{1,0:T(8,128)S(1)}, u32[]{:S(2)}, u32[]{:S(2)}) collective-permute-start(f32[128,512]{1,0:T(8,128)S(1)} %add_add_fusion.1), channel_id=1, source_target_pairs={{0,16},{4,52},{8,24},{12,60},{16,32},{20,4},{24,40},{28,12},{32,48... | collective-permute-start | bytes 786440 | tf_op jit(solution)/shard_map/ppermute | solution.py:177
  63.9 0.0 collective-permute-done.13
  64.0 3.6 %collective-permute-start.14 = (f32[128,512]{1,0:T(8,128)S(1)}, f32[128,512]{1,0:T(8,128)S(1)}, u32[]{:S(2)}, u32[]{:S(2)}) collective-permute-start(f32[128,512]{1,0:T(8,128)S(1)} %add.26), channel_id=1, source_target_pairs={{0,12},{4,56},{8,20},{12,0},{16,28},{20,8},{24,36},{28,16},{32,44}... | collective-permute-start | bytes 786440 | tf_op jit(solution)/shard_map/ppermute | solution.py:178
  67.6 0.0 collective-permute-done.8
  67.6 2.8 %collective-permute-done.11 = f32[128,512]{1,0:T(8,128)S(1)} collective-permute-done((f32[128,512]{1,0:T(8,128)S(1)}, f32[128,512]{1,0:T(8,128)S(1)}, u32[]{:S(2)}, u32[]{:S(2)}) %collective-permute-start.11) | collective-permute-done | bytes 262176 | tf_op jit(solution)/shard_map/ppermute | solution.py:177
  70.3 4.9 %collective-permute-done.14 = f32[128,512]{1,0:T(8,128)S(1)} collective-permute-done((f32[128,512]{1,0:T(8,128)S(1)}, f32[128,512]{1,0:T(8,128)S(1)}, u32[]{:S(2)}, u32[]{:S(2)}) %collective-permute-start.14) | collective-permute-done | bytes 262176 | tf_op jit(solution)/shard_map/ppermute | solution.py:178
  75.2 0.8 %add_add_fusion = f32[128,512]{1,0:T(8,128)} fusion(f32[128,512]{1,0:T(8,128)S(1)} %collective-permute-done.14, f32[128,512]{1,0:T(8,128)S(1)} %collective-permute-done.11, f32[128,512]{1,0:T(8,128)S(1)} %get-tuple-element.31, f32[128,512]{1,0:T(8,128)S(1)} %collective-permute-done.8), kind=kLoop, calls=%fused_computation | loop fusion | flops 196608 | bytes 1310720 | tf_op jit(solution)/shard_map/add | solution.py:179
  (2 shorter events, 0.1 us)
Async XLA Ops:
  0.0 14.8 %collective-permute-start = (f32[128,512]{1,0:T(8,128)}, f32[128,512]{1,0:T(8,128)S(1)}, u32[]{:S(2)}, u32[]{:S(2)}) collective-permute-start(f32[128,512]{1,0:T(8,128)} %b0.1), channel_id=1, source_target_pairs={{0,256},{4,260},{8,264},{12,268},{16,272},{20,276},{24,280},{28,28... | collective-permute-start | bytes 786440 | tf_op jit(solution)/shard_map/ppermute | solution.py:158
  5.5 11.2 %collective-permute-start.3 = (f32[128,512]{1,0:T(8,128)}, f32[128,512]{1,0:T(8,128)S(1)}, u32[]{:S(2)}, u32[]{:S(2)}) collective-permute-start(f32[128,512]{1,0:T(8,128)} %b0.1), channel_id=1, source_target_pairs={{0,64},{64,0},{128,192},{192,128},{256,320},{320,256},{384,448},{4... | collective-permute-start | bytes 786440 | tf_op jit(solution)/shard_map/ppermute | solution.py:155
  9.5 13.2 %collective-permute-start.2 = (f32[128,512]{1,0:T(8,128)}, f32[128,512]{1,0:T(8,128)S(1)}, u32[]{:S(2)}, u32[]{:S(2)}) collective-permute-start(f32[128,512]{1,0:T(8,128)} %b0.1), channel_id=1, source_target_pairs={{0,128},{4,388},{8,136},{12,396},{16,144},{20,404},{24,152},{28,41... | collective-permute-start | bytes 786440 | tf_op jit(solution)/shard_map/ppermute | solution.py:158
  12.3 10.4 %collective-permute-start.1 = (f32[128,512]{1,0:T(8,128)}, f32[128,512]{1,0:T(8,128)S(1)}, u32[]{:S(2)}, u32[]{:S(2)}) collective-permute-start(f32[128,512]{1,0:T(8,128)} %b0.1), channel_id=1, source_target_pairs={{0,384},{4,132},{8,392},{12,140},{16,400},{20,148},{24,408},{28,15... | collective-permute-start | bytes 786440 | tf_op jit(solution)/shard_map/ppermute | solution.py:158
  14.8 13.0 %collective-permute-start.4 = (f32[128,512]{1,0:T(8,128)S(1)}, f32[128,512]{1,0:T(8,128)S(1)}, u32[]{:S(2)}, u32[]{:S(2)}) collective-permute-start(f32[128,512]{1,0:T(8,128)S(1)} %collective-permute-done.b1), channel_id=1, source_target_pairs={{0,64},{64,0},{128,192},{192,128},{256,320},{320,256},{384,448},{4... | collective-permute-start | bytes 786440 | tf_op jit(solution)/shard_map/ppermute | solution.py:155
  16.7 11.0 %collective-permute-start.6 = (f32[128,512]{1,0:T(8,128)S(1)}, f32[128,512]{1,0:T(8,128)S(1)}, u32[]{:S(2)}, u32[]{:S(2)}) collective-permute-start(f32[128,512]{1,0:T(8,128)S(1)} %collective-permute-done.3.b0), channel_id=1, source_target_pairs={{0,128},{4,388},{8,136},{12,396},{16,144},{20,404},{24,152},{28,41... | collective-permute-start | bytes 786440 | tf_op jit(solution)/shard_map/ppermute | solution.py:158
  20.7 9.9 %collective-permute-start.5 = (f32[128,512]{1,0:T(8,128)S(1)}, f32[128,512]{1,0:T(8,128)S(1)}, u32[]{:S(2)}, u32[]{:S(2)}) collective-permute-start(f32[128,512]{1,0:T(8,128)S(1)} %collective-permute-done.3.b0), channel_id=1, source_target_pairs={{0,384},{4,132},{8,392},{12,140},{16,400},{20,148},{24,408},{28,15... | collective-permute-start | bytes 786440 | tf_op jit(solution)/shard_map/ppermute | solution.py:158
  22.7 1.0 %copy-start = (f32[128,512]{1,0:T(8,128)S(1)}, f32[128,512]{1,0:T(8,128)}, u32[]{:S(2)}) copy-start(f32[128,512]{1,0:T(8,128)} %b0.1) | copy-start | bytes 786436
  32.6 9.0 %collective-permute-start.7 = (f32[1024,512]{1,0:T(8,128)S(1)}, f32[1024,512]{1,0:T(8,128)S(1)}, u32[]{:S(2)}, u32[]{:S(2)}) collective-permute-start(f32[1024,512]{1,0:T(8,128)S(1)} %get-tuple-element.25), channel_id=1, source_target_pairs={{0,4},{4,0},{8,12},{12,8},{16,20},{20,16},{24,28},{28,24},{32,36},... | collective-permute-start | bytes 6291464 | tf_op jit(solution)/shard_map/ppermute | solution.py:170
  41.8 9.9 %collective-permute-start.12 = (f32[128,512]{1,0:T(8,128)S(1)}, f32[128,512]{1,0:T(8,128)S(1)}, u32[]{:S(2)}, u32[]{:S(2)}) collective-permute-start(f32[128,512]{1,0:T(8,128)S(1)} %get-tuple-element.38), channel_id=1, source_target_pairs={{0,8},{4,60},{8,16},{12,4},{16,24},{20,12},{24,32},{28,20},{32,40}... | collective-permute-start | bytes 786440 | tf_op jit(solution)/shard_map/ppermute | solution.py:172
  44.9 11.0 %collective-permute-start.9 = (f32[128,512]{1,0:T(8,128)S(1)}, f32[128,512]{1,0:T(8,128)S(1)}, u32[]{:S(2)}, u32[]{:S(2)}) collective-permute-start(f32[128,512]{1,0:T(8,128)S(1)} %get-tuple-element.34), channel_id=1, source_target_pairs={{0,8},{4,60},{8,16},{12,4},{16,24},{20,12},{24,32},{28,20},{32,40}... | collective-permute-start | bytes 786440 | tf_op jit(solution)/shard_map/ppermute | solution.py:174
  47.9 11.2 %collective-permute-start.10 = (f32[128,512]{1,0:T(8,128)S(1)}, f32[128,512]{1,0:T(8,128)S(1)}, u32[]{:S(2)}, u32[]{:S(2)}) collective-permute-start(f32[128,512]{1,0:T(8,128)S(1)} %get-tuple-element.35), channel_id=1, source_target_pairs={{0,16},{4,52},{8,24},{12,60},{16,32},{20,4},{24,40},{28,12},{32,48... | collective-permute-start | bytes 786440 | tf_op jit(solution)/shard_map/ppermute | solution.py:173
  51.8 12.1 %collective-permute-start.13 = (f32[128,512]{1,0:T(8,128)S(1)}, f32[128,512]{1,0:T(8,128)S(1)}, u32[]{:S(2)}, u32[]{:S(2)}) collective-permute-start(f32[128,512]{1,0:T(8,128)S(1)} %add.25), channel_id=1, source_target_pairs={{0,8},{4,60},{8,16},{12,4},{16,24},{20,12},{24,32},{28,20},{32,40}... | collective-permute-start | bytes 786440 | tf_op jit(solution)/shard_map/ppermute | solution.py:175
  53.8 13.7 %collective-permute-start.8 = (f32[128,512]{1,0:T(8,128)S(1)}, f32[128,512]{1,0:T(8,128)S(1)}, u32[]{:S(2)}, u32[]{:S(2)}) collective-permute-start(f32[128,512]{1,0:T(8,128)S(1)} %get-tuple-element.32), channel_id=1, source_target_pairs={{0,8},{4,60},{8,16},{12,4},{16,24},{20,12},{24,32},{28,20},{32,40}... | collective-permute-start | bytes 786440 | tf_op jit(solution)/shard_map/ppermute | solution.py:176
  59.2 11.2 %collective-permute-start.11 = (f32[128,512]{1,0:T(8,128)S(1)}, f32[128,512]{1,0:T(8,128)S(1)}, u32[]{:S(2)}, u32[]{:S(2)}) collective-permute-start(f32[128,512]{1,0:T(8,128)S(1)} %add_add_fusion.1), channel_id=1, source_target_pairs={{0,16},{4,52},{8,24},{12,60},{16,32},{20,4},{24,40},{28,12},{32,48... | collective-permute-start | bytes 786440 | tf_op jit(solution)/shard_map/ppermute | solution.py:177
  64.0 11.3 %collective-permute-start.14 = (f32[128,512]{1,0:T(8,128)S(1)}, f32[128,512]{1,0:T(8,128)S(1)}, u32[]{:S(2)}, u32[]{:S(2)}) collective-permute-start(f32[128,512]{1,0:T(8,128)S(1)} %add.26), channel_id=1, source_target_pairs={{0,12},{4,56},{8,20},{12,0},{16,28},{20,8},{24,36},{28,16},{32,44}... | collective-permute-start | bytes 786440 | tf_op jit(solution)/shard_map/ppermute | solution.py:178

commit v8 on v7

--- a/solution.py
+++ b/solution.py
@@ -82,17 +82,26 @@
         copy.wait()
 
 
-def late_kernel(sums, a_high, a_low, b0, b1, b2, b3, out, b_high, b_low):
+def store(rows, value, out, zero_out):
+    if rows.stop <= 896:
+        out[rows, :] = value
+    else:
+        out[rows.start : 896, :] = value[:128]
+        zero_out[...] = value[128:]
+
+
+def late_kernel(sums, a_high, a_low, b0, b1, b2, b3, out, zero_out, b_high, b_low):
     place_parts((b0, b1, b2, b3), b_high, b_low)
     for step in range(4):
         rows = slice(256 * step, 256 * step + 256)
-        out[rows, :] = sums[rows, :] + three_dots(a_high[rows, :], a_low[rows, :], b_high, b_low)
+        value = sums[rows, :] + three_dots(a_high[rows, :], a_low[rows, :], b_high, b_low)
+        store(rows, value, out, zero_out)
 
 
-def whole_kernel(a_ref, near_high, near_low, far_high, far_low, out):
+def whole_kernel(a_ref, near_high, near_low, far_high, far_low, out, zero_out):
     def body(z, rows):
         near = three_dots(*parts_of(a_ref, rows, z), near_high, near_low)
-        out[rows, :] = near + three_dots(*parts_of(a_ref, rows, 1 - z), far_high, far_low)
+        store(rows, near + three_dots(*parts_of(a_ref, rows, 1 - z), far_high, far_low), out, zero_out)
 
     for_each_tile(body)
 
@@ -112,13 +121,13 @@
 def add_kernel(first, second, *outs):
     _, core, _, _ = place()
     starts = [pl.multiple_of(256 * block + side * 128, 128) for block in range(3) for side in (core, 1 - core)]
-    for start, out in zip(starts + [768, 896], outs):
+    for start, out in zip(starts + [768], outs):
         rows = pl.ds(start, 128)
         out[...] = first[rows, :] + second[rows, :]
 
 
 def add(first, second):
-    counts = (128,) * 8
+    counts = (128,) * 7
     return pl.pallas_call(
         add_kernel,
         in_specs=[VMEM] * 2,
@@ -163,20 +172,22 @@
     sums, parts, b_parts = ((1024, 512), F32), [((1024, 512), BF16)] * 2, [((512, 512), BF16)] * 2
     outs = [sums] + parts + b_parts + [((1024, 1024), F32)]
     first, a_high, a_low, near_high, near_low, a_kept = product(early_kernel, outs, True, 40, left_matrix, *near_b)
-    given, far_high, far_low = product(late_kernel, [sums] + b_parts, False, 14, first, a_high, a_low, *far_b)
-    kept = product(whole_kernel, [sums], False, 14, a_kept, near_high, near_low, far_high, far_low)[0]
+    swapped_sums = [((896, 512), F32), ((128, 512), F32)]
+    given, zero_given, far_high, far_low = product(late_kernel, swapped_sums + b_parts, False, 14, first, a_high, a_low, *far_b)
+    kept, zero = product(whole_kernel, swapped_sums, False, 14, a_kept, near_high, near_low, far_high, far_low)
 
-    three_own, three_other, one_own, one_other, two_own, two_other, four, zero = add(
+    three_own, three_other, one_own, one_other, two_own, two_other, four = add(
         lax.ppermute(given, "ka", CORES), kept
     )
     got_three_other = lax.ppermute(three_other, "ka", along_y(1))
+    got_three_own = lax.ppermute(three_own, "ka", along_y(1))
     got_four = lax.ppermute(four, "ka", along_y(2))
-    got_three_own = lax.ppermute(three_own, "ka", along_y(1))
     got_two_other = lax.ppermute(two_other + got_three_other, "ka", along_y(1))
     near_own = lax.ppermute(one_own, "ka", along_y(1))
     far_own = lax.ppermute(two_own + got_three_own + got_four, "ka", along_y(2))
     far_other = lax.ppermute(one_other + got_two_other, "ka", along_y(1, 1))
-    return zero + near_own + far_own + far_other
+    zero_got = lax.ppermute(zero_given, "ka", CORES)
+    return zero + zero_got + near_own + far_own + far_other
 
 
 def solution(mesh):

time: 76.6 us -> 76.5 us (level)
  waiting for transfers between devices: 14 us -> 10.8 us
  starting transfers between devices: 50.2 us -> 53.2 us
    ppermute x0 -> x1, starting transfers between devices: none -> 3.54 us  [shards(): zero_got = lax.ppermute(zero_given, 'ka', CORES)]
    ppermute x1, waiting for transfers between devices: 3.15 us -> 0.01 us  [shards(): got_four = lax.ppermute(four, 'ka', along_y(2))]
    ppermute x1, starting transfers between devices: 4.76 us -> 2.22 us  [shards(): far_own = lax.ppermute(two_own + got_three_own + got_four, 'ka', along_y(2))]
    ppermute x1, starting transfers between devices: 2.08 us -> 4.21 us  [shards(): near_own = lax.ppermute(one_own, 'ka', along_y(1))]
    ppermute x1, waiting for transfers between devices: 2.76 us -> 4.25 us  [shards(): far_own = lax.ppermute(two_own + got_three_own + got_four, 'ka', along_y(2))]
    ppermute x1, waiting for transfers between devices: 4.91 us -> 3.71 us  [shards(): far_other = lax.ppermute(one_other + got_two_other, 'ka', along_y(1, 1))]
  transfers between devices with their start and end apart: 15 -> 16, of which waited for: 5 -> 3; matrix products, arithmetic and copies ran while one was open for 0% -> 0% of each run, Pallas kernels for 10% -> 10%
where the time goes in v8:
time: 76.5 us; the launch traced here: 75.9 us
  starting transfers between devices  53.2 us (70%)
  waiting for transfers between devices  10.8 us (14%)
  Pallas kernels  9.77 us (13%)
  other arithmetic  0.96 us (1%)
  local copies, waits for them, and re-layouts  0.94 us (1%)
    ppermute x5, starting transfers between devices, from_row(): return [lax.ppermute(b, ('ma', 'ka'), by_x(offset)) for offset in offsets]  16.6 us
    pallas_call x3, Pallas kernels, product(): pl.pallas_call(kernel, in_specs=[pl.BlockSpec(memory_space=pl.ANY) if rea...  9.56 us
    ppermute x2, starting transfers between devices, other_half(): return lax.ppermute(b, 'ma', HALVES)  5.92 us
    ppermute x1, starting transfers between devices, shards(): lax.ppermute(given, 'ka', CORES)  5.25 us
    ppermute x1, waiting for transfers between devices, shards(): far_own = lax.ppermute(two_own + got_three_own + got_four, 'ka', along_y(2))  4.25 us
    ppermute x1, starting transfers between devices, shards(): near_own = lax.ppermute(one_own, 'ka', along_y(1))  4.21 us
    ppermute x1, starting transfers between devices, shards(): got_four = lax.ppermute(four, 'ka', along_y(2))  3.78 us
    ppermute x1, waiting for transfers between devices, shards(): far_other = lax.ppermute(one_other + got_two_other, 'ka', along_y(1, 1))  3.71 us
  transfers between devices with their start and end apart: 16, of which 3 were waited for; matrix products, arithmetic and copies ran while one was open for 0% of the time, Pallas kernels for 10%

profile of v8, /device:TPU:1, one launch (start us, length us, event | category | flops | bytes accessed | tf_op | source)
XLA Modules:
  0.0 75.9 jit_solution(11300474743741476146)
XLA Ops:
  0.0 5.5 %collective-permute-start = (f32[128,512]{1,0:T(8,128)}, f32[128,512]{1,0:T(8,128)S(1)}, u32[]{:S(2)}, u32[]{:S(2)}) collective-permute-start(f32[128,512]{1,0:T(8,128)} %b0.1), channel_id=1, source_target_pairs={{0,256},{4,260},{8,264},{12,268},{16,272},{20,276},{24,280},{28,28... | collective-permute-start | bytes 786440 | tf_op jit(solution)/shard_map/ppermute | solution.py:167
  5.5 4.0 %collective-permute-start.3 = (f32[128,512]{1,0:T(8,128)}, f32[128,512]{1,0:T(8,128)S(1)}, u32[]{:S(2)}, u32[]{:S(2)}) collective-permute-start(f32[128,512]{1,0:T(8,128)} %b0.1), channel_id=1, source_target_pairs={{0,64},{64,0},{128,192},{192,128},{256,320},{320,256},{384,448},{4... | collective-permute-start | bytes 786440 | tf_op jit(solution)/shard_map/ppermute | solution.py:164
  9.5 2.8 %collective-permute-start.2 = (f32[128,512]{1,0:T(8,128)}, f32[128,512]{1,0:T(8,128)S(1)}, u32[]{:S(2)}, u32[]{:S(2)}) collective-permute-start(f32[128,512]{1,0:T(8,128)} %b0.1), channel_id=1, source_target_pairs={{0,128},{4,388},{8,136},{12,396},{16,144},{20,404},{24,152},{28,41... | collective-permute-start | bytes 786440 | tf_op jit(solution)/shard_map/ppermute | solution.py:167
  12.3 2.5 %collective-permute-start.1 = (f32[128,512]{1,0:T(8,128)}, f32[128,512]{1,0:T(8,128)S(1)}, u32[]{:S(2)}, u32[]{:S(2)}) collective-permute-start(f32[128,512]{1,0:T(8,128)} %b0.1), channel_id=1, source_target_pairs={{0,384},{4,132},{8,392},{12,140},{16,400},{20,148},{24,408},{28,15... | collective-permute-start | bytes 786440 | tf_op jit(solution)/shard_map/ppermute | solution.py:167
  14.8 0.0 collective-permute-done.b1
  14.8 1.9 %collective-permute-start.4 = (f32[128,512]{1,0:T(8,128)S(1)}, f32[128,512]{1,0:T(8,128)S(1)}, u32[]{:S(2)}, u32[]{:S(2)}) collective-permute-start(f32[128,512]{1,0:T(8,128)S(1)} %collective-permute-done.b1), channel_id=1, source_target_pairs={{0,64},{64,0},{128,192},{192,128},{256,320},{320,256},{384,448},{4... | collective-permute-start | bytes 786440 | tf_op jit(solution)/shard_map/ppermute | solution.py:164
  16.7 0.0 collective-permute-done.3.b0
  16.7 4.0 %collective-permute-start.6 = (f32[128,512]{1,0:T(8,128)S(1)}, f32[128,512]{1,0:T(8,128)S(1)}, u32[]{:S(2)}, u32[]{:S(2)}) collective-permute-start(f32[128,512]{1,0:T(8,128)S(1)} %collective-permute-done.3.b0), channel_id=1, source_target_pairs={{0,128},{4,388},{8,136},{12,396},{16,144},{20,404},{24,152},{28,41... | collective-permute-start | bytes 786440 | tf_op jit(solution)/shard_map/ppermute | solution.py:167
  20.7 1.9 %collective-permute-start.5 = (f32[128,512]{1,0:T(8,128)S(1)}, f32[128,512]{1,0:T(8,128)S(1)}, u32[]{:S(2)}, u32[]{:S(2)}) collective-permute-start(f32[128,512]{1,0:T(8,128)S(1)} %collective-permute-done.3.b0), channel_id=1, source_target_pairs={{0,384},{4,132},{8,392},{12,140},{16,400},{20,148},{24,408},{28,15... | collective-permute-start | bytes 786440 | tf_op jit(solution)/shard_map/ppermute | solution.py:167
  22.6 0.0 collective-permute-done.2.b3
  22.7 0.0 collective-permute-done.1.b2
  22.7 0.0 copy-start
  22.7 0.9 %copy-done = f32[128,512]{1,0:T(8,128)S(1)} copy-done((f32[128,512]{1,0:T(8,128)S(1)}, f32[128,512]{1,0:T(8,128)}, u32[]{:S(2)}) %copy-start) | copy-done | bytes 262168
  23.6 4.1 %shard_map.28 = (f32[1024,512]{1,0:T(8,128)S(1)}, bf16[1024,512]{1,0:T(8,128)(2,1)S(1)}, bf16[1024,512]{1,0:T(8,128)(2,1)S(1)}, bf16[512,512]{1,0:T(8,128)(2,1)S...) custom-call(f32[2048,1024]{1,0:T(8,128)} %a_hbm.1, f32[128,512]{1,0:T(8,128)S(1)} %copy-done, ...), custom_call_target="tpu_custom_call" | custom-call | flops 1610612736 | bytes 8388608 | tf_op jit(solution)/shard_map/pallas_call | solution.py:110
  27.8 0.0 collective-permute-done.4.b1
  27.8 0.0 collective-permute-done.6.b3
  27.8 2.8 %collective-permute-done.5.b2 = f32[128,512]{1,0:T(8,128)S(1)} collective-permute-done((f32[128,512]{1,0:T(8,128)S(1)}, f32[128,512]{1,0:T(8,128)S(1)}, u32[]{:S(2)}, u32[]{:S(2)}) %collective-permute-start.5) | collective-permute-done | bytes 262176 | tf_op jit(solution)/shard_map/ppermute | solution.py:167
  30.6 2.0 %shard_map.29 = (f32[896,512]{1,0:T(8,128)S(1)}, f32[128,512]{1,0:T(8,128)S(1)}, bf16[512,512]{1,0:T(8,128)(2,1)S(1)}, bf16[512,512]{1,0:T(8,128)(2,1)S(1)}) custom-call(f32[1024,512]{1,0:T(8,128)S(1)} %get-tuple-element.27.sums, bf16[1024,512]{1,0:T(8,128)(2,1)S(1)} %get-tuple-element.28.a_high, bf16[1024,512]{1,0:T(8,128)(2,1)S(1)} %get-tuple-element.29.a_low, ...), custom_call_target="tpu_custom_call" | custom-call | flops 1610612736 | bytes 8388608 | tf_op jit(solution)/shard_map/pallas_call | solution.py:110
  32.6 5.2 %collective-permute-start.8 = (f32[896,512]{1,0:T(8,128)S(1)}, f32[896,512]{1,0:T(8,128)S(1)}, u32[]{:S(2)}, u32[]{:S(2)}) collective-permute-start(f32[896,512]{1,0:T(8,128)S(1)} %get-tuple-element.34), channel_id=1, source_target_pairs={{0,4},{4,0},{8,12},{12,8},{16,20},{20,16},{24,28},{28,24},{32,36},... | collective-permute-start | bytes 5505032 | tf_op jit(solution)/shard_map/ppermute | solution.py:180
  37.9 3.4 %shard_map.30 = (f32[896,512]{1,0:T(8,128)S(1)}, f32[128,512]{1,0:T(8,128)S(1)}) custom-call(f32[1024,1024]{1,0:T(8,128)S(1)} %get-tuple-element.24.a_ref, bf16[512,512]{1,0:T(8,128)(2,1)S(1)} %get-tuple-element.25.near_high, bf16[512,512]{1,0:T(8,128)(2,1)S(1)} %get-tuple-element.26.near_low, bf16[512,512]{1,0:T(8,128)(2,1)S(1)} %get-tuple-element.30.far_high, ...), custom_call_target="tpu_custom_call" | custom-call | flops 1610612736 | bytes 8388608 | tf_op jit(solution)/shard_map/pallas_call | solution.py:110
  41.3 0.0 collective-permute-done.8.first
  41.3 0.2 shard_map.31
  41.5 3.1 %collective-permute-start.13 = (f32[128,512]{1,0:T(8,128)S(1)}, f32[128,512]{1,0:T(8,128)S(1)}, u32[]{:S(2)}, u32[]{:S(2)}) collective-permute-start(f32[128,512]{1,0:T(8,128)S(1)} %get-tuple-element.42), channel_id=1, source_target_pairs={{0,8},{4,60},{8,16},{12,4},{16,24},{20,12},{24,32},{28,20},{32,40}... | collective-permute-start | bytes 786440 | tf_op jit(solution)/shard_map/ppermute | solution.py:182
  44.6 3.0 %collective-permute-start.10 = (f32[128,512]{1,0:T(8,128)S(1)}, f32[128,512]{1,0:T(8,128)S(1)}, u32[]{:S(2)}, u32[]{:S(2)}) collective-permute-start(f32[128,512]{1,0:T(8,128)S(1)} %get-tuple-element.38), channel_id=1, source_target_pairs={{0,8},{4,60},{8,16},{12,4},{16,24},{20,12},{24,32},{28,20},{32,40}... | collective-permute-start | bytes 786440 | tf_op jit(solution)/shard_map/ppermute | solution.py:183
  47.6 3.8 %collective-permute-start.11 = (f32[128,512]{1,0:T(8,128)S(1)}, f32[128,512]{1,0:T(8,128)S(1)}, u32[]{:S(2)}, u32[]{:S(2)}) collective-permute-start(f32[128,512]{1,0:T(8,128)S(1)} %get-tuple-element.39), channel_id=1, source_target_pairs={{0,16},{4,52},{8,24},{12,60},{16,32},{20,4},{24,40},{28,12},{32,48... | collective-permute-start | bytes 786440 | tf_op jit(solution)/shard_map/ppermute | solution.py:184
  51.4 0.0 collective-permute-done.13
  51.5 2.1 %collective-permute-start.14 = (f32[128,512]{1,0:T(8,128)S(1)}, f32[128,512]{1,0:T(8,128)S(1)}, u32[]{:S(2)}, u32[]{:S(2)}) collective-permute-start(f32[128,512]{1,0:T(8,128)S(1)} %add.29), channel_id=1, source_target_pairs={{0,8},{4,60},{8,16},{12,4},{16,24},{20,12},{24,32},{28,20},{32,40}... | collective-permute-start | bytes 786440 | tf_op jit(solution)/shard_map/ppermute | solution.py:185
  53.5 3.5 %collective-permute-start.7 = (f32[128,512]{1,0:T(8,128)S(1)}, f32[128,512]{1,0:T(8,128)S(1)}, u32[]{:S(2)}, u32[]{:S(2)}) collective-permute-start(f32[128,512]{1,0:T(8,128)S(1)} %get-tuple-element.33), channel_id=1, source_target_pairs={{0,4},{4,0},{8,12},{12,8},{16,20},{20,16},{24,28},{28,24},{32,36},... | collective-permute-start | bytes 786440 | tf_op jit(solution)/shard_map/ppermute | solution.py:189
  57.1 4.2 %collective-permute-start.9 = (f32[128,512]{1,0:T(8,128)S(1)}, f32[128,512]{1,0:T(8,128)S(1)}, u32[]{:S(2)}, u32[]{:S(2)}) collective-permute-start(f32[128,512]{1,0:T(8,128)S(1)} %get-tuple-element.36), channel_id=1, source_target_pairs={{0,8},{4,60},{8,16},{12,4},{16,24},{20,12},{24,32},{28,20},{32,40}... | collective-permute-start | bytes 786440 | tf_op jit(solution)/shard_map/ppermute | solution.py:186
  61.3 0.0 collective-permute-done.10
  61.3 0.0 collective-permute-done.11
  61.3 0.1 add_add_fusion.1
  61.4 2.2 %collective-permute-start.12 = (f32[128,512]{1,0:T(8,128)S(1)}, f32[128,512]{1,0:T(8,128)S(1)}, u32[]{:S(2)}, u32[]{:S(2)}) collective-permute-start(f32[128,512]{1,0:T(8,128)S(1)} %add_add_fusion.1), channel_id=1, source_target_pairs={{0,16},{4,52},{8,24},{12,60},{16,32},{20,4},{24,40},{28,12},{32,48... | collective-permute-start | bytes 786440 | tf_op jit(solution)/shard_map/ppermute | solution.py:187
  63.6 0.0 collective-permute-done.14
  63.7 3.5 %collective-permute-start.15 = (f32[128,512]{1,0:T(8,128)S(1)}, f32[128,512]{1,0:T(8,128)S(1)}, u32[]{:S(2)}, u32[]{:S(2)}) collective-permute-start(f32[128,512]{1,0:T(8,128)S(1)} %add.30), channel_id=1, source_target_pairs={{0,12},{4,56},{8,20},{12,0},{16,28},{20,8},{24,36},{28,16},{32,44}... | collective-permute-start | bytes 786440 | tf_op jit(solution)/shard_map/ppermute | solution.py:188
  67.2 0.0 collective-permute-done.7
  67.2 0.0 collective-permute-done.9
  67.2 4.2 %collective-permute-done.12 = f32[128,512]{1,0:T(8,128)S(1)} collective-permute-done((f32[128,512]{1,0:T(8,128)S(1)}, f32[128,512]{1,0:T(8,128)S(1)}, u32[]{:S(2)}, u32[]{:S(2)}) %collective-permute-start.12) | collective-permute-done | bytes 262176 | tf_op jit(solution)/shard_map/ppermute | solution.py:187
  71.4 3.7 %collective-permute-done.15 = f32[128,512]{1,0:T(8,128)S(1)} collective-permute-done((f32[128,512]{1,0:T(8,128)S(1)}, f32[128,512]{1,0:T(8,128)S(1)}, u32[]{:S(2)}, u32[]{:S(2)}) %collective-permute-start.15) | collective-permute-done | bytes 262176 | tf_op jit(solution)/shard_map/ppermute | solution.py:188
  75.1 0.8 %add_add_fusion = f32[128,512]{1,0:T(8,128)} fusion(f32[128,512]{1,0:T(8,128)S(1)} %collective-permute-done.15, f32[128,512]{1,0:T(8,128)S(1)} %collective-permute-done.12, f32[128,512]{1,0:T(8,128)S(1)} %collective-permute-done.9, f32[128,512]{1,0:T(8,128)S(1)} %get-tuple-element.32, f32[128,512]{1,0:T(8,128)S(1)} %collective-permute-done.7), kind=kLoop, calls=%fused_computation | loop fusion | flops 262144 | bytes 1572864 | tf_op jit(solution)/shard_map/add | solution.py:190
  (2 shorter events, 0.1 us)
Async XLA Ops:
  0.0 14.8 %collective-permute-start = (f32[128,512]{1,0:T(8,128)}, f32[128,512]{1,0:T(8,128)S(1)}, u32[]{:S(2)}, u32[]{:S(2)}) collective-permute-start(f32[128,512]{1,0:T(8,128)} %b0.1), channel_id=1, source_target_pairs={{0,256},{4,260},{8,264},{12,268},{16,272},{20,276},{24,280},{28,28... | collective-permute-start | bytes 786440 | tf_op jit(solution)/shard_map/ppermute | solution.py:167
  5.5 11.2 %collective-permute-start.3 = (f32[128,512]{1,0:T(8,128)}, f32[128,512]{1,0:T(8,128)S(1)}, u32[]{:S(2)}, u32[]{:S(2)}) collective-permute-start(f32[128,512]{1,0:T(8,128)} %b0.1), channel_id=1, source_target_pairs={{0,64},{64,0},{128,192},{192,128},{256,320},{320,256},{384,448},{4... | collective-permute-start | bytes 786440 | tf_op jit(solution)/shard_map/ppermute | solution.py:164
  9.5 13.2 %collective-permute-start.2 = (f32[128,512]{1,0:T(8,128)}, f32[128,512]{1,0:T(8,128)S(1)}, u32[]{:S(2)}, u32[]{:S(2)}) collective-permute-start(f32[128,512]{1,0:T(8,128)} %b0.1), channel_id=1, source_target_pairs={{0,128},{4,388},{8,136},{12,396},{16,144},{20,404},{24,152},{28,41... | collective-permute-start | bytes 786440 | tf_op jit(solution)/shard_map/ppermute | solution.py:167
  12.3 10.4 %collective-permute-start.1 = (f32[128,512]{1,0:T(8,128)}, f32[128,512]{1,0:T(8,128)S(1)}, u32[]{:S(2)}, u32[]{:S(2)}) collective-permute-start(f32[128,512]{1,0:T(8,128)} %b0.1), channel_id=1, source_target_pairs={{0,384},{4,132},{8,392},{12,140},{16,400},{20,148},{24,408},{28,15... | collective-permute-start | bytes 786440 | tf_op jit(solution)/shard_map/ppermute | solution.py:167
  14.8 13.0 %collective-permute-start.4 = (f32[128,512]{1,0:T(8,128)S(1)}, f32[128,512]{1,0:T(8,128)S(1)}, u32[]{:S(2)}, u32[]{:S(2)}) collective-permute-start(f32[128,512]{1,0:T(8,128)S(1)} %collective-permute-done.b1), channel_id=1, source_target_pairs={{0,64},{64,0},{128,192},{192,128},{256,320},{320,256},{384,448},{4... | collective-permute-start | bytes 786440 | tf_op jit(solution)/shard_map/ppermute | solution.py:164
  16.7 11.0 %collective-permute-start.6 = (f32[128,512]{1,0:T(8,128)S(1)}, f32[128,512]{1,0:T(8,128)S(1)}, u32[]{:S(2)}, u32[]{:S(2)}) collective-permute-start(f32[128,512]{1,0:T(8,128)S(1)} %collective-permute-done.3.b0), channel_id=1, source_target_pairs={{0,128},{4,388},{8,136},{12,396},{16,144},{20,404},{24,152},{28,41... | collective-permute-start | bytes 786440 | tf_op jit(solution)/shard_map/ppermute | solution.py:167
  20.7 9.9 %collective-permute-start.5 = (f32[128,512]{1,0:T(8,128)S(1)}, f32[128,512]{1,0:T(8,128)S(1)}, u32[]{:S(2)}, u32[]{:S(2)}) collective-permute-start(f32[128,512]{1,0:T(8,128)S(1)} %collective-permute-done.3.b0), channel_id=1, source_target_pairs={{0,384},{4,132},{8,392},{12,140},{16,400},{20,148},{24,408},{28,15... | collective-permute-start | bytes 786440 | tf_op jit(solution)/shard_map/ppermute | solution.py:167
  22.7 1.0 %copy-start = (f32[128,512]{1,0:T(8,128)S(1)}, f32[128,512]{1,0:T(8,128)}, u32[]{:S(2)}) copy-start(f32[128,512]{1,0:T(8,128)} %b0.1) | copy-start | bytes 786436
  32.6 8.7 %collective-permute-start.8 = (f32[896,512]{1,0:T(8,128)S(1)}, f32[896,512]{1,0:T(8,128)S(1)}, u32[]{:S(2)}, u32[]{:S(2)}) collective-permute-start(f32[896,512]{1,0:T(8,128)S(1)} %get-tuple-element.34), channel_id=1, source_target_pairs={{0,4},{4,0},{8,12},{12,8},{16,20},{20,16},{24,28},{28,24},{32,36},... | collective-permute-start | bytes 5505032 | tf_op jit(solution)/shard_map/ppermute | solution.py:180
  41.5 9.9 %collective-permute-start.13 = (f32[128,512]{1,0:T(8,128)S(1)}, f32[128,512]{1,0:T(8,128)S(1)}, u32[]{:S(2)}, u32[]{:S(2)}) collective-permute-start(f32[128,512]{1,0:T(8,128)S(1)} %get-tuple-element.42), channel_id=1, source_target_pairs={{0,8},{4,60},{8,16},{12,4},{16,24},{20,12},{24,32},{28,20},{32,40}... | collective-permute-start | bytes 786440 | tf_op jit(solution)/shard_map/ppermute | solution.py:182
  44.6 16.7 %collective-permute-start.10 = (f32[128,512]{1,0:T(8,128)S(1)}, f32[128,512]{1,0:T(8,128)S(1)}, u32[]{:S(2)}, u32[]{:S(2)}) collective-permute-start(f32[128,512]{1,0:T(8,128)S(1)} %get-tuple-element.38), channel_id=1, source_target_pairs={{0,8},{4,60},{8,16},{12,4},{16,24},{20,12},{24,32},{28,20},{32,40}... | collective-permute-start | bytes 786440 | tf_op jit(solution)/shard_map/ppermute | solution.py:183
  47.6 13.7 %collective-permute-start.11 = (f32[128,512]{1,0:T(8,128)S(1)}, f32[128,512]{1,0:T(8,128)S(1)}, u32[]{:S(2)}, u32[]{:S(2)}) collective-permute-start(f32[128,512]{1,0:T(8,128)S(1)} %get-tuple-element.39), channel_id=1, source_target_pairs={{0,16},{4,52},{8,24},{12,60},{16,32},{20,4},{24,40},{28,12},{32,48... | collective-permute-start | bytes 786440 | tf_op jit(solution)/shard_map/ppermute | solution.py:184
  51.5 12.1 %collective-permute-start.14 = (f32[128,512]{1,0:T(8,128)S(1)}, f32[128,512]{1,0:T(8,128)S(1)}, u32[]{:S(2)}, u32[]{:S(2)}) collective-permute-start(f32[128,512]{1,0:T(8,128)S(1)} %add.29), channel_id=1, source_target_pairs={{0,8},{4,60},{8,16},{12,4},{16,24},{20,12},{24,32},{28,20},{32,40}... | collective-permute-start | bytes 786440 | tf_op jit(solution)/shard_map/ppermute | solution.py:185
  53.5 13.6 %collective-permute-start.7 = (f32[128,512]{1,0:T(8,128)S(1)}, f32[128,512]{1,0:T(8,128)S(1)}, u32[]{:S(2)}, u32[]{:S(2)}) collective-permute-start(f32[128,512]{1,0:T(8,128)S(1)} %get-tuple-element.33), channel_id=1, source_target_pairs={{0,4},{4,0},{8,12},{12,8},{16,20},{20,16},{24,28},{28,24},{32,36},... | collective-permute-start | bytes 786440 | tf_op jit(solution)/shard_map/ppermute | solution.py:189
  57.1 10.1 %collective-permute-start.9 = (f32[128,512]{1,0:T(8,128)S(1)}, f32[128,512]{1,0:T(8,128)S(1)}, u32[]{:S(2)}, u32[]{:S(2)}) collective-permute-start(f32[128,512]{1,0:T(8,128)S(1)} %get-tuple-element.36), channel_id=1, source_target_pairs={{0,8},{4,60},{8,16},{12,4},{16,24},{20,12},{24,32},{28,20},{32,40}... | collective-permute-start | bytes 786440 | tf_op jit(solution)/shard_map/ppermute | solution.py:186
  61.4 10.0 %collective-permute-start.12 = (f32[128,512]{1,0:T(8,128)S(1)}, f32[128,512]{1,0:T(8,128)S(1)}, u32[]{:S(2)}, u32[]{:S(2)}) collective-permute-start(f32[128,512]{1,0:T(8,128)S(1)} %add_add_fusion.1), channel_id=1, source_target_pairs={{0,16},{4,52},{8,24},{12,60},{16,32},{20,4},{24,40},{28,12},{32,48... | collective-permute-start | bytes 786440 | tf_op jit(solution)/shard_map/ppermute | solution.py:187
  63.7 11.5 %collective-permute-start.15 = (f32[128,512]{1,0:T(8,128)S(1)}, f32[128,512]{1,0:T(8,128)S(1)}, u32[]{:S(2)}, u32[]{:S(2)}) collective-permute-start(f32[128,512]{1,0:T(8,128)S(1)} %add.30), channel_id=1, source_target_pairs={{0,12},{4,56},{8,20},{12,0},{16,28},{20,8},{24,36},{28,16},{32,44}... | collective-permute-start | bytes 786440 | tf_op jit(solution)/shard_map/ppermute | solution.py:188
